TPU v7x, 32 devices: a whole 2x2x4 slice. The times are simulated.
32 devices in a mesh: grp: 2 (over x), ep: 16 (over z, y, core).
Axes of the slice: x: 2, y: 2, z: 4, core: 2. Of those that a mesh axis runs over, the one named last changes fastest.
Arguments:
- upstream: bfloat16 [4096, 2048], P(('grp', 'ep')), parts along dimension 0, may hold values from -6 to 6
- inputs: bfloat16 [4096, 2048], P(('grp', 'ep')), parts along dimension 0, may hold values from -6 to 6
- expert_ids: int32 [4096, 2], P(('grp', 'ep')), parts along dimension 0, may hold values from 0 to 7, all different within a row; in each aligned block of 128 rows (0 to 127, 128 to 255, ...) at most 48 rows name the same one
- gate_weights: bfloat16 [4096, 2], P(('grp', 'ep')), parts along dimension 0, may hold values from 0.099609375 to 1
- w_in: bfloat16 [16, 2048, 768], P('ep'), may hold values from -0.125 to 0.125
- w_down: bfloat16 [16, 384, 2048], P('ep'), may hold values from -0.21875 to 0.21875
Outputs:
- grad_inputs: bfloat16 [4096, 2048], P(('grp', 'ep')), parts along dimension 0
- grad_gates: float32 [4096, 2], P(('grp', 'ep')), parts along dimension 0
- grad_w_in: bfloat16 [32, 2048, 768], P(('grp', 'ep')), parts along dimension 0
- grad_w_down: bfloat16 [32, 384, 2048], P(('grp', 'ep')), parts along dimension 0
There are 2 independent parts, one for each index of `grp`. A program takes and returns all parts, laid end to end along the dimension named above; an argument that names none is the same for every part. Nothing has to cross between parts.
Inputs may be any that keep to these rules, and one draw needn't show every extreme that they name: `expert_ids`: each token names 2 different experts, every expert is named by some token, and among the tokens of one index of ep no expert is named more than 48 times; some expert is named exactly 48 times in some such block.
All inputs are finite; a program needn't handle non-finite values.
Results may differ from a plain program's by a relative error of at most 0.0067.
Values may be sent and summed in bfloat16 or wider, within the bound.
No kernel may reach another device: no remote copies, remote signals or barrier semaphores. Data moves between devices by JAX's collectives and lax.ppermute only.
A program may use at most 128 MiB of HBM per device.

v0:
```python
import math

import jax
import jax.numpy as jnp
from jax import lax
from jax.sharding import PartitionSpec as P


def half_terms(token_rows, grad_rows, gate_rows, weight_in, weight_down, factor):
    halfwidth = weight_down.shape[0]
    gate_up = jnp.dot(token_rows, weight_in, preferred_element_type=jnp.float32)
    gate_pre = gate_up[:, :halfwidth]
    up_pre = gate_up[:, halfwidth:]
    squash = jax.nn.sigmoid(gate_pre)
    active = gate_pre * squash
    hidden = active * up_pre
    pulled = lax.dot_general(
        grad_rows, weight_down, (((1,), (1,)), ((), ())), preferred_element_type=jnp.float32
    )
    gate_col = gate_rows.astype(jnp.float32)[:, None]
    gate_part = jnp.sum(hidden * pulled, axis=1).astype(jnp.bfloat16)
    hidden_grad = gate_col * pulled
    gate_grad = hidden_grad * up_pre * squash * (1.0 + gate_pre * (1.0 - squash))
    up_grad = hidden_grad * active
    pre_grad = jnp.concatenate([gate_grad, up_grad], axis=1).astype(jnp.bfloat16)
    scaled = (gate_col * hidden).astype(jnp.bfloat16)
    grad_in = lax.dot_general(
        token_rows, pre_grad, (((0,), (0,)), ((), ())), preferred_element_type=jnp.float32
    )
    grad_down = lax.dot_general(
        scaled, grad_rows, (((0,), (0,)), ((), ())), preferred_element_type=jnp.float32
    )
    returned = lax.dot_general(
        pre_grad, weight_in, (((1,), (1,)), ((), ())), preferred_element_type=jnp.float32
    )
    return (
        (grad_in * factor).astype(jnp.bfloat16),
        (grad_down * factor).astype(jnp.bfloat16),
        returned.astype(jnp.bfloat16),
        gate_part,
    )


def per_device(upstream, inputs, expert_ids, gate_weights, w_in, w_down):
    devices = lax.axis_size("ep")
    experts = devices // 2
    tokens = upstream.shape[0]
    features = upstream.shape[1]
    choose = expert_ids.shape[1]
    routed = tokens * choose
    capacity = routed * 3 // devices
    flat_ids = expert_ids.reshape(routed)
    onehot = (flat_ids[:, None] == jnp.arange(experts, dtype=jnp.int32)[None, :]).astype(jnp.int32)
    earlier = jnp.cumsum(onehot, axis=0) - onehot
    position = jnp.sum(earlier * onehot, axis=1)
    target = flat_ids * capacity + position
    source = (
        jnp.full((experts * capacity,), routed, jnp.int32)
        .at[target]
        .set(jnp.arange(routed, dtype=jnp.int32))
    )
    filled = source < routed
    token_of = jnp.where(filled, source // choose, tokens)
    zero_row = jnp.zeros((1, features), jnp.bfloat16)
    x_buffer = jnp.concatenate([inputs, zero_row], axis=0)[token_of].reshape(
        experts, capacity, features
    )
    up_buffer = jnp.concatenate([upstream, zero_row], axis=0)[token_of].reshape(
        experts, capacity, features
    )
    gate_flat = jnp.concatenate(
        [gate_weights.reshape(routed), jnp.zeros((1,), jnp.bfloat16)], axis=0
    )
    gate_buffer = gate_flat[source].reshape(experts, 1, capacity)
    gate_send = jnp.broadcast_to(gate_buffer, (experts, 2, capacity)).reshape(devices, capacity)
    x_send = jnp.broadcast_to(x_buffer[:, None], (experts, 2, capacity, features)).reshape(
        devices, capacity, features
    )
    up_send = jnp.broadcast_to(up_buffer[:, None], (experts, 2, capacity, features)).reshape(
        devices, capacity, features
    )
    x_recv, up_recv, gate_recv = (
        lax.all_to_all(x_send, "ep", split_axis=0, concat_axis=0, tiled=True),
        lax.all_to_all(up_send, "ep", split_axis=0, concat_axis=0, tiled=True),
        lax.all_to_all(gate_send, "ep", split_axis=0, concat_axis=0, tiled=True),
    )
    all_rows = devices * capacity
    factor = 1.0 / math.sqrt(2 * routed)
    grad_in, grad_down, returned, gate_part = half_terms(
        x_recv.reshape(all_rows, features),
        up_recv.reshape(all_rows, features),
        gate_recv.reshape(all_rows),
        w_in[0],
        w_down[0],
        factor,
    )
    back_rows, back_gates = (
        lax.all_to_all(
            returned.reshape(devices, capacity, features),
            "ep",
            split_axis=0,
            concat_axis=0,
            tiled=True,
        ),
        lax.all_to_all(
            gate_part.reshape(devices, capacity), "ep", split_axis=0, concat_axis=0, tiled=True
        ),
    )
    paired_rows = back_rows.reshape(experts, 2, capacity, features)
    summed = (
        (paired_rows[:, 0].astype(jnp.float32) + paired_rows[:, 1].astype(jnp.float32))
        .astype(jnp.bfloat16)
        .reshape(experts * capacity, features)
    )
    paired_gates = back_gates.reshape(experts, 2, capacity)
    gate_sum = (
        paired_gates[:, 0].astype(jnp.float32) + paired_gates[:, 1].astype(jnp.float32)
    ).reshape(experts * capacity)
    grad_inputs = jnp.sum(
        summed[target].astype(jnp.float32).reshape(tokens, choose, features), axis=1
    ).astype(jnp.bfloat16)
    grad_gates = gate_sum[target].reshape(tokens, choose)
    return (grad_inputs, grad_gates, grad_in[None], grad_down[None])


def solution(mesh):
    return jax.shard_map(
        per_device,
        mesh=mesh,
        in_specs=(
            P(("grp", "ep"), None),
            P(("grp", "ep"), None),
            P(("grp", "ep"), None),
            P(("grp", "ep"), None),
            P("ep", None, None),
            P("ep", None, None),
        ),
        out_specs=(
            P(("grp", "ep"), None),
            P(("grp", "ep"), None),
            P(("grp", "ep"), None, None),
            P(("grp", "ep"), None, None),
        ),
        check_vma=False,
    )
```

profile of v0, /device:TPU:15, one launch (start us, length us, event | category | flops | bytes accessed | tf_op | source)
XLA Modules:
  0.0 291.0 jit_solution(14127624864948558928)
XLA Ops:
  6.3 2.8 gather_fusion
  9.8 6.6 %all-to-all-start = ((bf16[16,1,48]{2,1,0:T(2,128)(2,1)}), bf16[16,1,48]{2,1,0:T(2,128)(2,1)S(1)}, u32[]{:S(2)}, u32[]{:S(2)}) async-start(bf16[16,1,48]{2,1,0:T(2,128)(2,1)} %copy.31), calls=%async_computation | async-start | bytes 16384 | tf_op jit(solution)/shard_map/all_to_all | solution.py:85
  16.4 1.9 concatenate.15
  18.3 6.2 %gather_fusion.2 = bf16[384,2048]{1,0:T(8,128)(2,1)} fusion(bf16[129,2048]{1,0:T(8,128)(2,1)} %concatenate.15, s32[1024]{0:T(1024)S(1)} %get-tuple-element.21), kind=kCustom, calls=%fused_computation.2 | custom fusion | bytes 3147264 | tf_op jit(solution)/shard_map/gather | solution.py:65
  24.4 3.5 %broadcast_in_dim.52 = bf16[8,2,48,2048]{3,2,1,0:T(8,128)(2,1)} broadcast(bf16[8,48,2048]{2,1,0:T(8,128)(2,1)} %bitcast.52), dimensions={0,2,3} | broadcast | bytes 4718592 | tf_op jit(solution)/shard_map/broadcast_in_dim | solution.py:76
  27.9 6.0 %all-to-all-start.2 = ((bf16[16,48,2048]{2,1,0:T(8,128)(2,1)}), bf16[16,48,2048]{2,1,0:T(8,128)(2,1)}, u32[]{:S(2)}, u32[]{:S(2)}) async-start(bf16[16,48,2048]{2,1,0:T(8,128)(2,1)} %bitcast.50), calls=%async_computation.2 | async-start | bytes 6291456 | tf_op jit(solution)/shard_map/all_to_all | solution.py:83
  35.8 6.2 %gather_fusion.1 = bf16[384,2048]{1,0:T(8,128)(2,1)} fusion(bf16[129,2048]{1,0:T(8,128)(2,1)} %concatenate.14, s32[1024]{0:T(1024)S(1)} %get-tuple-element.21), kind=kCustom, calls=%fused_computation.1 | custom fusion | bytes 3147264 | tf_op jit(solution)/shard_map/gather | solution.py:68
  42.0 61.9 %all-to-all-done.2 = bf16[16,48,2048]{2,1,0:T(8,128)(2,1)} async-done(((bf16[16,48,2048]{2,1,0:T(8,128)(2,1)}), bf16[16,48,2048]{2,1,0:T(8,128)(2,1)}, u32[]{:S(2)}, u32[]{:S(2)}) %all-to-all-start.2) | async-done | bytes 3145760 | tf_op jit(solution)/shard_map/all_to_all | solution.py:83
  103.9 3.5 %broadcast_in_dim.50 = bf16[8,2,48,2048]{3,2,1,0:T(8,128)(2,1)} broadcast(bf16[8,48,2048]{2,1,0:T(8,128)(2,1)} %bitcast.51), dimensions={0,2,3} | broadcast | bytes 4718592 | tf_op jit(solution)/shard_map/broadcast_in_dim | solution.py:79
  107.4 4.9 %all-to-all-start.1 = ((bf16[16,48,2048]{2,1,0:T(8,128)(2,1)}), bf16[16,48,2048]{2,1,0:T(8,128)(2,1)}, u32[]{:S(2)}, u32[]{:S(2)}) async-start(bf16[16,48,2048]{2,1,0:T(8,128)(2,1)} %bitcast.49), calls=%async_computation.1 | async-start | bytes 6291456 | tf_op jit(solution)/shard_map/all_to_all | solution.py:84
  112.4 6.0 %fusion.1 = f32[768,768]{0,1:T(8,128)} fusion(bf16[768,2048]{1,0:T(8,128)(2,1)} %bitcast.11, bf16[1,2048,768]{2,1,0:T(8,128)(2,1)S(1)} %copy-done), kind=kOutput, calls=%fused_computation.9 | convolution fusion | flops 2415919104 | bytes 8650752 | tf_op jit(solution)/shard_map/dot_general | solution.py:11
  118.4 63.9 %all-to-all-done.1 = bf16[16,48,2048]{2,1,0:T(8,128)(2,1)} async-done(((bf16[16,48,2048]{2,1,0:T(8,128)(2,1)}), bf16[16,48,2048]{2,1,0:T(8,128)(2,1)}, u32[]{:S(2)}, u32[]{:S(2)}) %all-to-all-start.1) | async-done | bytes 3145760 | tf_op jit(solution)/shard_map/all_to_all | solution.py:84
  182.3 5.9 %multiply_convert_fusion.4 = (bf16[768,384]{0,1:T(8,128)(2,1)}, bf16[768,384]{0,1:T(8,128)(2,1)}, bf16[768]{0:T(1024)(128)(2,1)S(1)}) fusion(f32[768,768]{0,1:T(8,128)} %fusion.1, f32[768]{0:T(1024)S(1)} %reshape.139, bf16[768,2048]{1,0:T(8,128)(2,1)} %bitcast.7, bf16[1,384,2048]{2,1,0:T(8,128)(2,1)} %param.11), kind=kOutput, calls=%fused_computation.23 | convolution fusion | flops 1212972288 | bytes 8262144 | tf_op jit(solution)/shard_map/dot_general | solution.py:17
  188.9 4.9 %all-to-all-start.4 = ((bf16[16,1,48]{2,1,0:T(2,128)(2,1)}), bf16[16,1,48]{2,1,0:T(2,128)(2,1)S(1)}, u32[]{:S(2)}, u32[]{:S(2)}) async-start(bf16[16,1,48]{2,1,0:T(2,128)(2,1)} %convert_element_type.91), calls=%async_computation.4 | async-start | bytes 16384 | tf_op jit(solution)/shard_map/all_to_all | solution.py:105
  193.8 5.4 %convolution_convert_fusion = bf16[768,2048]{1,0:T(8,128)(2,1)} fusion(bf16[1,2048,768]{2,1,0:T(8,128)(2,1)S(1)} %copy-done, bf16[768,384]{0,1:T(8,128)(2,1)} %get-tuple-element.17, bf16[768,384]{0,1:T(8,128)(2,1)} %get-tuple-element.16), kind=kOutput, calls=%fused_computation.7 | convolution fusion | flops 2419851264 | bytes 7471104 | tf_op jit(solution)/shard_map/dot_general | solution.py:33
  199.2 6.0 %all-to-all-start.3 = ((bf16[16,48,2048]{2,1,0:T(8,128)(2,1)}), bf16[16,48,2048]{2,1,0:T(8,128)(2,1)}, u32[]{:S(2)}, u32[]{:S(2)}) async-start(bf16[16,48,2048]{2,1,0:T(8,128)(2,1)} %bitcast.53), calls=%async_computation.3 | async-start | bytes 6291456 | tf_op jit(solution)/shard_map/all_to_all | solution.py:98
  205.3 5.3 %fusion.4 = bf16[1,384,2048]{2,1,0:T(8,128)(2,1)} fusion(bf16[768,2048]{1,0:T(8,128)(2,1)} %bitcast.7, f32[768]{0:T(1024)S(1)} %reshape.139, f32[768,768]{0,1:T(8,128)} %fusion.1), kind=kOutput, calls=%fused_computation.14 | convolution fusion | flops 1211596800 | bytes 7080960 | tf_op jit(solution)/shard_map/dot_general | solution.py:30
  210.5 6.3 %fusion.3 = bf16[1,2048,768]{2,1,0:T(8,128)(2,1)} fusion(bf16[768,2048]{1,0:T(8,128)(2,1)} %bitcast.11, bf16[768,384]{0,1:T(8,128)(2,1)S(1)} %copy-done.2, bf16[768,384]{0,1:T(8,128)(2,1)S(1)} %copy-done.1), kind=kOutput, calls=%fused_computation.13 | convolution fusion | flops 2421424128 | bytes 7471104 | tf_op jit(solution)/shard_map/dot_general | solution.py:27
  216.9 1.9 gather_fusion.4
  219.6 55.6 %all-to-all-done.3 = bf16[16,48,2048]{2,1,0:T(8,128)(2,1)} async-done(((bf16[16,48,2048]{2,1,0:T(8,128)(2,1)}), bf16[16,48,2048]{2,1,0:T(8,128)(2,1)}, u32[]{:S(2)}, u32[]{:S(2)}) %all-to-all-start.3) | async-done | bytes 3145760 | tf_op jit(solution)/shard_map/all_to_all | solution.py:98
  275.2 3.7 %add_convert_fusion = bf16[8,1,48,2048]{3,2,0,1:T(8,128)(2,1)} fusion(bf16[8,2,48,2048]{3,2,1,0:T(8,128)(2,1)} %bitcast.14), kind=kLoop, calls=%fused_computation.12 | loop fusion | flops 3145728 | bytes 4718592 | tf_op jit(solution)/shard_map/convert_element_type | solution.py:112
  278.9 4.9 %gather_fusion.3 = bf16[256,2048]{1,0:T(8,128)(2,1)} fusion(bf16[384,2048]{1,0:T(8,128)(2,1)} %bitcast.48, s32[1024]{0:T(1024)S(1)} %pad_clamp_fusion), kind=kCustom, calls=%fused_computation.3 | custom fusion | bytes 2098176 | tf_op jit(solution)/shard_map/gather | solution.py:120
  283.9 2.5 gather.21
  286.4 4.6 %reduce_sum.34 = bf16[128,2048]{1,0:T(8,128)(2,1)} reduce(bf16[128,2,2048]{2,1,0:T(2,128)(2,1)} %gather.21, bf16[]{:T(256)} %constant.13.clone.1), dimensions={1}, to_apply=%region_4.5 | reduce | flops 262144 | bytes 1572866 | tf_op jit(solution)/shard_map/reduce_sum | solution.py:119
  (41 shorter events, 9.9 us)
Async XLA Ops:
  0.6 111.8 %copy-start = (bf16[1,2048,768]{2,1,0:T(8,128)(2,1)S(1)}, bf16[1,2048,768]{2,1,0:T(8,128)(2,1)}, u32[]{:S(2)}) copy-start(bf16[1,2048,768]{2,1,0:T(8,128)(2,1)} %param.10) | copy-start | bytes 9437188
  9.8 14.6 %all-to-all-start = ((bf16[16,1,48]{2,1,0:T(2,128)(2,1)}), bf16[16,1,48]{2,1,0:T(2,128)(2,1)S(1)}, u32[]{:S(2)}, u32[]{:S(2)}) async-start(bf16[16,1,48]{2,1,0:T(2,128)(2,1)} %copy.31), calls=%async_computation | async-start | bytes 16384 | tf_op jit(solution)/shard_map/all_to_all | solution.py:85
  27.9 76.0 %all-to-all-start.2 = ((bf16[16,48,2048]{2,1,0:T(8,128)(2,1)}), bf16[16,48,2048]{2,1,0:T(8,128)(2,1)}, u32[]{:S(2)}, u32[]{:S(2)}) async-start(bf16[16,48,2048]{2,1,0:T(8,128)(2,1)} %bitcast.50), calls=%async_computation.2 | async-start | bytes 6291456 | tf_op jit(solution)/shard_map/all_to_all | solution.py:83
  107.4 74.9 %all-to-all-start.1 = ((bf16[16,48,2048]{2,1,0:T(8,128)(2,1)}), bf16[16,48,2048]{2,1,0:T(8,128)(2,1)}, u32[]{:S(2)}, u32[]{:S(2)}) async-start(bf16[16,48,2048]{2,1,0:T(8,128)(2,1)} %bitcast.49), calls=%async_computation.1 | async-start | bytes 6291456 | tf_op jit(solution)/shard_map/all_to_all | solution.py:84
  188.9 10.3 %all-to-all-start.4 = ((bf16[16,1,48]{2,1,0:T(2,128)(2,1)}), bf16[16,1,48]{2,1,0:T(2,128)(2,1)S(1)}, u32[]{:S(2)}, u32[]{:S(2)}) async-start(bf16[16,1,48]{2,1,0:T(2,128)(2,1)} %convert_element_type.91), calls=%async_computation.4 | async-start | bytes 16384 | tf_op jit(solution)/shard_map/all_to_all | solution.py:105
  199.2 76.0 %all-to-all-start.3 = ((bf16[16,48,2048]{2,1,0:T(8,128)(2,1)}), bf16[16,48,2048]{2,1,0:T(8,128)(2,1)}, u32[]{:S(2)}, u32[]{:S(2)}) async-start(bf16[16,48,2048]{2,1,0:T(8,128)(2,1)} %bitcast.53), calls=%async_computation.3 | async-start | bytes 6291456 | tf_op jit(solution)/shard_map/all_to_all | solution.py:98
  205.2 5.3 %copy-start.1 = (bf16[768,384]{0,1:T(8,128)(2,1)S(1)}, bf16[768,384]{0,1:T(8,128)(2,1)}, u32[]{:S(2)}) copy-start(bf16[768,384]{0,1:T(8,128)(2,1)} %get-tuple-element.16) | copy-start | bytes 1769476
  205.2 5.3 %copy-start.2 = (bf16[768,384]{0,1:T(8,128)(2,1)S(1)}, bf16[768,384]{0,1:T(8,128)(2,1)}, u32[]{:S(2)}) copy-start(bf16[768,384]{0,1:T(8,128)(2,1)} %get-tuple-element.17) | copy-start | bytes 1769476
where the time goes:
time: 292 us; the launch traced here: 291 us
  waiting for transfers between devices  181 us (62%)
  local copies, waits for them, and re-layouts  41.7 us (14%)
  matrix products  28.8 us (10%)
  starting transfers between devices  28.4 us (10%)
  other arithmetic  9.91 us (3%)
    all_to_all x1, waiting for transfers between devices, per_device(): lax.all_to_all(up_send, 'ep', split_axis=0, concat_axis=0, tiled=True)  63.9 us
    all_to_all x1, waiting for transfers between devices, per_device(): lax.all_to_all(x_send, 'ep', split_axis=0, concat_axis=0, tiled=True)  61.9 us
    all_to_all x1, waiting for transfers between devices, per_device(): lax.all_to_all(returned.reshape(devices, capacity, features), 'ep', split...  55.6 us
    gather x2, local copies, waits for them, and re-layouts, per_device(): summed[target].astype(jnp.float32).reshape(tokens, choose, features)  7.48 us
    all_to_all x1, starting transfers between devices, per_device(): lax.all_to_all(gate_send, 'ep', split_axis=0, concat_axis=0, tiled=True)  6.55 us
    dot_general x1, matrix products, half_terms(): lax.dot_general(token_rows, pre_grad, (((0,), (0,)), ((), ())), preferred...  6.27 us
    gather x1, local copies, waits for them, and re-layouts, per_device(): jnp.concatenate([inputs, zero_row], axis=0)[token_of]  6.17 us
    gather x1, local copies, waits for them, and re-layouts, per_device(): jnp.concatenate([upstream, zero_row], axis=0)[token_of]  6.17 us
  transfers between devices with their start and end apart: 5, of which 3 were waited for; matrix products, arithmetic and copies ran while one was open for 14% of the time, Pallas kernels for 0%

commit v1 on v0

v1 whole, which is shorter than its diff:
```python
import functools
import math

import jax
import jax.numpy as jnp
from jax import lax
from jax.experimental import pallas as pl
from jax.experimental.pallas import tpu as pltpu
from jax.sharding import PartitionSpec as P

F32 = jnp.float32
BF16 = jnp.bfloat16
LANES = 128
VMEM_LIMIT = 40 * 1024 * 1024


def dot(a, b, contract):
    return lax.dot_general(a, b, ((contract[:1], contract[1:]), ((), ())), preferred_element_type=F32)


def places(ids, experts):
    choose, tokens = ids.shape
    names = lax.broadcasted_iota(jnp.int32, (experts, tokens), 0)
    marks = [(names == ids[k : k + 1, :]).astype(F32) for k in range(choose)]
    earlier = lax.broadcasted_iota(jnp.int32, (tokens, tokens), 0) < lax.broadcasted_iota(
        jnp.int32, (tokens, tokens), 1
    )
    counts = dot(sum(marks).astype(BF16), earlier.astype(BF16), (1, 0))
    return [jnp.sum(counts * mark, axis=0, keepdims=True).astype(jnp.int32) for mark in marks]


def picks(ids, place, expert, first, rows):
    choose, tokens = ids.shape
    slot = lax.broadcasted_iota(jnp.int32, (rows, tokens), 0) + first
    return [
        ((ids[k : k + 1, :] == expert) & (place[k] == slot)).astype(F32) for k in range(choose)
    ]


def pack_kernel(experts, first, rows, chip_ref, ids_ref, gates_ref, x_ref, up_ref, *out_refs):
    width = x_ref.shape[1]
    ids = ids_ref[...]
    gates = gates_ref[...].astype(F32)
    place = places(ids, experts)
    chip = chip_ref[0]
    plain, gated = [], []
    for step in range(experts):
        ones = picks(ids, place, chip ^ step, first, rows)
        plain.append(sum(ones))
        gated.append(sum(one * gates[k : k + 1, :] for k, one in enumerate(ones)))
    x_rows = dot(jnp.concatenate(plain, axis=0).astype(BF16), x_ref[...], (1, 0)).astype(BF16)
    up_rows = dot(jnp.concatenate(gated, axis=0).astype(BF16), up_ref[...], (1, 0)).astype(BF16)
    for step in range(experts):
        out_refs[step][:, :width] = x_rows[step * rows : (step + 1) * rows]
        out_refs[step][:, width:] = up_rows[step * rows : (step + 1) * rows]


def expert_kernel(blocks, rows, *refs):
    ins, outs = refs[:blocks], refs[blocks + 4 :]
    w_in_refs, w_down_refs = refs[blocks : blocks + 2], refs[blocks + 2 : blocks + 4]
    back_refs = outs[:blocks]
    x_out, up_out, grad_refs, hidden_refs = outs[blocks], outs[blocks + 1], outs[blocks + 2 : blocks + 4], outs[blocks + 4 : blocks + 6]
    width = x_out.shape[1]
    half = w_down_refs[0].shape[0]
    for b in range(blocks):
        x_out[b * rows : (b + 1) * rows, :] = ins[b][:, :width]
        up_out[b * rows : (b + 1) * rows, :] = ins[b][:, width:]
    x_rows, up_rows = x_out[...], up_out[...]
    gate_parts = []
    for w_in_ref, w_down_ref, grad_ref, hidden_ref in zip(w_in_refs, w_down_refs, grad_refs, hidden_refs):
        pre = dot(x_rows, w_in_ref[...], (1, 0))
        pulled = dot(up_rows, w_down_ref[...], (1, 1))
        gate_pre, up_pre = pre[:, :half], pre[:, half:]
        squash = jax.nn.sigmoid(gate_pre)
        active = gate_pre * squash
        hidden = active * up_pre
        gate_parts.append(jnp.sum(hidden * pulled, axis=1, keepdims=True))
        grad_ref[:, :half] = (pulled * up_pre * squash * (1.0 + gate_pre * (1.0 - squash))).astype(BF16)
        grad_ref[:, half:] = (pulled * active).astype(BF16)
        hidden_ref[...] = hidden.astype(BF16)
    back = sum(
        dot(grad_ref[...], w_in_ref[...], (1, 1)) for grad_ref, w_in_ref in zip(grad_refs, w_in_refs)
    ).astype(BF16)
    lane = lax.broadcasted_iota(jnp.int32, (blocks * rows, LANES), 1)
    gate_lanes = jnp.where(lane == 0, gate_parts[0], jnp.where(lane == 1, gate_parts[1], 0.0)).astype(BF16)
    for b in range(blocks):
        back_refs[b][:, :width] = back[b * rows : (b + 1) * rows]
        back_refs[b][:, width:] = gate_lanes[b * rows : (b + 1) * rows]


def weight_kernel(chunks, scale, *refs):
    lefts, rights, rest = refs[:chunks], refs[chunks : 2 * chunks], refs[2 * chunks :]
    total = sum(dot(left[...], right[...], (0, 0)) for left, right in zip(lefts, rights))
    if scale is not None:
        total = (total + rest[0][...].astype(F32)) * scale
    rest[-1][...] = total.astype(BF16)


def combine_kernel(experts, spans, chip_ref, ids_ref, gates_ref, *refs):
    blocks, (out_ref, gate_ref) = refs[:-2], refs[-2:]
    width = out_ref.shape[1]
    ids = ids_ref[...]
    choose = ids.shape[0]
    place = places(ids, experts)
    chip = chip_ref[0]
    ones = [[] for _ in range(choose)]
    values = []
    at = 0
    for first, rows in spans:
        for step in range(experts):
            for k, one in enumerate(picks(ids, place, chip ^ step, first, rows)):
                ones[k].append(one)
            values.append(blocks[at][...])
            at += 1
    ones = [jnp.concatenate(one, axis=0).astype(BF16) for one in ones]
    rows_in = jnp.concatenate(values, axis=0)
    out_ref[...] = dot(sum(ones), rows_in[:, :width], (0, 0)).astype(BF16)
    for k in range(choose):
        parts = dot(rows_in[:, width:], ones[k], (0, 0))
        gate_ref[k : k + 1, :] = (parts[0:1, :] + parts[1:2, :]) / gates_ref[k : k + 1, :].astype(F32)


def whole():
    return pl.BlockSpec(memory_space=pltpu.VMEM)


def call(kernel, out_shape, scalars, *args, flops=0):
    nbytes = sum(a.size * a.dtype.itemsize for a in args) + sum(
        math.prod(o.shape) * o.dtype.itemsize for o in out_shape
    )
    return pl.pallas_call(
        kernel,
        out_shape=tuple(out_shape),
        in_specs=[pl.BlockSpec(memory_space=pltpu.SMEM)] * len(scalars) + [whole()] * len(args),
        out_specs=tuple(whole() for _ in out_shape),
        compiler_params=pltpu.CompilerParams(vmem_limit_bytes=VMEM_LIMIT),
        cost_estimate=pl.CostEstimate(flops=flops, bytes_accessed=nbytes, transcendentals=0),
    )(*scalars, *args)


def weight_grad(lefts, rights, received=None, scale=None):
    rows_of = [left.shape[0] for left in lefts]
    depth, columns = lefts[0].shape[1], rights[0].shape[1]
    tile = 512 if depth % 512 == 0 else depth
    if depth <= 512:
        tile = 128
    in_specs = [pl.BlockSpec((r, tile), lambda i: (0, i)) for r in rows_of]
    in_specs += [pl.BlockSpec((r, columns), lambda i: (0, 0)) for r in rows_of]
    args = [*lefts, *rights]
    if received is not None:
        in_specs.append(pl.BlockSpec((tile, columns), lambda i: (i, 0)))
        args.append(received)
    return pl.pallas_call(
        functools.partial(weight_kernel, len(lefts), scale),
        grid=(depth // tile,),
        out_shape=jax.ShapeDtypeStruct((depth, columns), BF16),
        in_specs=in_specs,
        out_specs=pl.BlockSpec((tile, columns), lambda i: (i, 0)),
        compiler_params=pltpu.CompilerParams(vmem_limit_bytes=VMEM_LIMIT),
        cost_estimate=pl.CostEstimate(
            flops=2 * sum(rows_of) * depth * columns,
            bytes_accessed=2 * (sum(rows_of) * (depth + columns) + depth * columns),
            transcendentals=0,
        ),
    )(*args)


def per_device(upstream, inputs, expert_ids, gate_weights, w_in, w_down):
    devices = lax.axis_size("ep")
    experts = devices // 2
    tokens, features = upstream.shape
    choose = expert_ids.shape[1]
    routed = tokens * choose
    capacity = routed * 3 // devices
    half = w_down.shape[1]
    room = -(-capacity // 16) * 16
    spans = [(0, room)] if room <= 16 else [(0, room - 16), (room - 16, 16)]
    chip = (lax.axis_index("ep") // 2).astype(jnp.int32).reshape(1)
    ids, gates = expert_ids.T, gate_weights.T
    factor = 1.0 / math.sqrt(2 * routed)

    def swap(value):
        return lax.ppermute(value, "ep", [(d, d ^ 1) for d in range(devices)])

    def exchange(blocks):
        return [
            block if step == 0 else lax.ppermute(block, "ep", [(d, d ^ (2 * step)) for d in range(devices)])
            for step, block in enumerate(blocks)
        ]

    own_in, own_down = w_in[0], w_down[0]
    other_in, other_down = swap(own_in), swap(own_down)

    arrived = []
    for first, rows in spans:
        sent = call(
            functools.partial(pack_kernel, experts, first, rows),
            [jax.ShapeDtypeStruct((rows, 2 * features), BF16)] * experts,
            [chip],
            ids,
            gates,
            inputs,
            upstream,
            flops=4 * rows * experts * tokens * features,
        )
        arrived.append(exchange(sent))

    returned, x_all, up_all, own_grad, other_grad, own_hidden, other_hidden = [], [], [], [], [], [], []
    for (first, rows), blocks in zip(spans, arrived):
        total = rows * experts
        out = call(
            functools.partial(expert_kernel, experts, rows),
            [jax.ShapeDtypeStruct((rows, features + LANES), BF16)] * experts
            + [jax.ShapeDtypeStruct((total, features), BF16)] * 2
            + [jax.ShapeDtypeStruct((total, 2 * half), BF16)] * 2
            + [jax.ShapeDtypeStruct((total, half), BF16)] * 2,
            [],
            *blocks,
            own_in,
            other_in,
            own_down,
            other_down,
            flops=20 * total * half * features,
        )
        returned += exchange(out[:experts])
        for keep, value in zip((x_all, up_all, own_grad, other_grad, own_hidden, other_hidden), out[experts:]):
            keep.append(value)

    other_part_in = swap(weight_grad(x_all, other_grad))
    other_part_down = swap(weight_grad(other_hidden, up_all))
    grad_in = weight_grad(x_all, own_grad, other_part_in, factor)
    grad_down = weight_grad(own_hidden, up_all, other_part_down, factor)

    grad_inputs, grad_gates = call(
        functools.partial(combine_kernel, experts, spans),
        [jax.ShapeDtypeStruct((tokens, features), BF16), jax.ShapeDtypeStruct((choose, tokens), F32)],
        [chip],
        ids,
        gates,
        *returned,
        flops=2 * room * experts * tokens * features,
    )
    return (grad_inputs, grad_gates.T, grad_in[None], grad_down[None])


def solution(mesh):
    rows = P(("grp", "ep"), None)
    return jax.shard_map(
        per_device,
        mesh=mesh,
        in_specs=(rows, rows, rows, rows, P("ep", None, None), P("ep", None, None)),
        out_specs=(rows, rows, P(("grp", "ep"), None, None), P(("grp", "ep"), None, None)),
        check_vma=False,
    )
```

time: 292 us -> 161 us (0.55)
  the two profiles are of different devices: /device:TPU:15 before, /device:TPU:0 now
where the time goes in v1:
time: 161 us
  waiting for transfers between devices  65.5 us (41%)
  starting transfers between devices  60.1 us (37%)
  Pallas kernels  26 us (16%)
  local copies, waits for them, and re-layouts  8.62 us (5%)
    ppermute x28, waiting for transfers between devices, exchange(): lax.ppermute(block, 'ep', [(d, d ^ 2 * step) for d in range(devices)])  65.5 us
    ppermute x28, starting transfers between devices, exchange(): lax.ppermute(block, 'ep', [(d, d ^ 2 * step) for d in range(devices)])  58.9 us
    pallas_call x5, Pallas kernels, call(): pl.pallas_call(kernel, out_shape=tuple(out_shape), in_specs=[pl.BlockSpec...  15.5 us
    pallas_call x4, Pallas kernels, weight_grad(): pl.pallas_call(functools.partial(weight_kernel, len(lefts), scale), grid=...  10.5 us
    unnamed x22, local copies, waits for them, and re-layouts  8.62 us
  transfers between devices with their start and end apart: 32, of which 12 were waited for; matrix products, arithmetic and copies ran while one was open for 0% of the time, Pallas kernels for 9%

profile of v1, /device:TPU:0, one launch (start us, length us, event | category | flops | bytes accessed | tf_op | source)
XLA Modules:
  0.0 161.1 jit_solution(16445281907764581125)
XLA Ops:
  5.5 3.0 %collective-permute-start = (bf16[32,4096]{1,0:T(8,128)(2,1)S(1)}, bf16[32,4096]{1,0:T(8,128)(2,1)S(1)}, u32[]{:S(2)}, u32[]{:S(2)}) collective-permute-start(bf16[32,4096]{1,0:T(8,128)(2,1)S(1)} %get-tuple-element.51), channel_id=1, source_target_pairs={{0,2},{1,3},{2,0},{3,1},{4,6},{5,7},{6,4},{7,5},{8,10},{9,11},{10,... | collective-permute-start | bytes 786440 | tf_op jit(solution)/shard_map/ppermute | solution.py:187
  11.2 6.6 %collective-permute-done.16.refs_1_ = bf16[16,4096]{1,0:T(8,128)(2,1)S(1)} collective-permute-done((bf16[16,4096]{1,0:T(8,128)(2,1)S(1)}, bf16[16,4096]{1,0:T(8,128)(2,1)S(1)}, u32[]{:S(2)}, u32[]{:S(2)}) %collective-permute-start.16) | collective-permute-done | bytes 131104 | tf_op jit(solution)/shard_map/ppermute | solution.py:187
  21.1 2.6 %collective-permute-start.3 = (bf16[32,4096]{1,0:T(8,128)(2,1)S(1)}, bf16[32,4096]{1,0:T(8,128)(2,1)S(1)}, u32[]{:S(2)}, u32[]{:S(2)}) collective-permute-start(bf16[32,4096]{1,0:T(8,128)(2,1)S(1)} %get-tuple-element.54), channel_id=1, source_target_pairs={{0,8},{1,9},{2,10},{3,11},{4,12},{5,13},{6,14},{7,15},{8,0},{9,1},... | collective-permute-start | bytes 786440 | tf_op jit(solution)/shard_map/ppermute | solution.py:187
  23.7 9.1 %collective-permute-done.1.refs_2_ = bf16[32,4096]{1,0:T(8,128)(2,1)S(1)} collective-permute-done((bf16[32,4096]{1,0:T(8,128)(2,1)S(1)}, bf16[32,4096]{1,0:T(8,128)(2,1)S(1)}, u32[]{:S(2)}, u32[]{:S(2)}) %collective-permute-start.1) | collective-permute-done | bytes 262176 | tf_op jit(solution)/shard_map/ppermute | solution.py:187
  32.7 2.9 %collective-permute-start.4 = (bf16[32,4096]{1,0:T(8,128)(2,1)S(1)}, bf16[32,4096]{1,0:T(8,128)(2,1)S(1)}, u32[]{:S(2)}, u32[]{:S(2)}) collective-permute-start(bf16[32,4096]{1,0:T(8,128)(2,1)S(1)} %get-tuple-element.55), channel_id=1, source_target_pairs={{0,10},{1,11},{2,8},{3,9},{4,14},{5,15},{6,12},{7,13},{8,2},{9,3},... | collective-permute-start | bytes 786440 | tf_op jit(solution)/shard_map/ppermute | solution.py:187
  35.6 3.1 %collective-permute-done.2.refs_3_ = bf16[32,4096]{1,0:T(8,128)(2,1)S(1)} collective-permute-done((bf16[32,4096]{1,0:T(8,128)(2,1)S(1)}, bf16[32,4096]{1,0:T(8,128)(2,1)S(1)}, u32[]{:S(2)}, u32[]{:S(2)}) %collective-permute-start.2) | collective-permute-done | bytes 262176 | tf_op jit(solution)/shard_map/ppermute | solution.py:187
  38.6 2.8 %collective-permute-start.5 = (bf16[32,4096]{1,0:T(8,128)(2,1)S(1)}, bf16[32,4096]{1,0:T(8,128)(2,1)S(1)}, u32[]{:S(2)}, u32[]{:S(2)}) collective-permute-start(bf16[32,4096]{1,0:T(8,128)(2,1)S(1)} %get-tuple-element.56), channel_id=1, source_target_pairs={{0,12},{1,13},{2,14},{3,15},{4,8},{5,9},{6,10},{7,11},{8,4},{9,5},... | collective-permute-start | bytes 786440 | tf_op jit(solution)/shard_map/ppermute | solution.py:187
  42.2 20.2 %collective-permute-done.4.refs_5_ = bf16[32,4096]{1,0:T(8,128)(2,1)S(1)} collective-permute-done((bf16[32,4096]{1,0:T(8,128)(2,1)S(1)}, bf16[32,4096]{1,0:T(8,128)(2,1)S(1)}, u32[]{:S(2)}, u32[]{:S(2)}) %collective-permute-start.4) | collective-permute-done | bytes 262176 | tf_op jit(solution)/shard_map/ppermute | solution.py:187
  62.4 5.0 %collective-permute-start.19 = (bf16[16,4096]{1,0:T(8,128)(2,1)S(1)}, bf16[16,4096]{1,0:T(8,128)(2,1)S(1)}, u32[]{:S(2)}, u32[]{:S(2)}) collective-permute-start(bf16[16,4096]{1,0:T(8,128)(2,1)S(1)} %get-tuple-element.70), channel_id=1, source_target_pairs={{0,8},{1,9},{2,10},{3,11},{4,12},{5,13},{6,14},{7,15},{8,0},{9,1},... | collective-permute-start | bytes 393224 | tf_op jit(solution)/shard_map/ppermute | solution.py:187
  67.4 9.7 %collective-permute-start.20 = (bf16[16,4096]{1,0:T(8,128)(2,1)S(1)}, bf16[16,4096]{1,0:T(8,128)(2,1)S(1)}, u32[]{:S(2)}, u32[]{:S(2)}) collective-permute-start(bf16[16,4096]{1,0:T(8,128)(2,1)S(1)} %get-tuple-element.71), channel_id=1, source_target_pairs={{0,10},{1,11},{2,8},{3,9},{4,14},{5,15},{6,12},{7,13},{8,2},{9,3},... | collective-permute-start | bytes 393224 | tf_op jit(solution)/shard_map/ppermute | solution.py:187
  77.2 2.5 %collective-permute-start.21 = (bf16[16,4096]{1,0:T(8,128)(2,1)S(1)}, bf16[16,4096]{1,0:T(8,128)(2,1)S(1)}, u32[]{:S(2)}, u32[]{:S(2)}) collective-permute-start(bf16[16,4096]{1,0:T(8,128)(2,1)S(1)} %get-tuple-element.72), channel_id=1, source_target_pairs={{0,12},{1,13},{2,14},{3,15},{4,8},{5,9},{6,10},{7,11},{8,4},{9,5},... | collective-permute-start | bytes 393224 | tf_op jit(solution)/shard_map/ppermute | solution.py:187
  84.8 7.3 %shard_map.94 = (bf16[32,2176]{1,0:T(8,128)(2,1)S(1)}, bf16[32,2176]{1,0:T(8,128)(2,1)S(1)}, bf16[32,2176]{1,0:T(8,128)(2,1)S(1)}, bf16[32,2176]{1,0:T(8,128)(2,...) custom-call(bf16[32,4096]{1,0:T(8,128)(2,1)S(1)} %get-tuple-element., ...), custom_call_target="tpu_custom_call" | custom-call | flops 4026531840 | bytes 15925248 | tf_op jit(solution)/shard_map/pallas_call | solution.py:131
  94.1 5.4 %shard_map.96 = (bf16[16,2176]{1,0:T(8,128)(2,1)S(1)}, bf16[16,2176]{1,0:T(8,128)(2,1)S(1)}, bf16[16,2176]{1,0:T(8,128)(2,1)S(1)}, bf16[16,2176]{1,0:T(8,128)(2,...) custom-call(bf16[16,4096]{1,0:T(8,128)(2,1)S(1)} %get-tuple-element., ...), custom_call_target="tpu_custom_call" | custom-call | flops 2013265920 | bytes 12681216 | tf_op jit(solution)/shard_map/pallas_call | solution.py:131
  99.5 2.8 %shard_map.98 = bf16[2048,768]{1,0:T(8,128)(2,1)S(1)} custom-call(bf16[256,2048]{1,0:T(8,128)(2,1)S(1)} %get-tuple-element.84.refs_0_, bf16[128,2048]{1,0:T(8,128)(2,1)S(1)} %get-tuple-element.85.refs_1_, bf16[256,768]{1,0:T(8,128)(2,1)S(1)} %get-tuple-element.88.refs_2_, bf16[128,768]{1,0:T(8,128)(2,1)S(1)} %get-tuple-element.89.refs_3_), custom_call_target="tpu_custom_call" | custom-call | flops 1207959552 | bytes 5308416 | tf_op jit(solution)/shard_map/pallas_call | solution.py:153
  105.3 3.7 %collective-permute-start.24 = (bf16[16,2176]{1,0:T(8,128)(2,1)S(1)}, bf16[16,2176]{1,0:T(8,128)(2,1)S(1)}, u32[]{:S(2)}, u32[]{:S(2)}) collective-permute-start(bf16[16,2176]{1,0:T(8,128)(2,1)S(1)} %get-tuple-element.76), channel_id=1, source_target_pairs={{0,4},{1,5},{2,6},{3,7},{4,0},{5,1},{6,2},{7,3},{8,12},{9,13},{10,... | collective-permute-start | bytes 208904 | tf_op jit(solution)/shard_map/ppermute | solution.py:187
  109.4 3.5 %collective-permute-start.26 = (bf16[16,2176]{1,0:T(8,128)(2,1)S(1)}, bf16[16,2176]{1,0:T(8,128)(2,1)S(1)}, u32[]{:S(2)}, u32[]{:S(2)}) collective-permute-start(bf16[16,2176]{1,0:T(8,128)(2,1)S(1)} %get-tuple-element.78), channel_id=1, source_target_pairs={{0,8},{1,9},{2,10},{3,11},{4,12},{5,13},{6,14},{7,15},{8,0},{9,1},... | collective-permute-start | bytes 208904 | tf_op jit(solution)/shard_map/ppermute | solution.py:187
  121.3 2.3 %collective-permute-start.29 = (bf16[16,2176]{1,0:T(8,128)(2,1)S(1)}, bf16[16,2176]{1,0:T(8,128)(2,1)S(1)}, u32[]{:S(2)}, u32[]{:S(2)}) collective-permute-start(bf16[16,2176]{1,0:T(8,128)(2,1)S(1)} %get-tuple-element.81), channel_id=1, source_target_pairs={{0,14},{1,15},{2,12},{3,13},{4,10},{5,11},{6,8},{7,9},{8,6},{9,7},... | collective-permute-start | bytes 208904 | tf_op jit(solution)/shard_map/ppermute | solution.py:187
  123.8 5.3 %collective-permute-done.29.refs_15_ = bf16[16,2176]{1,0:T(8,128)(2,1)S(1)} collective-permute-done((bf16[16,2176]{1,0:T(8,128)(2,1)S(1)}, bf16[16,2176]{1,0:T(8,128)(2,1)S(1)}, u32[]{:S(2)}, u32[]{:S(2)}) %collective-permute-start.29) | collective-permute-done | bytes 69664 | tf_op jit(solution)/shard_map/ppermute | solution.py:187
  132.1 3.9 %collective-permute-done.11.refs_3_ = bf16[32,2176]{1,0:T(8,128)(2,1)S(1)} collective-permute-done((bf16[32,2176]{1,0:T(8,128)(2,1)S(1)}, bf16[32,2176]{1,0:T(8,128)(2,1)S(1)}, u32[]{:S(2)}, u32[]{:S(2)}) %collective-permute-start.11) | collective-permute-done | bytes 139296 | tf_op jit(solution)/shard_map/ppermute | solution.py:187
  137.8 7.7 %collective-permute-done.12.refs_4_ = bf16[32,2176]{1,0:T(8,128)(2,1)S(1)} collective-permute-done((bf16[32,2176]{1,0:T(8,128)(2,1)S(1)}, bf16[32,2176]{1,0:T(8,128)(2,1)S(1)}, u32[]{:S(2)}, u32[]{:S(2)}) %collective-permute-start.12) | collective-permute-done | bytes 139296 | tf_op jit(solution)/shard_map/ppermute | solution.py:187
  145.6 2.4 %collective-permute-start.15 = (bf16[32,2176]{1,0:T(8,128)(2,1)S(1)}, bf16[32,2176]{1,0:T(8,128)(2,1)S(1)}, u32[]{:S(2)}, u32[]{:S(2)}) collective-permute-start(bf16[32,2176]{1,0:T(8,128)(2,1)S(1)} %get-tuple-element.65), channel_id=1, source_target_pairs={{0,14},{1,15},{2,12},{3,13},{4,10},{5,11},{6,8},{7,9},{8,6},{9,7},... | collective-permute-start | bytes 417800 | tf_op jit(solution)/shard_map/ppermute | solution.py:187
  149.0 4.4 %collective-permute-done.15.refs_7_ = bf16[32,2176]{1,0:T(8,128)(2,1)S(1)} collective-permute-done((bf16[32,2176]{1,0:T(8,128)(2,1)S(1)}, bf16[32,2176]{1,0:T(8,128)(2,1)S(1)}, u32[]{:S(2)}, u32[]{:S(2)}) %collective-permute-start.15) | collective-permute-done | bytes 139296 | tf_op jit(solution)/shard_map/ppermute | solution.py:187
  154.8 2.6 %shard_map.101 = bf16[384,2048]{1,0:T(8,128)(2,1)} custom-call(bf16[256,384]{1,0:T(8,128)(2,1)S(1)} %get-tuple-element.90.refs_0_, bf16[128,384]{1,0:T(8,128)(2,1)S(1)} %get-tuple-element.91.refs_1_, bf16[256,2048]{1,0:T(8,128)(2,1)S(1)} %get-tuple-element.92.refs_2_, bf16[128,2048]{1,0:T(8,128)(2,1)S(1)} %get-tuple-element.93.refs_3_, ...), custom_call_target="tpu_custom_call" | custom-call | flops 603979776 | bytes 3440640 | tf_op jit(solution)/shard_map/pallas_call | solution.py:153
  157.4 3.7 %shard_map.99 = bf16[2048,768]{1,0:T(8,128)(2,1)} custom-call(bf16[256,2048]{1,0:T(8,128)(2,1)S(1)} %get-tuple-element.84.refs_0_, bf16[128,2048]{1,0:T(8,128)(2,1)S(1)} %get-tuple-element.85.refs_1_, bf16[256,768]{1,0:T(8,128)(2,1)S(1)} %get-tuple-element.86.refs_2_, bf16[128,768]{1,0:T(8,128)(2,1)S(1)} %get-tuple-element.87.refs_3_, ...), custom_call_target="tpu_custom_call" | custom-call | flops 1207959552 | bytes 5308416 | tf_op jit(solution)/shard_map/pallas_call | solution.py:153
  (71 shorter events, 38.0 us)
Async XLA Ops:
  0.6 79.0 %collective-permute-start.7 = (bf16[2048,768]{1,0:T(8,128)(2,1)}, bf16[2048,768]{1,0:T(8,128)(2,1)S(1)}, u32[]{:S(2)}, u32[]{:S(2)}) collective-permute-start(bf16[2048,768]{1,0:T(8,128)(2,1)} %bitcast.8), channel_id=1, source_target_pairs={{0,1},{1,0},{2,3},{3,2},{4,5},{5,4},{6,7},{7,6},{8,9},{9,8},{10,11... | collective-permute-start | bytes 9437192 | tf_op jit(solution)/shard_map/ppermute | solution.py:183
  1.1 76.0 %collective-permute-start.8 = (bf16[384,2048]{1,0:T(8,128)(2,1)}, bf16[384,2048]{1,0:T(8,128)(2,1)}, u32[]{:S(2)}, u32[]{:S(2)}) collective-permute-start(bf16[384,2048]{1,0:T(8,128)(2,1)} %bitcast.11), channel_id=1, source_target_pairs={{0,1},{1,0},{2,3},{3,2},{4,5},{5,4},{6,7},{7,6},{8,9},{9,8},{10,11... | collective-permute-start | bytes 4718600 | tf_op jit(solution)/shard_map/ppermute | solution.py:183
  5.5 15.6 %collective-permute-start = (bf16[32,4096]{1,0:T(8,128)(2,1)S(1)}, bf16[32,4096]{1,0:T(8,128)(2,1)S(1)}, u32[]{:S(2)}, u32[]{:S(2)}) collective-permute-start(bf16[32,4096]{1,0:T(8,128)(2,1)S(1)} %get-tuple-element.51), channel_id=1, source_target_pairs={{0,2},{1,3},{2,0},{3,1},{4,6},{5,7},{6,4},{7,5},{8,10},{9,11},{10,... | collective-permute-start | bytes 786440 | tf_op jit(solution)/shard_map/ppermute | solution.py:187
  9.1 8.8 %collective-permute-start.16 = (bf16[16,4096]{1,0:T(8,128)(2,1)S(1)}, bf16[16,4096]{1,0:T(8,128)(2,1)S(1)}, u32[]{:S(2)}, u32[]{:S(2)}) collective-permute-start(bf16[16,4096]{1,0:T(8,128)(2,1)S(1)} %get-tuple-element.67), channel_id=1, source_target_pairs={{0,2},{1,3},{2,0},{3,1},{4,6},{5,7},{6,4},{7,5},{8,10},{9,11},{10,... | collective-permute-start | bytes 393224 | tf_op jit(solution)/shard_map/ppermute | solution.py:187
  9.2 10.5 %collective-permute-start.17 = (bf16[16,4096]{1,0:T(8,128)(2,1)S(1)}, bf16[16,4096]{1,0:T(8,128)(2,1)S(1)}, u32[]{:S(2)}, u32[]{:S(2)}) collective-permute-start(bf16[16,4096]{1,0:T(8,128)(2,1)S(1)} %get-tuple-element.68), channel_id=1, source_target_pairs={{0,4},{1,5},{2,6},{3,7},{4,0},{5,1},{6,2},{7,3},{8,12},{9,13},{10,... | collective-permute-start | bytes 393224 | tf_op jit(solution)/shard_map/ppermute | solution.py:187
  17.9 14.8 %collective-permute-start.1 = (bf16[32,4096]{1,0:T(8,128)(2,1)S(1)}, bf16[32,4096]{1,0:T(8,128)(2,1)S(1)}, u32[]{:S(2)}, u32[]{:S(2)}) collective-permute-start(bf16[32,4096]{1,0:T(8,128)(2,1)S(1)} %get-tuple-element.52), channel_id=1, source_target_pairs={{0,4},{1,5},{2,6},{3,7},{4,0},{5,1},{6,2},{7,3},{8,12},{9,13},{10,... | collective-permute-start | bytes 786440 | tf_op jit(solution)/shard_map/ppermute | solution.py:187
  19.7 19.0 %collective-permute-start.2 = (bf16[32,4096]{1,0:T(8,128)(2,1)S(1)}, bf16[32,4096]{1,0:T(8,128)(2,1)S(1)}, u32[]{:S(2)}, u32[]{:S(2)}) collective-permute-start(bf16[32,4096]{1,0:T(8,128)(2,1)S(1)} %get-tuple-element.53), channel_id=1, source_target_pairs={{0,6},{1,7},{2,4},{3,5},{4,2},{5,3},{6,0},{7,1},{8,14},{9,15},{10,... | collective-permute-start | bytes 786440 | tf_op jit(solution)/shard_map/ppermute | solution.py:187
  21.1 20.4 %collective-permute-start.3 = (bf16[32,4096]{1,0:T(8,128)(2,1)S(1)}, bf16[32,4096]{1,0:T(8,128)(2,1)S(1)}, u32[]{:S(2)}, u32[]{:S(2)}) collective-permute-start(bf16[32,4096]{1,0:T(8,128)(2,1)S(1)} %get-tuple-element.54), channel_id=1, source_target_pairs={{0,8},{1,9},{2,10},{3,11},{4,12},{5,13},{6,14},{7,15},{8,0},{9,1},... | collective-permute-start | bytes 786440 | tf_op jit(solution)/shard_map/ppermute | solution.py:187
  32.7 29.7 %collective-permute-start.4 = (bf16[32,4096]{1,0:T(8,128)(2,1)S(1)}, bf16[32,4096]{1,0:T(8,128)(2,1)S(1)}, u32[]{:S(2)}, u32[]{:S(2)}) collective-permute-start(bf16[32,4096]{1,0:T(8,128)(2,1)S(1)} %get-tuple-element.55), channel_id=1, source_target_pairs={{0,10},{1,11},{2,8},{3,9},{4,14},{5,15},{6,12},{7,13},{8,2},{9,3},... | collective-permute-start | bytes 786440 | tf_op jit(solution)/shard_map/ppermute | solution.py:187
  38.6 23.7 %collective-permute-start.5 = (bf16[32,4096]{1,0:T(8,128)(2,1)S(1)}, bf16[32,4096]{1,0:T(8,128)(2,1)S(1)}, u32[]{:S(2)}, u32[]{:S(2)}) collective-permute-start(bf16[32,4096]{1,0:T(8,128)(2,1)S(1)} %get-tuple-element.56), channel_id=1, source_target_pairs={{0,12},{1,13},{2,14},{3,15},{4,8},{5,9},{6,10},{7,11},{8,4},{9,5},... | collective-permute-start | bytes 786440 | tf_op jit(solution)/shard_map/ppermute | solution.py:187
  41.4 26.0 %collective-permute-start.6 = (bf16[32,4096]{1,0:T(8,128)(2,1)S(1)}, bf16[32,4096]{1,0:T(8,128)(2,1)S(1)}, u32[]{:S(2)}, u32[]{:S(2)}) collective-permute-start(bf16[32,4096]{1,0:T(8,128)(2,1)S(1)} %get-tuple-element.57), channel_id=1, source_target_pairs={{0,14},{1,15},{2,12},{3,13},{4,10},{5,11},{6,8},{7,9},{8,6},{9,7},... | collective-permute-start | bytes 786440 | tf_op jit(solution)/shard_map/ppermute | solution.py:187
  62.4 29.8 %collective-permute-start.18 = (bf16[16,4096]{1,0:T(8,128)(2,1)S(1)}, bf16[16,4096]{1,0:T(8,128)(2,1)S(1)}, u32[]{:S(2)}, u32[]{:S(2)}) collective-permute-start(bf16[16,4096]{1,0:T(8,128)(2,1)S(1)} %get-tuple-element.69), channel_id=1, source_target_pairs={{0,6},{1,7},{2,4},{3,5},{4,2},{5,3},{6,0},{7,1},{8,14},{9,15},{10,... | collective-permute-start | bytes 393224 | tf_op jit(solution)/shard_map/ppermute | solution.py:187
  62.4 29.8 %collective-permute-start.19 = (bf16[16,4096]{1,0:T(8,128)(2,1)S(1)}, bf16[16,4096]{1,0:T(8,128)(2,1)S(1)}, u32[]{:S(2)}, u32[]{:S(2)}) collective-permute-start(bf16[16,4096]{1,0:T(8,128)(2,1)S(1)} %get-tuple-element.70), channel_id=1, source_target_pairs={{0,8},{1,9},{2,10},{3,11},{4,12},{5,13},{6,14},{7,15},{8,0},{9,1},... | collective-permute-start | bytes 393224 | tf_op jit(solution)/shard_map/ppermute | solution.py:187
  67.4 24.7 %collective-permute-start.20 = (bf16[16,4096]{1,0:T(8,128)(2,1)S(1)}, bf16[16,4096]{1,0:T(8,128)(2,1)S(1)}, u32[]{:S(2)}, u32[]{:S(2)}) collective-permute-start(bf16[16,4096]{1,0:T(8,128)(2,1)S(1)} %get-tuple-element.71), channel_id=1, source_target_pairs={{0,10},{1,11},{2,8},{3,9},{4,14},{5,15},{6,12},{7,13},{8,2},{9,3},... | collective-permute-start | bytes 393224 | tf_op jit(solution)/shard_map/ppermute | solution.py:187
  77.2 15.0 %collective-permute-start.21 = (bf16[16,4096]{1,0:T(8,128)(2,1)S(1)}, bf16[16,4096]{1,0:T(8,128)(2,1)S(1)}, u32[]{:S(2)}, u32[]{:S(2)}) collective-permute-start(bf16[16,4096]{1,0:T(8,128)(2,1)S(1)} %get-tuple-element.72), channel_id=1, source_target_pairs={{0,12},{1,13},{2,14},{3,15},{4,8},{5,9},{6,10},{7,11},{8,4},{9,5},... | collective-permute-start | bytes 393224 | tf_op jit(solution)/shard_map/ppermute | solution.py:187
  79.7 12.5 %collective-permute-start.22 = (bf16[16,4096]{1,0:T(8,128)(2,1)S(1)}, bf16[16,4096]{1,0:T(8,128)(2,1)S(1)}, u32[]{:S(2)}, u32[]{:S(2)}) collective-permute-start(bf16[16,4096]{1,0:T(8,128)(2,1)S(1)} %get-tuple-element.73), channel_id=1, source_target_pairs={{0,14},{1,15},{2,12},{3,13},{4,10},{5,11},{6,8},{7,9},{8,6},{9,7},... | collective-permute-start | bytes 393224 | tf_op jit(solution)/shard_map/ppermute | solution.py:187
  102.3 55.1 %collective-permute-start.30 = (bf16[2048,768]{1,0:T(8,128)(2,1)S(1)}, bf16[2048,768]{1,0:T(8,128)(2,1)S(1)}, u32[]{:S(2)}, u32[]{:S(2)}) collective-permute-start(bf16[2048,768]{1,0:T(8,128)(2,1)S(1)} %shard_map.98), channel_id=1, source_target_pairs={{0,1},{1,0},{2,3},{3,2},{4,5},{5,4},{6,7},{7,6},{8,9},{9,8},{10,11... | collective-permute-start | bytes 9437192 | tf_op jit(solution)/shard_map/ppermute | solution.py:183
  103.9 51.0 %collective-permute-start.31 = (bf16[384,2048]{1,0:T(8,128)(2,1)S(1)}, bf16[384,2048]{1,0:T(8,128)(2,1)S(1)}, u32[]{:S(2)}, u32[]{:S(2)}) collective-permute-start(bf16[384,2048]{1,0:T(8,128)(2,1)S(1)} %shard_map.100), channel_id=1, source_target_pairs={{0,1},{1,0},{2,3},{3,2},{4,5},{5,4},{6,7},{7,6},{8,9},{9,8},{10,11... | collective-permute-start | bytes 4718600 | tf_op jit(solution)/shard_map/ppermute | solution.py:183
  109.4 8.3 %collective-permute-start.26 = (bf16[16,2176]{1,0:T(8,128)(2,1)S(1)}, bf16[16,2176]{1,0:T(8,128)(2,1)S(1)}, u32[]{:S(2)}, u32[]{:S(2)}) collective-permute-start(bf16[16,2176]{1,0:T(8,128)(2,1)S(1)} %get-tuple-element.78), channel_id=1, source_target_pairs={{0,8},{1,9},{2,10},{3,11},{4,12},{5,13},{6,14},{7,15},{8,0},{9,1},... | collective-permute-start | bytes 208904 | tf_op jit(solution)/shard_map/ppermute | solution.py:187
  112.9 8.4 %collective-permute-start.27 = (bf16[16,2176]{1,0:T(8,128)(2,1)S(1)}, bf16[16,2176]{1,0:T(8,128)(2,1)S(1)}, u32[]{:S(2)}, u32[]{:S(2)}) collective-permute-start(bf16[16,2176]{1,0:T(8,128)(2,1)S(1)} %get-tuple-element.79), channel_id=1, source_target_pairs={{0,10},{1,11},{2,8},{3,9},{4,14},{5,15},{6,12},{7,13},{8,2},{9,3},... | collective-permute-start | bytes 208904 | tf_op jit(solution)/shard_map/ppermute | solution.py:187
  114.7 14.4 %collective-permute-start.9 = (bf16[32,2176]{1,0:T(8,128)(2,1)S(1)}, bf16[32,2176]{1,0:T(8,128)(2,1)S(1)}, u32[]{:S(2)}, u32[]{:S(2)}) collective-permute-start(bf16[32,2176]{1,0:T(8,128)(2,1)S(1)} %get-tuple-element.59), channel_id=1, source_target_pairs={{0,2},{1,3},{2,0},{3,1},{4,6},{5,7},{6,4},{7,5},{8,10},{9,11},{10,... | collective-permute-start | bytes 417800 | tf_op jit(solution)/shard_map/ppermute | solution.py:187
  129.1 16.4 %collective-permute-start.12 = (bf16[32,2176]{1,0:T(8,128)(2,1)S(1)}, bf16[32,2176]{1,0:T(8,128)(2,1)S(1)}, u32[]{:S(2)}, u32[]{:S(2)}) collective-permute-start(bf16[32,2176]{1,0:T(8,128)(2,1)S(1)} %get-tuple-element.62), channel_id=1, source_target_pairs={{0,8},{1,9},{2,10},{3,11},{4,12},{5,13},{6,14},{7,15},{8,0},{9,1},... | collective-permute-start | bytes 417800 | tf_op jit(solution)/shard_map/ppermute | solution.py:187
  131.2 17.8 %collective-permute-start.13 = (bf16[32,2176]{1,0:T(8,128)(2,1)S(1)}, bf16[32,2176]{1,0:T(8,128)(2,1)S(1)}, u32[]{:S(2)}, u32[]{:S(2)}) collective-permute-start(bf16[32,2176]{1,0:T(8,128)(2,1)S(1)} %get-tuple-element.63), channel_id=1, source_target_pairs={{0,10},{1,11},{2,8},{3,9},{4,14},{5,15},{6,12},{7,13},{8,2},{9,3},... | collective-permute-start | bytes 417800 | tf_op jit(solution)/shard_map/ppermute | solution.py:187
  136.0 13.1 %collective-permute-start.14 = (bf16[32,2176]{1,0:T(8,128)(2,1)S(1)}, bf16[32,2176]{1,0:T(8,128)(2,1)S(1)}, u32[]{:S(2)}, u32[]{:S(2)}) collective-permute-start(bf16[32,2176]{1,0:T(8,128)(2,1)S(1)} %get-tuple-element.64), channel_id=1, source_target_pairs={{0,12},{1,13},{2,14},{3,15},{4,8},{5,9},{6,10},{7,11},{8,4},{9,5},... | collective-permute-start | bytes 417800 | tf_op jit(solution)/shard_map/ppermute | solution.py:187
  (19 other events, 179.8 us)

commit v2 on v1

v2 whole, which is shorter than its diff:
```python
import functools
import math

import jax
import jax.numpy as jnp
from jax import lax
from jax.experimental import pallas as pl
from jax.experimental.pallas import tpu as pltpu
from jax.sharding import PartitionSpec as P

F32 = jnp.float32
BF16 = jnp.bfloat16
LANES = 128
MIB = 1024 * 1024
ORDER = (1, 2, 6, 4, 7, 5, 3)
SLAB = 512
EARLY = 3


def dot(a, b, contract):
    return lax.dot_general(a, b, ((contract[:1], contract[1:]), ((), ())), preferred_element_type=F32)


def places(ids, experts):
    choose, tokens = ids.shape
    names = lax.broadcasted_iota(jnp.int32, (experts, tokens), 0)
    marks = [(names == ids[k : k + 1, :]).astype(F32) for k in range(choose)]
    earlier = lax.broadcasted_iota(jnp.int32, (tokens, tokens), 0) < lax.broadcasted_iota(
        jnp.int32, (tokens, tokens), 1
    )
    counts = dot(sum(marks).astype(BF16), earlier.astype(BF16), (1, 0))
    return [jnp.sum(counts * mark, axis=0, keepdims=True).astype(jnp.int32) for mark in marks]


def picks(ids, place, expert, first, rows):
    choose, tokens = ids.shape
    slot = lax.broadcasted_iota(jnp.int32, (rows, tokens), 0) + first
    return [
        ((ids[k : k + 1, :] == expert) & (place[k] == slot)).astype(F32) for k in range(choose)
    ]


def load(pairs, sems):
    copies = [pltpu.make_async_copy(a, b, sems.at[n]) for n, (a, b) in enumerate(pairs)]
    for copy in copies:
        copy.start()
    return copies


def targets(steps, experts, chip):
    return [chip ^ n if steps else n for n in range(experts)]


def rows_of(chip, step, rows):
    return pl.ds(pl.multiple_of((chip ^ step) * rows, 16), rows)


def pack_kernel(experts, rows, steps, with_x, held, chip_ref, *refs):
    hbm, refs = refs[: 3 + with_x], refs[3 + with_x + held :]
    sends, kept_ones = len(steps) + with_x, 2 * with_x
    ones_refs, refs = refs[sends : sends + kept_ones], refs[:sends] + refs[sends + kept_ones :]
    outs, local, sends_local, sems = refs[:sends], refs[sends : 2 * sends + 3 + with_x][: 3 + with_x], refs[-1 - sends : -1], refs[-1]
    copies = load(zip(hbm, local), sems)
    copies[0].wait()
    copies[1].wait()
    ids = local[0][...]
    gates = local[1][...].astype(F32)
    place = places(ids, experts)
    chip = chip_ref[0]
    gated = [
        sum(one * gates[k : k + 1, :] for k, one in enumerate(picks(ids, place, chip ^ step, 0, rows)))
        for step in steps
    ]
    kept = []
    if with_x:
        plain = [picks(ids, place, e, 0, rows) for e in range(experts)]
        for k, one_ref in enumerate(ones_refs):
            one_ref[...] = jnp.concatenate([one[k] for one in plain], axis=0).astype(BF16)
        copies[3].wait()
        x_rows = dot(sum(ref[...] for ref in ones_refs), local[3][...], (1, 0))
        sends_local[-1][...] = x_rows.astype(BF16)
        kept += load([(sends_local[-1], outs[-1])], sems.at[4:])
    copies[2].wait()
    up_rows = dot(jnp.concatenate(gated, axis=0).astype(BF16), local[2][...], (1, 0)).astype(BF16)
    for b in range(len(steps)):
        sends_local[b][...] = up_rows[b * rows : (b + 1) * rows]
    kept += load(zip(sends_local[: len(steps)], outs), sems.at[5:])
    for copy in kept:
        copy.wait()


def forward_kernel(steps, chip_ref, x_ref, *refs):
    w_in_refs, (x_out, *terms), x_local, sem = refs[:2], refs[2:-2], refs[-2], refs[-1]
    half = terms[0].shape[1]
    rows = x_ref.shape[0] // len(steps)
    for b, step in enumerate(steps):
        x_local[b * rows : (b + 1) * rows, :] = x_ref[rows_of(chip_ref[0], step, rows), :]
    x_rows = x_local[...]
    kept = load([(x_local, x_out)], sem)
    for h in range(2):
        slope_ref, active_ref, hidden_ref, hidden16_ref = terms[4 * h : 4 * h + 4]
        pre = dot(x_rows, w_in_refs[h][...], (1, 0))
        gate_pre, up_pre = pre[:, :half], pre[:, half:]
        squash = jax.nn.sigmoid(gate_pre)
        active = gate_pre * squash
        hidden = active * up_pre
        slope_ref[...] = up_pre * squash * (1.0 + gate_pre * (1.0 - squash))
        active_ref[...] = active
        hidden_ref[...] = hidden
        hidden16_ref[...] = hidden.astype(BF16)
    kept[0].wait()


def backward_kernel(steps, slab, chip_ref, *refs):
    count = len(steps)
    ins, terms, (w_down, other_down, w_in, other_in) = refs[:count], refs[count : count + 6], refs[count + 6 : count + 10]
    back_out, share_out, grad_out, grad_ref, share_ref, back_ref, sems = refs[-7:]
    total = grad_ref.shape[0]
    rows = total // count
    half, width = w_down.shape
    at = 4 * half
    for b, ref in enumerate(ins):
        share_ref[b * rows : (b + 1) * rows, at:] = ref[...]
    share_ref[:, 3 * half : at] = jnp.zeros((total, half), BF16)
    gate_parts = []
    for h, (weight, grad) in enumerate(((w_down, grad_ref), (other_down, share_ref))):
        slope, active, hidden = [ref[...] for ref in terms[3 * h : 3 * h + 3]]
        pulled = dot(share_ref[:, at:], weight[...], (1, 1))
        gate_parts.append(jnp.sum(hidden * pulled, axis=1, keepdims=True))
        grad[:, :half] = (pulled * slope).astype(BF16)
        grad[:, half : 2 * half] = (pulled * active).astype(BF16)
    share_ref[:, 2 * half : 3 * half] = hidden.astype(BF16)
    kept = load([(share_ref, share_out), (grad_ref, grad_out)], sems)
    lane = lax.broadcasted_iota(jnp.int32, (total, LANES), 1)
    back_ref[:, width:] = jnp.where(
        lane == 0, gate_parts[0], jnp.where(lane == 1, gate_parts[1], 0.0)
    ).astype(BF16)
    for n, first in enumerate(range(0, width, slab)):
        cut = slice(first, first + slab)
        back = dot(grad_ref[...], w_in[cut, :], (1, 1)) + dot(share_ref[:, : 2 * half], other_in[cut, :], (1, 1))
        back_ref[:, cut] = back.astype(BF16)
        if first + slab == width:
            cut = slice(first, width + LANES)
        kept += load(
            [
                (back_ref.at[b * rows : (b + 1) * rows, cut], back_out.at[rows_of(chip_ref[0], step, rows), cut])
                for b, step in enumerate(steps)
            ],
            sems.at[2 + n * count :],
        )
    for copy in kept:
        copy.wait()


def weight_kernel(count, scale, *refs):
    out_ref, lefts, rights = refs[-1], refs[:count], refs[count:-1]
    left = jnp.concatenate([ref[...] for ref in lefts], axis=0)
    right = jnp.concatenate([ref[...] for ref in rights], axis=0)
    out_ref[...] = (dot(left, right, (0, 0)) * scale).astype(BF16)


def combine_kernel(gates_ref, rows_ref, *refs):
    ones, (out_ref, gate_ref) = refs[:-4], refs[-2:]
    width = out_ref.shape[1]
    out_ref[...] = dot(sum(one[...] for one in ones), rows_ref[:, :width], (0, 0)).astype(BF16)
    for k, one in enumerate(ones):
        terms = dot(rows_ref[:, width:], one[...], (0, 0))
        gate_ref[k : k + 1, :] = (terms[0:1, :] + terms[1:2, :]) / gates_ref[k : k + 1, :].astype(F32)


def whole():
    return pl.BlockSpec(memory_space=pltpu.VMEM)


def anywhere(free=False):
    return pl.BlockSpec(memory_space=pl.ANY if free else pltpu.HBM)


def call(kernel, out_shape, chip, args, scratch, flops, mib, near=(), free=(), far_out=()):
    nbytes = sum(a.size * a.dtype.itemsize for a in args) + sum(
        math.prod(o.shape) * jnp.dtype(o.dtype).itemsize for o in out_shape
    )
    args = [
        a if n in free else pltpu.with_memory_space_constraint(a, pltpu.VMEM if n in near else pltpu.HBM)
        for n, a in enumerate(args)
    ]
    return pl.pallas_call(
        kernel,
        out_shape=tuple(out_shape),
        in_specs=[pl.BlockSpec(memory_space=pltpu.SMEM)] * len(chip)
        + [whole() if n in near else anywhere(n in free) for n in range(len(args))],
        out_specs=tuple(anywhere() if n in far_out else whole() for n in range(len(out_shape))),
        scratch_shapes=scratch,
        compiler_params=pltpu.CompilerParams(vmem_limit_bytes=mib * MIB),
        cost_estimate=pl.CostEstimate(flops=flops, bytes_accessed=nbytes, transcendentals=0),
    )(*chip, *args)


def weight_grad(lefts, rights, scale, by_left):
    depth, columns = lefts[0][2], rights[0][2]
    grid = (depth if by_left else columns) // 512
    rows = [array.shape[0] for array, _, _ in lefts]

    def spec(operand, cut):
        array, at, size = operand
        if cut:
            return pl.BlockSpec((array.shape[0], 512), lambda i: (0, at // 512 + i))
        return pl.BlockSpec((array.shape[0], size), lambda i: (0, at // size))

    return pl.pallas_call(
        functools.partial(weight_kernel, len(lefts), scale),
        grid=(grid,),
        out_shape=pltpu.HBM((depth, columns), BF16),
        in_specs=[spec(left, by_left) for left in lefts] + [spec(right, not by_left) for right in rights],
        out_specs=pl.BlockSpec((512, columns), lambda i: (i, 0)) if by_left else pl.BlockSpec((depth, 512), lambda i: (0, i)),
        compiler_params=pltpu.CompilerParams(vmem_limit_bytes=16 * MIB),
        cost_estimate=pl.CostEstimate(
            flops=2 * sum(rows) * depth * columns,
            bytes_accessed=2 * (sum(rows) * (depth + columns) + depth * columns),
            transcendentals=0,
        ),
    )(*[array for array, _, _ in lefts + rights])


def per_device(upstream, inputs, expert_ids, gate_weights, w_in, w_down):
    devices = lax.axis_size("ep")
    experts = devices // 2
    tokens, features = upstream.shape
    choose = expert_ids.shape[1]
    routed = tokens * choose
    capacity = routed * 3 // devices
    half = w_down.shape[1]
    rows = -(-capacity // 16) * 16
    total = rows * experts
    chip = [(lax.axis_index("ep") // 2).astype(jnp.int32).reshape(1)]
    ids, gates = expert_ids.T, gate_weights.T
    factor = 1.0 / math.sqrt(2 * routed)
    steps = (*(ORDER if experts == 8 else range(1, experts)), 0)
    groups = [[2 * e + c for e in range(experts)] for c in range(2)]

    def swap(value):
        return lax.ppermute(value, "ep", [(d, d ^ 1) for d in range(devices)])

    def send(blocks):
        return {
            step: lax.ppermute(blocks[step], "ep", [(d, d ^ (2 * step)) for d in range(devices)]) if step else blocks[0]
            for step in blocks
        }

    def send_all(block):
        return lax.all_to_all(block, "ep", 0, 0, axis_index_groups=groups, tiled=True)

    def like(*values):
        return [pltpu.VMEM(value.shape, value.dtype) for value in values]

    def far(rows, width):
        return pltpu.HBM((rows, width), BF16)

    def near(rows, width, dtype=BF16):
        return pltpu.VMEM((rows, width), dtype)

    def dma(count):
        return pltpu.SemaphoreType.DMA((count,))

    w_in, w_down = w_in[0], w_down[0]
    other_in, other_down = swap(w_in), swap(w_down)

    def pack(these, with_x, held=()):
        tokens_in = [ids, gates, upstream, inputs][: 3 + with_x]
        sends = [(rows, features)] * len(these) + [(total, features)] * with_x
        return call(
            functools.partial(pack_kernel, experts, rows, these, with_x, len(held)),
            [far(*size) for size in sends] + [near(total, tokens)] * (choose * with_x),
            chip,
            [*tokens_in, *held],
            like(*tokens_in) + [near(*size) for size in sends] + [dma(5 + len(these))],
            4 * total * tokens * features,
            16,
            (),
            tuple(range(3 + with_x, 3 + with_x + len(held))),
            tuple(range(len(sends))),
        )

    early = EARLY if experts == 8 else experts // 2
    *up_sent, x_sent, one, two = pack(steps[:early], 1)
    up_sent += pack(steps[early:], 0, [other_in, other_down])
    x_rows = send_all(x_sent)
    up_blocks = send(dict(zip(steps, up_sent)))

    x_rows, *terms = call(
        functools.partial(forward_kernel, steps),
        [far(total, features)] + ([near(total, half, F32)] * 3 + [near(total, half)]) * 2,
        chip,
        [x_rows, w_in, other_in],
        [near(total, features), dma(1)],
        8 * total * half * features,
        16,
        (0, 1, 2),
        (),
        (0,),
    )
    operands = [*terms[:3], *terms[4:7], w_down, other_down, w_in, other_in]
    width, share_width = features + LANES, features + 4 * half
    back, own_share, own_grad = call(
        functools.partial(backward_kernel, steps, SLAB),
        [far(total, width), far(total, share_width), far(total, 2 * half)],
        chip,
        [*[up_blocks[step] for step in steps], *operands],
        [near(total, 2 * half), near(total, share_width), near(total, width), dma(2 + experts * features // SLAB)],
        12 * total * half * features,
        16,
        tuple(range(experts + len(operands))),
        (),
        (0, 1, 2),
    )
    returned = send_all(back)

    other_share = swap(own_share)
    x_pairs = [(x_rows, 0, features), (swap(x_rows), 0, features)]
    grad_pairs = [(own_grad, 0, 2 * half), (other_share, 0, 2 * half)]
    grad_in = weight_grad(x_pairs, grad_pairs, factor, True)
    hidden_pairs = [(terms[3], 0, half), (other_share, 2 * half, half)]
    up_pairs = [(share, 4 * half, features) for share in (own_share, other_share)]
    grad_down = weight_grad(hidden_pairs, up_pairs, factor, False)

    grad_inputs, grad_gates = call(
        combine_kernel,
        [jax.ShapeDtypeStruct((tokens, features), BF16), jax.ShapeDtypeStruct((choose, tokens), F32)],
        [],
        [gates, returned, one, two, grad_in, grad_down],
        [],
        2 * total * tokens * features,
        12,
        (0, 1, 2, 3),
    )
    return (grad_inputs, grad_gates.T, grad_in[None], grad_down[None])


def solution(mesh):
    rows = P(("grp", "ep"), None)
    return jax.shard_map(
        per_device,
        mesh=mesh,
        in_specs=(rows, rows, rows, rows, P("ep", None, None), P("ep", None, None)),
        out_specs=(rows, rows, P(("grp", "ep"), None, None), P(("grp", "ep"), None, None)),
        check_vma=False,
    )
```

time: 161 us -> 139 us (0.86)
  starting transfers between devices: 60.1 us -> 28.3 us
  waiting for transfers between devices: 65.5 us -> 75.1 us
  local copies, waits for them, and re-layouts: 8.62 us -> 5.71 us
  Pallas kernels: 26 us -> 28.3 us
    all_to_all x0 -> x2, waiting for transfers between devices: none -> 48.6 us  [send_all(): lax.all_to_all(block, 'ep', 0, 0, axis_index_groups=groups, tiled=True)]
    ppermute x28 -> x7, starting transfers between devices: 58.9 us -> 15.7 us  [send(): lax.ppermute(blocks[step], 'ep', [(d, d ^ 2 * step) for d in range(device...]
    ppermute x28 -> x7, waiting for transfers between devices: 65.5 us -> 26 us  [send(): lax.ppermute(blocks[step], 'ep', [(d, d ^ 2 * step) for d in range(device...]
    all_to_all x0 -> x2, starting transfers between devices: none -> 11.3 us  [send_all(): lax.all_to_all(block, 'ep', 0, 0, axis_index_groups=groups, tiled=True)]
    pallas_call x5, Pallas kernels: 15.5 us -> 20.5 us  [call(): pl.pallas_call(kernel, out_shape=tuple(out_shape), in_specs=[pl.BlockSpec...]
    unnamed x22 -> x34, local copies, waits for them, and re-layouts: 8.62 us -> 5.71 us
    pallas_call x4 -> x2, Pallas kernels: 10.5 us -> 7.8 us  [weight_grad(): pl.pallas_call(functools.partial(weight_kernel, len(lefts), scale), grid=...]
  transfers between devices with their start and end apart: 32 -> 13, of which waited for: 12 -> 7; matrix products, arithmetic and copies ran while one was open for 0% -> 0% of each run, Pallas kernels for 9% -> 14%
where the time goes in v2:
time: 139 us; the launch traced here: 138 us
  waiting for transfers between devices  75.1 us (54%)
  starting transfers between devices  28.3 us (20%)
  Pallas kernels  28.3 us (20%)
  local copies, waits for them, and re-layouts  5.71 us (4%)
    all_to_all x2, waiting for transfers between devices, send_all(): lax.all_to_all(block, 'ep', 0, 0, axis_index_groups=groups, tiled=True)  48.6 us
    ppermute x7, waiting for transfers between devices, send(): lax.ppermute(blocks[step], 'ep', [(d, d ^ 2 * step) for d in range(device...  26 us
    pallas_call x5, Pallas kernels, call(): pl.pallas_call(kernel, out_shape=tuple(out_shape), in_specs=[pl.BlockSpec...  20.5 us
    ppermute x7, starting transfers between devices, send(): lax.ppermute(blocks[step], 'ep', [(d, d ^ 2 * step) for d in range(device...  15.7 us
    all_to_all x2, starting transfers between devices, send_all(): lax.all_to_all(block, 'ep', 0, 0, axis_index_groups=groups, tiled=True)  11.3 us
    pallas_call x2, Pallas kernels, weight_grad(): pl.pallas_call(functools.partial(weight_kernel, len(lefts), scale), grid=...  7.8 us
    unnamed x34, local copies, waits for them, and re-layouts  5.71 us
  transfers between devices with their start and end apart: 13, of which 7 were waited for; matrix products, arithmetic and copies ran while one was open for 0% of the time, Pallas kernels for 14%

profile of v2, /device:TPU:0, one launch (start us, length us, event | category | flops | bytes accessed | tf_op | source)
XLA Modules:
  0.0 138.3 jit_solution(2716522568583791208)
XLA Ops:
  1.1 3.2 %shard_map.93 = (bf16[48,2048]{1,0:T(8,128)(2,1)}, bf16[48,2048]{1,0:T(8,128)(2,1)}, bf16[48,2048]{1,0:T(8,128)(2,1)}, bf16[384,2048]{1,0:T(8,128)(2,1)}, bf16[3...) custom-call(s32[1]{0:T(128)} %bitcast.1.chip_ref, s32[2,128]{1,0:T(2,128)} %bitcast.24, bf16[2,128]{1,0:T(2,128)(2,1)} %bitcast.17, ...), custom_call_target="tpu_custom_call" | custom-call | flops 402653184 | bytes 3409408 | tf_op jit(solution)/shard_map/pallas_call | solution.py:187
  5.0 7.0 %all-to-all-start = ((bf16[8,48,2048]{2,1,0:T(8,128)(2,1)}), bf16[8,48,2048]{2,1,0:T(8,128)(2,1)}, u32[]{:S(2)}, u32[]{:S(2)}) async-start(bf16[8,48,2048]{2,1,0:T(8,128)(2,1)} %bitcast.23), calls=%async_computation | async-start | bytes 3145728 | tf_op jit(solution)/shard_map/all_to_all | solution.py:251
  12.2 1.8 %collective-permute-start = (bf16[48,2048]{1,0:T(8,128)(2,1)}, bf16[48,2048]{1,0:T(8,128)(2,1)S(1)}, u32[]{:S(2)}, u32[]{:S(2)}) collective-permute-start(bf16[48,2048]{1,0:T(8,128)(2,1)} %get-tuple-element.28), channel_id=1, source_target_pairs={{0,2},{1,3},{2,0},{3,1},{4,6},{5,7},{6,4},{7,5},{8,10},{9,11},{10,... | collective-permute-start | bytes 589832 | tf_op jit(solution)/shard_map/ppermute | solution.py:246
  14.0 1.5 %collective-permute-start.1 = (bf16[48,2048]{1,0:T(8,128)(2,1)S(1)}, bf16[48,2048]{1,0:T(8,128)(2,1)S(1)}, u32[]{:S(2)}, u32[]{:S(2)}) collective-permute-start(bf16[48,2048]{1,0:T(8,128)(2,1)S(1)} %copy-done.16), channel_id=1, source_target_pairs={{0,4},{1,5},{2,6},{3,7},{4,0},{5,1},{6,2},{7,3},{8,12},{9,13},{10,... | collective-permute-start | bytes 589832 | tf_op jit(solution)/shard_map/ppermute | solution.py:246
  15.5 2.4 %collective-permute-start.2 = (bf16[48,2048]{1,0:T(8,128)(2,1)}, bf16[48,2048]{1,0:T(8,128)(2,1)}, u32[]{:S(2)}, u32[]{:S(2)}) collective-permute-start(bf16[48,2048]{1,0:T(8,128)(2,1)} %get-tuple-element.30), channel_id=1, source_target_pairs={{0,12},{1,13},{2,14},{3,15},{4,8},{5,9},{6,10},{7,11},{8,4},{9,5},... | collective-permute-start | bytes 589832 | tf_op jit(solution)/shard_map/ppermute | solution.py:246
  17.8 3.0 %shard_map.94 = (bf16[48,2048]{1,0:T(8,128)(2,1)}, bf16[48,2048]{1,0:T(8,128)(2,1)}, bf16[48,2048]{1,0:T(8,128)(2,1)}, bf16[48,2048]{1,0:T(8,128)(2,1)}, bf16[48,2048]{1,0:T(8,128)(2,1)}) custom-call(s32[1]{0:T(128)} %bitcast.1.chip_ref, s32[2,128]{1,0:T(2,128)} %bitcast.25, bf16[2,128]{1,0:T(2,128)(2,1)} %bitcast.18, bf16[128,2048]{1,0:T(8,128)(2,1)} %refs_2_.3, ...), custom_call_target="tpu_custom_call" | custom-call | flops 402653184 | bytes 6227456 | tf_op jit(solution)/shard_map/pallas_call | solution.py:187
  20.8 0.7 collective-permute-start.5
  21.6 2.4 %collective-permute-start.6 = (bf16[48,2048]{1,0:T(8,128)(2,1)}, bf16[48,2048]{1,0:T(8,128)(2,1)}, u32[]{:S(2)}, u32[]{:S(2)}) collective-permute-start(bf16[48,2048]{1,0:T(8,128)(2,1)} %get-tuple-element.32), channel_id=1, source_target_pairs={{0,14},{1,15},{2,12},{3,13},{4,10},{5,11},{6,8},{7,9},{8,6},{9,7},... | collective-permute-start | bytes 589832 | tf_op jit(solution)/shard_map/ppermute | solution.py:246
  23.9 6.8 %collective-permute-done.refs_0_ = bf16[48,2048]{1,0:T(8,128)(2,1)S(1)} collective-permute-done((bf16[48,2048]{1,0:T(8,128)(2,1)}, bf16[48,2048]{1,0:T(8,128)(2,1)S(1)}, u32[]{:S(2)}, u32[]{:S(2)}) %collective-permute-start) | collective-permute-done | bytes 196640 | tf_op jit(solution)/shard_map/ppermute | solution.py:246
  31.5 3.4 %collective-permute-start.7 = (bf16[48,2048]{1,0:T(8,128)(2,1)}, bf16[48,2048]{1,0:T(8,128)(2,1)}, u32[]{:S(2)}, u32[]{:S(2)}) collective-permute-start(bf16[48,2048]{1,0:T(8,128)(2,1)} %get-tuple-element.33), channel_id=1, source_target_pairs={{0,10},{1,11},{2,8},{3,9},{4,14},{5,15},{6,12},{7,13},{8,2},{9,3},... | collective-permute-start | bytes 589832 | tf_op jit(solution)/shard_map/ppermute | solution.py:246
  34.9 9.1 %collective-permute-done.1.refs_1_ = bf16[48,2048]{1,0:T(8,128)(2,1)S(1)} collective-permute-done((bf16[48,2048]{1,0:T(8,128)(2,1)S(1)}, bf16[48,2048]{1,0:T(8,128)(2,1)S(1)}, u32[]{:S(2)}, u32[]{:S(2)}) %collective-permute-start.1) | collective-permute-done | bytes 196640 | tf_op jit(solution)/shard_map/ppermute | solution.py:246
  44.7 3.5 %collective-permute-start.8 = (bf16[48,2048]{1,0:T(8,128)(2,1)}, bf16[48,2048]{1,0:T(8,128)(2,1)}, u32[]{:S(2)}, u32[]{:S(2)}) collective-permute-start(bf16[48,2048]{1,0:T(8,128)(2,1)} %get-tuple-element.34), channel_id=1, source_target_pairs={{0,6},{1,7},{2,4},{3,5},{4,2},{5,3},{6,0},{7,1},{8,14},{9,15},{10,... | collective-permute-start | bytes 589832 | tf_op jit(solution)/shard_map/ppermute | solution.py:246
  48.2 19.2 %all-to-all-done = bf16[8,48,2048]{2,1,0:T(8,128)(2,1)} async-done(((bf16[8,48,2048]{2,1,0:T(8,128)(2,1)}), bf16[8,48,2048]{2,1,0:T(8,128)(2,1)}, u32[]{:S(2)}, u32[]{:S(2)}) %all-to-all-start) | async-done | bytes 1572896 | tf_op jit(solution)/shard_map/all_to_all | solution.py:251
  67.4 1.9 %copy-done.2 = bf16[1,2048,768]{2,1,0:T(8,128)(2,1)S(1)} copy-done((bf16[1,2048,768]{2,1,0:T(8,128)(2,1)S(1)}, bf16[1,2048,768]{2,1,0:T(8,128)(2,1)}, u32[]{:S(2)}) %copy-start.2) | copy-done | bytes 3145752
  69.3 5.0 %shard_map.95 = (bf16[384,2048]{1,0:T(8,128)(2,1)}, f32[384,384]{1,0:T(8,128)S(1)}, f32[384,384]{1,0:T(8,128)S(1)}, f32[384,384]{1,0:T(8,128)S(1)}, bf16[384,384...) custom-call(s32[1]{0:T(128)} %bitcast.1.chip_ref, ...), custom_call_target="tpu_custom_call" | custom-call | flops 2415919104 | bytes 13565952 | tf_op jit(solution)/shard_map/pallas_call | solution.py:187
  74.3 1.5 %collective-permute-done.5.refs_3_ = bf16[48,2048]{1,0:T(8,128)(2,1)} collective-permute-done((bf16[48,2048]{1,0:T(8,128)(2,1)}, bf16[48,2048]{1,0:T(8,128)(2,1)}, u32[]{:S(2)}, u32[]{:S(2)}) %collective-permute-start.5) | collective-permute-done | bytes 196640 | tf_op jit(solution)/shard_map/ppermute | solution.py:246
  75.8 8.6 %collective-permute-done.7.refs_5_ = bf16[48,2048]{1,0:T(8,128)(2,1)} collective-permute-done((bf16[48,2048]{1,0:T(8,128)(2,1)}, bf16[48,2048]{1,0:T(8,128)(2,1)}, u32[]{:S(2)}, u32[]{:S(2)}) %collective-permute-start.7) | collective-permute-done | bytes 196640 | tf_op jit(solution)/shard_map/ppermute | solution.py:246
  84.4 6.7 %shard_map.96 = (bf16[384,2176]{1,0:T(8,128)(2,1)}, bf16[384,3584]{1,0:T(8,128)(2,1)}, bf16[384,768]{1,0:T(8,128)(2,1)}) custom-call(s32[1]{0:T(128)} %bitcast.1.chip_ref, bf16[48,2048]{1,0:T(8,128)(2,1)S(1)} %copy-done.9, bf16[48,2048]{1,0:T(8,128)(2,1)S(1)} %copy-done.11, bf16[48,2048]{1,0:T(8,128)(2,1)} %collective-permute-done.2.refs_2_, ...), custom_call_target="tpu_custom_call" | custom-call | flops 3623878656 | bytes 19562496 | tf_op jit(solution)/shard_map/pallas_call | solution.py:187
  91.2 4.3 %all-to-all-start.1 = ((bf16[8,48,2176]{2,1,0:T(8,128)(2,1)}), bf16[8,48,2176]{2,1,0:T(8,128)(2,1)}, u32[]{:S(2)}, u32[]{:S(2)}) async-start(bf16[8,48,2176]{2,1,0:T(8,128)(2,1)} %bitcast.22), calls=%async_computation.1 | async-start | bytes 3342336 | tf_op jit(solution)/shard_map/all_to_all | solution.py:251
  96.5 1.8 %copy-done.4 = bf16[384,3584]{1,0:T(8,128)(2,1)S(1)} copy-done((bf16[384,3584]{1,0:T(8,128)(2,1)S(1)}, bf16[384,3584]{1,0:T(8,128)(2,1)}, u32[]{:S(2)}) %copy-start.4) | copy-done | bytes 2752536
  98.3 3.2 %shard_map.98.refs_3_ = bf16[384,2048]{1,0:T(8,128)(2,1)} custom-call(bf16[384,384]{1,0:T(8,128)(2,1)S(1)} %get-tuple-element.49.refs_0_, bf16[384,3584]{1,0:T(8,128)(2,1)S(1)} %collective-permute-done.10.refs_3_.refs_1_, bf16[384,3584]{1,0:T(8,128)(2,1)S(1)} %copy-done.4, bf16[384,3584]{1,0:T(8,128)(2,1)S(1)} %collective-permute-done.10.refs_3_.refs_1_), custom_call_target="tpu_custom_call" | custom-call | flops 1207959552 | bytes 5308416 | tf_op jit(solution)/shard_map/pallas_call | solution.py:210
  101.5 4.6 %shard_map.97.refs_2_ = bf16[2048,768]{1,0:T(8,128)(2,1)} custom-call(bf16[384,2048]{1,0:T(8,128)(2,1)S(1)} %copy-done.5, bf16[384,2048]{1,0:T(8,128)(2,1)S(1)} %collective-permute-done.9.refs_1_, bf16[384,768]{1,0:T(8,128)(2,1)S(1)} %copy-done.7, bf16[384,3584]{1,0:T(8,128)(2,1)S(1)} %collective-permute-done.10.refs_3_.refs_1_), custom_call_target="tpu_custom_call" | custom-call | flops 2415919104 | bytes 7471104 | tf_op jit(solution)/shard_map/pallas_call | solution.py:210
  106.1 29.4 %all-to-all-done.1 = bf16[8,48,2176]{2,1,0:T(8,128)(2,1)} async-done(((bf16[8,48,2176]{2,1,0:T(8,128)(2,1)}), bf16[8,48,2176]{2,1,0:T(8,128)(2,1)}, u32[]{:S(2)}, u32[]{:S(2)}) %all-to-all-start.1) | async-done | bytes 1671200 | tf_op jit(solution)/shard_map/all_to_all | solution.py:251
  135.6 2.7 %shard_map.99 = (bf16[128,2048]{1,0:T(8,128)(2,1)}, f32[2,128]{1,0:T(2,128)}) custom-call(bf16[2,128]{1,0:T(2,128)(2,1)S(1)} %bitcast.19, bf16[384,2176]{1,0:T(8,128)(2,1)} %bitcast.8.rows_ref, bf16[384,128]{1,0:T(8,128)(2,1)S(1)} %get-tuple-element.44.refs_0_, bf16[384,128]{1,0:T(8,128)(2,1)S(1)} %copy-done.14, bf16[2048,768]{1,0:T(8,128)(2,1)} %shard_map.97.refs_2_, ...), custom_call_target="tpu_custom_call" | custom-call | flops 201326592 | bytes 7112192 | tf_op jit(solution)/shard_map/pallas_call | solution.py:187
  (43 shorter events, 3.8 us)
Async XLA Ops:
  0.6 17.2 %collective-permute-start.3 = (bf16[2048,768]{1,0:T(8,128)(2,1)}, bf16[2048,768]{1,0:T(8,128)(2,1)S(1)}, u32[]{:S(2)}, u32[]{:S(2)}) collective-permute-start(bf16[2048,768]{1,0:T(8,128)(2,1)} %bitcast.12), channel_id=1, source_target_pairs={{0,1},{1,0},{2,3},{3,2},{4,5},{5,4},{6,7},{7,6},{8,9},{9,8},{10,11... | collective-permute-start | bytes 9437192 | tf_op jit(solution)/shard_map/ppermute | solution.py:242
  5.0 9.0 %copy-start.16 = (bf16[48,2048]{1,0:T(8,128)(2,1)S(1)}, bf16[48,2048]{1,0:T(8,128)(2,1)}, u32[]{:S(2)}) copy-start(bf16[48,2048]{1,0:T(8,128)(2,1)} %get-tuple-element.29) | copy-start | bytes 589828
  5.0 62.4 %all-to-all-start = ((bf16[8,48,2048]{2,1,0:T(8,128)(2,1)}), bf16[8,48,2048]{2,1,0:T(8,128)(2,1)}, u32[]{:S(2)}, u32[]{:S(2)}) async-start(bf16[8,48,2048]{2,1,0:T(8,128)(2,1)} %bitcast.23), calls=%async_computation | async-start | bytes 3145728 | tf_op jit(solution)/shard_map/all_to_all | solution.py:251
  12.0 5.9 %collective-permute-start.4 = (bf16[384,2048]{1,0:T(8,128)(2,1)}, bf16[384,2048]{1,0:T(8,128)(2,1)S(1)}, u32[]{:S(2)}, u32[]{:S(2)}) collective-permute-start(bf16[384,2048]{1,0:T(8,128)(2,1)} %bitcast.15), channel_id=1, source_target_pairs={{0,1},{1,0},{2,3},{3,2},{4,5},{5,4},{6,7},{7,6},{8,9},{9,8},{10,11... | collective-permute-start | bytes 4718600 | tf_op jit(solution)/shard_map/ppermute | solution.py:242
  12.2 18.6 %collective-permute-start = (bf16[48,2048]{1,0:T(8,128)(2,1)}, bf16[48,2048]{1,0:T(8,128)(2,1)S(1)}, u32[]{:S(2)}, u32[]{:S(2)}) collective-permute-start(bf16[48,2048]{1,0:T(8,128)(2,1)} %get-tuple-element.28), channel_id=1, source_target_pairs={{0,2},{1,3},{2,0},{3,1},{4,6},{5,7},{6,4},{7,5},{8,10},{9,11},{10,... | collective-permute-start | bytes 589832 | tf_op jit(solution)/shard_map/ppermute | solution.py:246
  14.0 30.0 %collective-permute-start.1 = (bf16[48,2048]{1,0:T(8,128)(2,1)S(1)}, bf16[48,2048]{1,0:T(8,128)(2,1)S(1)}, u32[]{:S(2)}, u32[]{:S(2)}) collective-permute-start(bf16[48,2048]{1,0:T(8,128)(2,1)S(1)} %copy-done.16), channel_id=1, source_target_pairs={{0,4},{1,5},{2,6},{3,7},{4,0},{5,1},{6,2},{7,3},{8,12},{9,13},{10,... | collective-permute-start | bytes 589832 | tf_op jit(solution)/shard_map/ppermute | solution.py:246
  15.5 58.8 %collective-permute-start.2 = (bf16[48,2048]{1,0:T(8,128)(2,1)}, bf16[48,2048]{1,0:T(8,128)(2,1)}, u32[]{:S(2)}, u32[]{:S(2)}) collective-permute-start(bf16[48,2048]{1,0:T(8,128)(2,1)} %get-tuple-element.30), channel_id=1, source_target_pairs={{0,12},{1,13},{2,14},{3,15},{4,8},{5,9},{6,10},{7,11},{8,4},{9,5},... | collective-permute-start | bytes 589832 | tf_op jit(solution)/shard_map/ppermute | solution.py:246
  20.8 54.9 %collective-permute-start.5 = (bf16[48,2048]{1,0:T(8,128)(2,1)}, bf16[48,2048]{1,0:T(8,128)(2,1)}, u32[]{:S(2)}, u32[]{:S(2)}) collective-permute-start(bf16[48,2048]{1,0:T(8,128)(2,1)} %get-tuple-element.31), channel_id=1, source_target_pairs={{0,8},{1,9},{2,10},{3,11},{4,12},{5,13},{6,14},{7,15},{8,0},{9,1},... | collective-permute-start | bytes 589832 | tf_op jit(solution)/shard_map/ppermute | solution.py:246
  21.6 54.2 %collective-permute-start.6 = (bf16[48,2048]{1,0:T(8,128)(2,1)}, bf16[48,2048]{1,0:T(8,128)(2,1)}, u32[]{:S(2)}, u32[]{:S(2)}) collective-permute-start(bf16[48,2048]{1,0:T(8,128)(2,1)} %get-tuple-element.32), channel_id=1, source_target_pairs={{0,14},{1,15},{2,12},{3,13},{4,10},{5,11},{6,8},{7,9},{8,6},{9,7},... | collective-permute-start | bytes 589832 | tf_op jit(solution)/shard_map/ppermute | solution.py:246
  31.5 52.9 %collective-permute-start.7 = (bf16[48,2048]{1,0:T(8,128)(2,1)}, bf16[48,2048]{1,0:T(8,128)(2,1)}, u32[]{:S(2)}, u32[]{:S(2)}) collective-permute-start(bf16[48,2048]{1,0:T(8,128)(2,1)} %get-tuple-element.33), channel_id=1, source_target_pairs={{0,10},{1,11},{2,8},{3,9},{4,14},{5,15},{6,12},{7,13},{8,2},{9,3},... | collective-permute-start | bytes 589832 | tf_op jit(solution)/shard_map/ppermute | solution.py:246
  44.7 39.7 %collective-permute-start.8 = (bf16[48,2048]{1,0:T(8,128)(2,1)}, bf16[48,2048]{1,0:T(8,128)(2,1)}, u32[]{:S(2)}, u32[]{:S(2)}) collective-permute-start(bf16[48,2048]{1,0:T(8,128)(2,1)} %get-tuple-element.34), channel_id=1, source_target_pairs={{0,6},{1,7},{2,4},{3,5},{4,2},{5,3},{6,0},{7,1},{8,14},{9,15},{10,... | collective-permute-start | bytes 589832 | tf_op jit(solution)/shard_map/ppermute | solution.py:246
  69.3 15.1 %copy-start.1 = (bf16[384,2048]{1,0:T(8,128)(2,1)S(1)}, bf16[384,2048]{1,0:T(8,128)(2,1)}, u32[]{:S(2)}) copy-start(bf16[384,2048]{1,0:T(8,128)(2,1)} %copy-done) | copy-start | bytes 4718596
  69.3 15.1 %copy-start.3 = (bf16[1,2048,768]{2,1,0:T(8,128)(2,1)S(1)}, bf16[1,2048,768]{2,1,0:T(8,128)(2,1)}, u32[]{:S(2)}) copy-start(bf16[1,2048,768]{2,1,0:T(8,128)(2,1)} %param.10) | copy-start | bytes 9437188
  69.3 15.1 %copy-start.6 = (bf16[1,384,2048]{2,1,0:T(8,128)(2,1)S(1)}, bf16[1,384,2048]{2,1,0:T(8,128)(2,1)}, u32[]{:S(2)}) copy-start(bf16[1,384,2048]{2,1,0:T(8,128)(2,1)} %param.11) | copy-start | bytes 4718596
  69.3 15.1 %copy-start.9 = (bf16[48,2048]{1,0:T(8,128)(2,1)S(1)}, bf16[48,2048]{1,0:T(8,128)(2,1)}, u32[]{:S(2)}) copy-start(bf16[48,2048]{1,0:T(8,128)(2,1)} %copy-done.8) | copy-start | bytes 589828
  69.3 15.1 %copy-start.11 = (bf16[48,2048]{1,0:T(8,128)(2,1)S(1)}, bf16[48,2048]{1,0:T(8,128)(2,1)}, u32[]{:S(2)}) copy-start(bf16[48,2048]{1,0:T(8,128)(2,1)} %copy-done.10) | copy-start | bytes 589828
  69.3 15.1 %copy-start.12 = (bf16[48,2048]{1,0:T(8,128)(2,1)S(1)}, bf16[48,2048]{1,0:T(8,128)(2,1)}, u32[]{:S(2)}) copy-start(bf16[48,2048]{1,0:T(8,128)(2,1)} %get-tuple-element.35.refs_7_) | copy-start | bytes 589828
  91.1 5.4 %collective-permute-start.10 = (bf16[384,3584]{1,0:T(8,128)(2,1)}, bf16[384,3584]{1,0:T(8,128)(2,1)S(1)}, u32[]{:S(2)}, u32[]{:S(2)}) collective-permute-start(bf16[384,3584]{1,0:T(8,128)(2,1)} %get-tuple-element.48.refs_2_), channel_id=1, source_target_pairs={{0,1},{1,0},{2,3},{3,2},{4,5},{5,4},{6,7},{7,6},{8,9},{9,8},{10,11... | collective-permute-start | bytes 8257544 | tf_op jit(solution)/shard_map/ppermute | solution.py:242
  91.2 44.4 %all-to-all-start.1 = ((bf16[8,48,2176]{2,1,0:T(8,128)(2,1)}), bf16[8,48,2176]{2,1,0:T(8,128)(2,1)}, u32[]{:S(2)}, u32[]{:S(2)}) async-start(bf16[8,48,2176]{2,1,0:T(8,128)(2,1)} %bitcast.22), calls=%async_computation.1 | async-start | bytes 3342336 | tf_op jit(solution)/shard_map/all_to_all | solution.py:251
  95.5 6.0 %collective-permute-start.9 = (bf16[384,2048]{1,0:T(8,128)(2,1)}, bf16[384,2048]{1,0:T(8,128)(2,1)S(1)}, u32[]{:S(2)}, u32[]{:S(2)}) collective-permute-start(bf16[384,2048]{1,0:T(8,128)(2,1)} %get-tuple-element.46.refs_0_), channel_id=1, source_target_pairs={{0,1},{1,0},{2,3},{3,2},{4,5},{5,4},{6,7},{7,6},{8,9},{9,8},{10,11... | collective-permute-start | bytes 4718600 | tf_op jit(solution)/shard_map/ppermute | solution.py:242
  98.3 3.2 %copy-start.5 = (bf16[384,2048]{1,0:T(8,128)(2,1)S(1)}, bf16[384,2048]{1,0:T(8,128)(2,1)}, u32[]{:S(2)}) copy-start(bf16[384,2048]{1,0:T(8,128)(2,1)} %get-tuple-element.46.refs_0_) | copy-start | bytes 4718596
  98.3 3.2 %copy-start.7 = (bf16[384,768]{1,0:T(8,128)(2,1)S(1)}, bf16[384,768]{1,0:T(8,128)(2,1)}, u32[]{:S(2)}) copy-start(bf16[384,768]{1,0:T(8,128)(2,1)} %get-tuple-element.47.refs_2_) | copy-start | bytes 1769476
  101.5 34.0 %copy-start.14 = (bf16[384,128]{1,0:T(8,128)(2,1)S(1)}, bf16[384,128]{1,0:T(8,128)(2,1)}, u32[]{:S(2)}) copy-start(bf16[384,128]{1,0:T(8,128)(2,1)} %copy-done.13) | copy-start | bytes 294916
  101.5 34.0 %copy-start.15 = (bf16[128,2]{0,1:T(2,128)(2,1)S(1)}, bf16[128,2]{0,1:T(2,128)(2,1)}, u32[]{:S(2)}) copy-start(bf16[128,2]{0,1:T(2,128)(2,1)} %param.9) | copy-start | bytes 1540
  (6 other events, 8.7 us)

commit v3 on v2

--- a/solution.py
+++ b/solution.py
@@ -12,7 +12,8 @@
 BF16 = jnp.bfloat16
 LANES = 128
 MIB = 1024 * 1024
-ORDER = (1, 2, 6, 4, 7, 5, 3)
+GROUPS = ((2, 1, 6, 4, 5, 7, 3, 0),)
+HELD = 0
 SLAB = 512
 EARLY = 3
 
@@ -55,7 +56,7 @@
     return pl.ds(pl.multiple_of((chip ^ step) * rows, 16), rows)
 
 
-def pack_kernel(experts, rows, steps, with_x, held, chip_ref, *refs):
+def pack_kernel(experts, rows, steps, with_x, held, order, chip_ref, *refs):
     hbm, refs = refs[: 3 + with_x], refs[3 + with_x + held :]
     sends, kept_ones = len(steps) + with_x, 2 * with_x
     ones_refs, refs = refs[sends : sends + kept_ones], refs[:sends] + refs[sends + kept_ones :]
@@ -74,10 +75,11 @@
     kept = []
     if with_x:
         plain = [picks(ids, place, e, 0, rows) for e in range(experts)]
+        ones = [picks(ids, place, chip ^ step, 0, rows) for step in order]
         for k, one_ref in enumerate(ones_refs):
-            one_ref[...] = jnp.concatenate([one[k] for one in plain], axis=0).astype(BF16)
+            one_ref[...] = jnp.concatenate([one[k] for one in ones], axis=0).astype(BF16)
         copies[3].wait()
-        x_rows = dot(sum(ref[...] for ref in ones_refs), local[3][...], (1, 0))
+        x_rows = dot(jnp.concatenate([sum(one) for one in plain], axis=0).astype(BF16), local[3][...], (1, 0))
         sends_local[-1][...] = x_rows.astype(BF16)
         kept += load([(sends_local[-1], outs[-1])], sems.at[4:])
     copies[2].wait()
@@ -111,10 +113,10 @@
     kept[0].wait()
 
 
-def backward_kernel(steps, slab, chip_ref, *refs):
-    count = len(steps)
+def backward_kernel(count, first, held, *refs):
     ins, terms, (w_down, other_down, w_in, other_in) = refs[:count], refs[count : count + 6], refs[count + 6 : count + 10]
-    back_out, share_out, grad_out, grad_ref, share_ref, back_ref, sems = refs[-7:]
+    outs, (grad_ref, share_ref, back_ref, sems) = refs[count + 10 + held : -4], refs[-4:]
+    back_outs, (share_out, grad_out) = outs[:count], outs[count:]
     total = grad_ref.shape[0]
     rows = total // count
     half, width = w_down.shape
@@ -124,47 +126,49 @@
     share_ref[:, 3 * half : at] = jnp.zeros((total, half), BF16)
     gate_parts = []
     for h, (weight, grad) in enumerate(((w_down, grad_ref), (other_down, share_ref))):
-        slope, active, hidden = [ref[...] for ref in terms[3 * h : 3 * h + 3]]
+        slope, active, hidden = [ref[first * rows : first * rows + total, :] for ref in terms[3 * h : 3 * h + 3]]
         pulled = dot(share_ref[:, at:], weight[...], (1, 1))
         gate_parts.append(jnp.sum(hidden * pulled, axis=1, keepdims=True))
         grad[:, :half] = (pulled * slope).astype(BF16)
         grad[:, half : 2 * half] = (pulled * active).astype(BF16)
     share_ref[:, 2 * half : 3 * half] = hidden.astype(BF16)
     kept = load([(share_ref, share_out), (grad_ref, grad_out)], sems)
+    back = dot(grad_ref[...], w_in[...], (1, 1)) + dot(share_ref[:, : 2 * half], other_in[...], (1, 1))
+    back_ref[:, :width] = back.astype(BF16)
     lane = lax.broadcasted_iota(jnp.int32, (total, LANES), 1)
     back_ref[:, width:] = jnp.where(
         lane == 0, gate_parts[0], jnp.where(lane == 1, gate_parts[1], 0.0)
     ).astype(BF16)
-    for n, first in enumerate(range(0, width, slab)):
-        cut = slice(first, first + slab)
-        back = dot(grad_ref[...], w_in[cut, :], (1, 1)) + dot(share_ref[:, : 2 * half], other_in[cut, :], (1, 1))
-        back_ref[:, cut] = back.astype(BF16)
-        if first + slab == width:
-            cut = slice(first, width + LANES)
-        kept += load(
-            [
-                (back_ref.at[b * rows : (b + 1) * rows, cut], back_out.at[rows_of(chip_ref[0], step, rows), cut])
-                for b, step in enumerate(steps)
-            ],
-            sems.at[2 + n * count :],
-        )
+    kept += load(
+        [(back_ref.at[b * rows : (b + 1) * rows, :], out) for b, out in enumerate(back_outs)], sems.at[2:]
+    )
     for copy in kept:
         copy.wait()
 
 
-def weight_kernel(count, scale, *refs):
-    out_ref, lefts, rights = refs[-1], refs[:count], refs[count:-1]
-    left = jnp.concatenate([ref[...] for ref in lefts], axis=0)
-    right = jnp.concatenate([ref[...] for ref in rights], axis=0)
-    out_ref[...] = (dot(left, right, (0, 0)) * scale).astype(BF16)
-
-
-def combine_kernel(gates_ref, rows_ref, *refs):
-    ones, (out_ref, gate_ref) = refs[:-4], refs[-2:]
+def weight_kernel(parts, scale, *refs):
+    (x_own, x_other, hidden_own), refs = refs[:3], refs[3:]
+    in_out, down_out = refs[-2:]
+    hidden_other, grad_own, grad_other, up_own, up_other = [refs[n * parts : (n + 1) * parts] for n in range(5)]
+    for lefts, rights, out in (
+        ((x_own, x_other), (*grad_own, *grad_other), in_out),
+        ((hidden_own, *hidden_other), (*up_own, *up_other), down_out),
+    ):
+        left = jnp.concatenate([ref[...] for ref in lefts], axis=0)
+        right = jnp.concatenate([ref[...] for ref in rights], axis=0)
+        out[...] = (dot(left, right, (0, 0)) * scale).astype(BF16)
+
+
+def combine_kernel(blocks, gates_ref, one_ref, two_ref, *refs):
+    ins, (out_ref, gate_ref, rows_ref) = refs[:blocks], refs[-3:]
     width = out_ref.shape[1]
-    out_ref[...] = dot(sum(one[...] for one in ones), rows_ref[:, :width], (0, 0)).astype(BF16)
+    rows = rows_ref.shape[0] // blocks
+    for b, ref in enumerate(ins):
+        rows_ref[b * rows : (b + 1) * rows, :] = ref[...]
+    ones = (one_ref[...], two_ref[...])
+    out_ref[...] = dot(sum(ones), rows_ref[:, :width], (0, 0)).astype(BF16)
     for k, one in enumerate(ones):
-        terms = dot(rows_ref[:, width:], one[...], (0, 0))
+        terms = dot(rows_ref[:, width:], one, (0, 0))
         gate_ref[k : k + 1, :] = (terms[0:1, :] + terms[1:2, :]) / gates_ref[k : k + 1, :].astype(F32)
 
 
@@ -196,30 +200,38 @@
     )(*chip, *args)
 
 
-def weight_grad(lefts, rights, scale, by_left):
-    depth, columns = lefts[0][2], rights[0][2]
-    grid = (depth if by_left else columns) // 512
-    rows = [array.shape[0] for array, _, _ in lefts]
-
-    def spec(operand, cut):
-        array, at, size = operand
-        if cut:
-            return pl.BlockSpec((array.shape[0], 512), lambda i: (0, at // 512 + i))
-        return pl.BlockSpec((array.shape[0], size), lambda i: (0, at // size))
+def weight_grads(x_own, x_other, hidden, grads, own_shares, other_shares, scale):
+    rows, features = x_own.shape
+    half = hidden.shape[1]
+    tile = 512
+    sizes = [grad.shape[0] for grad in grads]
+
+    def cut(at, sizes):
+        return [pl.BlockSpec((n, tile), lambda i: (0, at // tile + i)) for n in sizes]
+
+    def full(width, at, sizes):
+        return [pl.BlockSpec((n, width), lambda i: (0, at // width)) for n in sizes]
 
     return pl.pallas_call(
-        functools.partial(weight_kernel, len(lefts), scale),
-        grid=(grid,),
-        out_shape=pltpu.HBM((depth, columns), BF16),
-        in_specs=[spec(left, by_left) for left in lefts] + [spec(right, not by_left) for right in rights],
-        out_specs=pl.BlockSpec((512, columns), lambda i: (i, 0)) if by_left else pl.BlockSpec((depth, 512), lambda i: (0, i)),
-        compiler_params=pltpu.CompilerParams(vmem_limit_bytes=16 * MIB),
+        functools.partial(weight_kernel, len(sizes), scale),
+        grid=(features // tile,),
+        out_shape=(pltpu.HBM((features, 2 * half), BF16), pltpu.HBM((half, features), BF16)),
+        in_specs=cut(0, [rows, rows])
+        + full(half, 0, [rows])
+        + full(half, 2 * half, sizes)
+        + full(2 * half, 0, sizes + sizes)
+        + cut(4 * half, sizes + sizes),
+        out_specs=(
+            pl.BlockSpec((tile, 2 * half), lambda i: (i, 0)),
+            pl.BlockSpec((half, tile), lambda i: (0, i)),
+        ),
+        compiler_params=pltpu.CompilerParams(vmem_limit_bytes=24 * MIB),
         cost_estimate=pl.CostEstimate(
-            flops=2 * sum(rows) * depth * columns,
-            bytes_accessed=2 * (sum(rows) * (depth + columns) + depth * columns),
+            flops=12 * rows * features * half,
+            bytes_accessed=4 * rows * (2 * features + 3 * half) + 6 * features * half,
             transcendentals=0,
         ),
-    )(*[array for array, _, _ in lefts + rights])
+    )(x_own, x_other, hidden, *other_shares, *grads, *other_shares, *own_shares, *other_shares)
 
 
 def per_device(upstream, inputs, expert_ids, gate_weights, w_in, w_down):
@@ -235,7 +247,8 @@
     chip = [(lax.axis_index("ep") // 2).astype(jnp.int32).reshape(1)]
     ids, gates = expert_ids.T, gate_weights.T
     factor = 1.0 / math.sqrt(2 * routed)
-    steps = (*(ORDER if experts == 8 else range(1, experts)), 0)
+    parts = GROUPS if experts == 8 else ((*range(1, experts - 1), 0), (experts - 1,))
+    steps = sum(parts, ())
     groups = [[2 * e + c for e in range(experts)] for c in range(2)]
 
     def swap(value):
@@ -269,8 +282,8 @@
         tokens_in = [ids, gates, upstream, inputs][: 3 + with_x]
         sends = [(rows, features)] * len(these) + [(total, features)] * with_x
         return call(
-            functools.partial(pack_kernel, experts, rows, these, with_x, len(held)),
-            [far(*size) for size in sends] + [near(total, tokens)] * (choose * with_x),
+            functools.partial(pack_kernel, experts, rows, these, with_x, len(held), steps),
+            [far(*size) for size in sends] + [pltpu.HBM((total, tokens), BF16)] * (choose * with_x),
             chip,
             [*tokens_in, *held],
             like(*tokens_in) + [near(*size) for size in sends] + [dma(5 + len(these))],
@@ -301,37 +314,39 @@
     )
     operands = [*terms[:3], *terms[4:7], w_down, other_down, w_in, other_in]
     width, share_width = features + LANES, features + 4 * half
-    back, own_share, own_grad = call(
-        functools.partial(backward_kernel, steps, SLAB),
-        [far(total, width), far(total, share_width), far(total, 2 * half)],
-        chip,
-        [*[up_blocks[step] for step in steps], *operands],
-        [near(total, 2 * half), near(total, share_width), near(total, width), dma(2 + experts * features // SLAB)],
-        12 * total * half * features,
-        16,
-        tuple(range(experts + len(operands))),
-        (),
-        (0, 1, 2),
-    )
-    returned = send_all(back)
-
-    other_share = swap(own_share)
-    x_pairs = [(x_rows, 0, features), (swap(x_rows), 0, features)]
-    grad_pairs = [(own_grad, 0, 2 * half), (other_share, 0, 2 * half)]
-    grad_in = weight_grad(x_pairs, grad_pairs, factor, True)
-    hidden_pairs = [(terms[3], 0, half), (other_share, 2 * half, half)]
-    up_pairs = [(share, 4 * half, features) for share in (own_share, other_share)]
-    grad_down = weight_grad(hidden_pairs, up_pairs, factor, False)
+    returned, shares, grads, first, held = {}, [], [], 0, []
+    for part in parts:
+        count, size = len(part), len(part) * rows
+        *back, share, grad = call(
+            functools.partial(backward_kernel, count, first, len(held)),
+            [far(rows, width)] * count + [far(size, share_width), far(size, 2 * half)],
+            [],
+            [*[up_blocks[step] for step in part], *operands, *held],
+            [near(size, 2 * half), near(size, share_width), near(size, width), dma(2 + count)],
+            12 * size * half * features,
+            16,
+            tuple(range(count + len(operands))),
+            tuple(range(count + len(operands), count + len(operands) + len(held))),
+            tuple(range(count + 2)),
+        )
+        returned.update(send(dict(zip(part, back))))
+        shares.append(share)
+        grads.append(grad)
+        first += count
+        held = [returned[step] for step in part[:HELD]]
+
+    other_shares = [swap(share) for share in shares]
+    grad_in, grad_down = weight_grads(x_rows, swap(x_rows), terms[3], grads, shares, other_shares, factor)
 
     grad_inputs, grad_gates = call(
-        combine_kernel,
+        functools.partial(combine_kernel, experts),
         [jax.ShapeDtypeStruct((tokens, features), BF16), jax.ShapeDtypeStruct((choose, tokens), F32)],
         [],
-        [gates, returned, one, two, grad_in, grad_down],
-        [],
+        [gates, one, two, *[returned[step] for step in steps], grad_in, grad_down],
+        [near(total, width)],
         2 * total * tokens * features,
         12,
-        (0, 1, 2, 3),
+        tuple(range(3 + experts)),
     )
     return (grad_inputs, grad_gates.T, grad_in[None], grad_down[None])
 

time: 139 us -> 132 us (0.950); the launches traced: 138 us -> 130 us
  waiting for transfers between devices: 75.1 us -> 60.6 us
  starting transfers between devices: 28.3 us -> 36.3 us
    all_to_all x2 -> x1, waiting for transfers between devices: 48.6 us -> 18.1 us  [send_all(): lax.all_to_all(block, 'ep', 0, 0, axis_index_groups=groups, tiled=True)]
    ppermute x7 -> x14, waiting for transfers between devices: 26 us -> 42.5 us  [send(): lax.ppermute(blocks[step], 'ep', [(d, d ^ 2 * step) for d in range(device...]
    ppermute x7 -> x14, starting transfers between devices: 15.7 us -> 28.2 us  [send(): lax.ppermute(blocks[step], 'ep', [(d, d ^ 2 * step) for d in range(device...]
    all_to_all x2 -> x1, starting transfers between devices: 11.3 us -> 6.87 us  [send_all(): lax.all_to_all(block, 'ep', 0, 0, axis_index_groups=groups, tiled=True)]
    pallas_call x2 -> x1, Pallas kernels: 7.8 us -> 6.23 us  [weight_grads(): pl.pallas_call(functools.partial(weight_kernel, len(sizes), scale), grid=...]
    unnamed x34 -> x26, local copies, waits for them, and re-layouts: 5.71 us -> 4.77 us
  transfers between devices with their start and end apart: 13 -> 19, of which waited for: 7 -> 7; matrix products, arithmetic and copies ran while one was open for 0% -> 0% of each run, Pallas kernels for 14% -> 14%
where the time goes in v3:
time: 132 us; the launch traced here: 130 us
  waiting for transfers between devices  60.6 us (46%)
  starting transfers between devices  36.3 us (27%)
  Pallas kernels  27.3 us (21%)
  local copies, waits for them, and re-layouts  4.77 us (4%)
    ppermute x14, waiting for transfers between devices, send(): lax.ppermute(blocks[step], 'ep', [(d, d ^ 2 * step) for d in range(device...  42.5 us
    ppermute x14, starting transfers between devices, send(): lax.ppermute(blocks[step], 'ep', [(d, d ^ 2 * step) for d in range(device...  28.2 us
    pallas_call x5, Pallas kernels, call(): pl.pallas_call(kernel, out_shape=tuple(out_shape), in_specs=[pl.BlockSpec...  21 us
    all_to_all x1, waiting for transfers between devices, send_all(): lax.all_to_all(block, 'ep', 0, 0, axis_index_groups=groups, tiled=True)  18.1 us
    all_to_all x1, starting transfers between devices, send_all(): lax.all_to_all(block, 'ep', 0, 0, axis_index_groups=groups, tiled=True)  6.87 us
    pallas_call x1, Pallas kernels, weight_grads(): pl.pallas_call(functools.partial(weight_kernel, len(sizes), scale), grid=...  6.23 us
    unnamed x26, local copies, waits for them, and re-layouts  4.77 us
  transfers between devices with their start and end apart: 19, of which 7 were waited for; matrix products, arithmetic and copies ran while one was open for 0% of the time, Pallas kernels for 14%

profile of v3, /device:TPU:0, one launch (start us, length us, event | category | flops | bytes accessed | tf_op | source)
XLA Modules:
  0.0 129.8 jit_solution(5356724356405881113)
XLA Ops:
  1.1 3.8 %shard_map.93 = (bf16[48,2048]{1,0:T(8,128)(2,1)}, bf16[48,2048]{1,0:T(8,128)(2,1)}, bf16[48,2048]{1,0:T(8,128)(2,1)}, bf16[384,2048]{1,0:T(8,128)(2,1)}, bf16[3...) custom-call(s32[1]{0:T(128)} %bitcast.1.chip_ref, s32[2,128]{1,0:T(2,128)} %bitcast.21, bf16[2,128]{1,0:T(2,128)(2,1)} %bitcast.15, ...), custom_call_target="tpu_custom_call" | custom-call | flops 402653184 | bytes 3409408 | tf_op jit(solution)/shard_map/pallas_call | solution.py:191
  5.0 6.9 %all-to-all-start = ((bf16[8,48,2048]{2,1,0:T(8,128)(2,1)}), bf16[8,48,2048]{2,1,0:T(8,128)(2,1)}, u32[]{:S(2)}, u32[]{:S(2)}) async-start(bf16[8,48,2048]{2,1,0:T(8,128)(2,1)} %bitcast.19), calls=%async_computation | async-start | bytes 3145728 | tf_op jit(solution)/shard_map/all_to_all | solution.py:264
  12.1 1.8 %collective-permute-start = (bf16[48,2048]{1,0:T(8,128)(2,1)}, bf16[48,2048]{1,0:T(8,128)(2,1)S(1)}, u32[]{:S(2)}, u32[]{:S(2)}) collective-permute-start(bf16[48,2048]{1,0:T(8,128)(2,1)} %get-tuple-element.39), channel_id=1, source_target_pairs={{0,4},{1,5},{2,6},{3,7},{4,0},{5,1},{6,2},{7,3},{8,12},{9,13},{10,... | collective-permute-start | bytes 589832 | tf_op jit(solution)/shard_map/ppermute | solution.py:259
  15.4 2.4 %collective-permute-start.2 = (bf16[48,2048]{1,0:T(8,128)(2,1)}, bf16[48,2048]{1,0:T(8,128)(2,1)}, u32[]{:S(2)}, u32[]{:S(2)}) collective-permute-start(bf16[48,2048]{1,0:T(8,128)(2,1)} %get-tuple-element.41), channel_id=1, source_target_pairs={{0,12},{1,13},{2,14},{3,15},{4,8},{5,9},{6,10},{7,11},{8,4},{9,5},... | collective-permute-start | bytes 589832 | tf_op jit(solution)/shard_map/ppermute | solution.py:259
  17.7 2.9 %shard_map.94 = (bf16[48,2048]{1,0:T(8,128)(2,1)}, bf16[48,2048]{1,0:T(8,128)(2,1)}, bf16[48,2048]{1,0:T(8,128)(2,1)}, bf16[48,2048]{1,0:T(8,128)(2,1)}, bf16[48,2048]{1,0:T(8,128)(2,1)}) custom-call(s32[1]{0:T(128)} %bitcast.1.chip_ref, s32[2,128]{1,0:T(2,128)} %bitcast.22, bf16[2,128]{1,0:T(2,128)(2,1)} %bitcast.16, bf16[128,2048]{1,0:T(8,128)(2,1)} %refs_2_.3, ...), custom_call_target="tpu_custom_call" | custom-call | flops 402653184 | bytes 6227456 | tf_op jit(solution)/shard_map/pallas_call | solution.py:191
  21.4 2.2 %collective-permute-start.6 = (bf16[48,2048]{1,0:T(8,128)(2,1)}, bf16[48,2048]{1,0:T(8,128)(2,1)}, u32[]{:S(2)}, u32[]{:S(2)}) collective-permute-start(bf16[48,2048]{1,0:T(8,128)(2,1)} %get-tuple-element.43), channel_id=1, source_target_pairs={{0,10},{1,11},{2,8},{3,9},{4,14},{5,15},{6,12},{7,13},{8,2},{9,3},... | collective-permute-start | bytes 589832 | tf_op jit(solution)/shard_map/ppermute | solution.py:259
  23.7 20.3 %collective-permute-done.refs_0_ = bf16[48,2048]{1,0:T(8,128)(2,1)S(1)} collective-permute-done((bf16[48,2048]{1,0:T(8,128)(2,1)}, bf16[48,2048]{1,0:T(8,128)(2,1)S(1)}, u32[]{:S(2)}, u32[]{:S(2)}) %collective-permute-start) | collective-permute-done | bytes 196640 | tf_op jit(solution)/shard_map/ppermute | solution.py:259
  44.0 3.6 %collective-permute-start.7 = (bf16[48,2048]{1,0:T(8,128)(2,1)}, bf16[48,2048]{1,0:T(8,128)(2,1)}, u32[]{:S(2)}, u32[]{:S(2)}) collective-permute-start(bf16[48,2048]{1,0:T(8,128)(2,1)} %get-tuple-element.44), channel_id=1, source_target_pairs={{0,14},{1,15},{2,12},{3,13},{4,10},{5,11},{6,8},{7,9},{8,6},{9,7},... | collective-permute-start | bytes 589832 | tf_op jit(solution)/shard_map/ppermute | solution.py:259
  49.1 18.1 %all-to-all-done = bf16[8,48,2048]{2,1,0:T(8,128)(2,1)} async-done(((bf16[8,48,2048]{2,1,0:T(8,128)(2,1)}), bf16[8,48,2048]{2,1,0:T(8,128)(2,1)}, u32[]{:S(2)}, u32[]{:S(2)}) %all-to-all-start) | async-done | bytes 1572896 | tf_op jit(solution)/shard_map/all_to_all | solution.py:264
  67.2 1.9 %copy-done.2 = bf16[1,2048,768]{2,1,0:T(8,128)(2,1)S(1)} copy-done((bf16[1,2048,768]{2,1,0:T(8,128)(2,1)S(1)}, bf16[1,2048,768]{2,1,0:T(8,128)(2,1)}, u32[]{:S(2)}) %copy-start.2) | copy-done | bytes 3145752
  69.1 5.0 %shard_map.95 = (bf16[384,2048]{1,0:T(8,128)(2,1)}, f32[384,384]{1,0:T(8,128)S(1)}, f32[384,384]{1,0:T(8,128)S(1)}, f32[384,384]{1,0:T(8,128)S(1)}, bf16[384,384...) custom-call(s32[1]{0:T(128)} %bitcast.1.chip_ref, ...), custom_call_target="tpu_custom_call" | custom-call | flops 2415919104 | bytes 13565952 | tf_op jit(solution)/shard_map/pallas_call | solution.py:191
  74.1 1.5 %collective-permute-done.5.refs_3_ = bf16[48,2048]{1,0:T(8,128)(2,1)} collective-permute-done((bf16[48,2048]{1,0:T(8,128)(2,1)}, bf16[48,2048]{1,0:T(8,128)(2,1)}, u32[]{:S(2)}, u32[]{:S(2)}) %collective-permute-start.5) | collective-permute-done | bytes 196640 | tf_op jit(solution)/shard_map/ppermute | solution.py:259
  75.6 5.1 %collective-permute-done.6.refs_4_ = bf16[48,2048]{1,0:T(8,128)(2,1)} collective-permute-done((bf16[48,2048]{1,0:T(8,128)(2,1)}, bf16[48,2048]{1,0:T(8,128)(2,1)}, u32[]{:S(2)}, u32[]{:S(2)}) %collective-permute-start.6) | collective-permute-done | bytes 196640 | tf_op jit(solution)/shard_map/ppermute | solution.py:259
  80.8 8.0 %shard_map.96 = (bf16[48,2176]{1,0:T(8,128)(2,1)}, bf16[48,2176]{1,0:T(8,128)(2,1)}, bf16[48,2176]{1,0:T(8,128)(2,1)}, bf16[48,2176]{1,0:T(8,128)(2,1)}, bf16[48...) custom-call(bf16[48,2048]{1,0:T(8,128)(2,1)S(1)} %collective-permute, ...), custom_call_target="tpu_custom_call" | custom-call | flops 3623878656 | bytes 19562496 | tf_op jit(solution)/shard_map/pallas_call | solution.py:191
  89.4 4.0 %collective-permute-start.9 = (bf16[48,2176]{1,0:T(8,128)(2,1)}, bf16[48,2176]{1,0:T(8,128)(2,1)S(1)}, u32[]{:S(2)}, u32[]{:S(2)}) collective-permute-start(bf16[48,2176]{1,0:T(8,128)(2,1)} %get-tuple-element.54), channel_id=1, source_target_pairs={{0,4},{1,5},{2,6},{3,7},{4,0},{5,1},{6,2},{7,3},{8,12},{9,13},{10,... | collective-permute-start | bytes 626696 | tf_op jit(solution)/shard_map/ppermute | solution.py:259
  94.0 2.3 %collective-permute-start.11 = (bf16[48,2176]{1,0:T(8,128)(2,1)}, bf16[48,2176]{1,0:T(8,128)(2,1)S(1)}, u32[]{:S(2)}, u32[]{:S(2)}) collective-permute-start(bf16[48,2176]{1,0:T(8,128)(2,1)} %get-tuple-element.56), channel_id=1, source_target_pairs={{0,12},{1,13},{2,14},{3,15},{4,8},{5,9},{6,10},{7,11},{8,4},{9,5},... | collective-permute-start | bytes 626696 | tf_op jit(solution)/shard_map/ppermute | solution.py:259
  96.2 3.0 %collective-permute-done.9.refs_0_ = bf16[48,2176]{1,0:T(8,128)(2,1)S(1)} collective-permute-done((bf16[48,2176]{1,0:T(8,128)(2,1)}, bf16[48,2176]{1,0:T(8,128)(2,1)S(1)}, u32[]{:S(2)}, u32[]{:S(2)}) %collective-permute-start.9) | collective-permute-done | bytes 208928 | tf_op jit(solution)/shard_map/ppermute | solution.py:259
  99.3 2.4 %collective-permute-start.12 = (bf16[48,2176]{1,0:T(8,128)(2,1)}, bf16[48,2176]{1,0:T(8,128)(2,1)S(1)}, u32[]{:S(2)}, u32[]{:S(2)}) collective-permute-start(bf16[48,2176]{1,0:T(8,128)(2,1)} %get-tuple-element.57), channel_id=1, source_target_pairs={{0,8},{1,9},{2,10},{3,11},{4,12},{5,13},{6,14},{7,15},{8,0},{9,1},... | collective-permute-start | bytes 626696 | tf_op jit(solution)/shard_map/ppermute | solution.py:259
  102.5 2.4 %collective-permute-start.14 = (bf16[48,2176]{1,0:T(8,128)(2,1)}, bf16[48,2176]{1,0:T(8,128)(2,1)S(1)}, u32[]{:S(2)}, u32[]{:S(2)}) collective-permute-start(bf16[48,2176]{1,0:T(8,128)(2,1)} %get-tuple-element.59), channel_id=1, source_target_pairs={{0,14},{1,15},{2,12},{3,13},{4,10},{5,11},{6,8},{7,9},{8,6},{9,7},... | collective-permute-start | bytes 626696 | tf_op jit(solution)/shard_map/ppermute | solution.py:259
  104.9 1.9 %collective-permute-start.15 = (bf16[48,2176]{1,0:T(8,128)(2,1)}, bf16[48,2176]{1,0:T(8,128)(2,1)S(1)}, u32[]{:S(2)}, u32[]{:S(2)}) collective-permute-start(bf16[48,2176]{1,0:T(8,128)(2,1)} %get-tuple-element.60), channel_id=1, source_target_pairs={{0,6},{1,7},{2,4},{3,5},{4,2},{5,3},{6,0},{7,1},{8,14},{9,15},{10,... | collective-permute-start | bytes 626696 | tf_op jit(solution)/shard_map/ppermute | solution.py:259
  106.8 1.8 %copy-done.4 = bf16[384,3584]{1,0:T(8,128)(2,1)S(1)} copy-done((bf16[384,3584]{1,0:T(8,128)(2,1)S(1)}, bf16[384,3584]{1,0:T(8,128)(2,1)}, u32[]{:S(2)}) %copy-start.4) | copy-done | bytes 2752536
  109.7 6.2 %shard_map.97 = (bf16[2048,768]{1,0:T(8,128)(2,1)}, bf16[384,2048]{1,0:T(8,128)(2,1)}) custom-call(bf16[384,2048]{1,0:T(8,128)(2,1)S(1)} %copy-done.6, bf16[384,2048]{1,0:T(8,128)(2,1)S(1)} %collective-permute-done.16.refs_1_, bf16[384,384]{1,0:T(8,128)(2,1)S(1)} %get-tuple-element.63.refs_2_, ...), custom_call_target="tpu_custom_call" | custom-call | flops 3623878656 | bytes 12779520 | tf_op jit(solution)/shard_map/pallas_call | solution.py:215
  115.9 7.0 %collective-permute-done.12.refs_3_ = bf16[48,2176]{1,0:T(8,128)(2,1)S(1)} collective-permute-done((bf16[48,2176]{1,0:T(8,128)(2,1)}, bf16[48,2176]{1,0:T(8,128)(2,1)S(1)}, u32[]{:S(2)}, u32[]{:S(2)}) %collective-permute-start.12) | collective-permute-done | bytes 208928 | tf_op jit(solution)/shard_map/ppermute | solution.py:259
  122.9 5.5 %collective-permute-done.13.refs_4_ = bf16[48,2176]{1,0:T(8,128)(2,1)S(1)} collective-permute-done((bf16[48,2176]{1,0:T(8,128)(2,1)}, bf16[48,2176]{1,0:T(8,128)(2,1)S(1)}, u32[]{:S(2)}, u32[]{:S(2)}) %collective-permute-start.13) | collective-permute-done | bytes 208928 | tf_op jit(solution)/shard_map/ppermute | solution.py:259
  (46 shorter events, 8.8 us)
Async XLA Ops:
  0.6 17.1 %collective-permute-start.3 = (bf16[2048,768]{1,0:T(8,128)(2,1)}, bf16[2048,768]{1,0:T(8,128)(2,1)S(1)}, u32[]{:S(2)}, u32[]{:S(2)}) collective-permute-start(bf16[2048,768]{1,0:T(8,128)(2,1)} %bitcast.10), channel_id=1, source_target_pairs={{0,1},{1,0},{2,3},{3,2},{4,5},{5,4},{6,7},{7,6},{8,9},{9,8},{10,11... | collective-permute-start | bytes 9437192 | tf_op jit(solution)/shard_map/ppermute | solution.py:255
  5.0 62.2 %all-to-all-start = ((bf16[8,48,2048]{2,1,0:T(8,128)(2,1)}), bf16[8,48,2048]{2,1,0:T(8,128)(2,1)}, u32[]{:S(2)}, u32[]{:S(2)}) async-start(bf16[8,48,2048]{2,1,0:T(8,128)(2,1)} %bitcast.19), calls=%async_computation | async-start | bytes 3145728 | tf_op jit(solution)/shard_map/all_to_all | solution.py:264
  11.9 5.9 %collective-permute-start.4 = (bf16[384,2048]{1,0:T(8,128)(2,1)}, bf16[384,2048]{1,0:T(8,128)(2,1)S(1)}, u32[]{:S(2)}, u32[]{:S(2)}) collective-permute-start(bf16[384,2048]{1,0:T(8,128)(2,1)} %bitcast.13), channel_id=1, source_target_pairs={{0,1},{1,0},{2,3},{3,2},{4,5},{5,4},{6,7},{7,6},{8,9},{9,8},{10,11... | collective-permute-start | bytes 4718600 | tf_op jit(solution)/shard_map/ppermute | solution.py:255
  12.1 31.9 %collective-permute-start = (bf16[48,2048]{1,0:T(8,128)(2,1)}, bf16[48,2048]{1,0:T(8,128)(2,1)S(1)}, u32[]{:S(2)}, u32[]{:S(2)}) collective-permute-start(bf16[48,2048]{1,0:T(8,128)(2,1)} %get-tuple-element.39), channel_id=1, source_target_pairs={{0,4},{1,5},{2,6},{3,7},{4,0},{5,1},{6,2},{7,3},{8,12},{9,13},{10,... | collective-permute-start | bytes 589832 | tf_op jit(solution)/shard_map/ppermute | solution.py:259
  13.9 33.7 %collective-permute-start.1 = (bf16[48,2048]{1,0:T(8,128)(2,1)}, bf16[48,2048]{1,0:T(8,128)(2,1)S(1)}, u32[]{:S(2)}, u32[]{:S(2)}) collective-permute-start(bf16[48,2048]{1,0:T(8,128)(2,1)} %get-tuple-element.40), channel_id=1, source_target_pairs={{0,2},{1,3},{2,0},{3,1},{4,6},{5,7},{6,4},{7,5},{8,10},{9,11},{10,... | collective-permute-start | bytes 589832 | tf_op jit(solution)/shard_map/ppermute | solution.py:259
  15.4 58.8 %collective-permute-start.2 = (bf16[48,2048]{1,0:T(8,128)(2,1)}, bf16[48,2048]{1,0:T(8,128)(2,1)}, u32[]{:S(2)}, u32[]{:S(2)}) collective-permute-start(bf16[48,2048]{1,0:T(8,128)(2,1)} %get-tuple-element.41), channel_id=1, source_target_pairs={{0,12},{1,13},{2,14},{3,15},{4,8},{5,9},{6,10},{7,11},{8,4},{9,5},... | collective-permute-start | bytes 589832 | tf_op jit(solution)/shard_map/ppermute | solution.py:259
  20.7 55.0 %collective-permute-start.5 = (bf16[48,2048]{1,0:T(8,128)(2,1)}, bf16[48,2048]{1,0:T(8,128)(2,1)}, u32[]{:S(2)}, u32[]{:S(2)}) collective-permute-start(bf16[48,2048]{1,0:T(8,128)(2,1)} %get-tuple-element.42), channel_id=1, source_target_pairs={{0,8},{1,9},{2,10},{3,11},{4,12},{5,13},{6,14},{7,15},{8,0},{9,1},... | collective-permute-start | bytes 589832 | tf_op jit(solution)/shard_map/ppermute | solution.py:259
  21.4 59.3 %collective-permute-start.6 = (bf16[48,2048]{1,0:T(8,128)(2,1)}, bf16[48,2048]{1,0:T(8,128)(2,1)}, u32[]{:S(2)}, u32[]{:S(2)}) collective-permute-start(bf16[48,2048]{1,0:T(8,128)(2,1)} %get-tuple-element.43), channel_id=1, source_target_pairs={{0,10},{1,11},{2,8},{3,9},{4,14},{5,15},{6,12},{7,13},{8,2},{9,3},... | collective-permute-start | bytes 589832 | tf_op jit(solution)/shard_map/ppermute | solution.py:259
  44.0 36.8 %collective-permute-start.7 = (bf16[48,2048]{1,0:T(8,128)(2,1)}, bf16[48,2048]{1,0:T(8,128)(2,1)}, u32[]{:S(2)}, u32[]{:S(2)}) collective-permute-start(bf16[48,2048]{1,0:T(8,128)(2,1)} %get-tuple-element.44), channel_id=1, source_target_pairs={{0,14},{1,15},{2,12},{3,13},{4,10},{5,11},{6,8},{7,9},{8,6},{9,7},... | collective-permute-start | bytes 589832 | tf_op jit(solution)/shard_map/ppermute | solution.py:259
  47.6 33.2 %collective-permute-start.8 = (bf16[48,2048]{1,0:T(8,128)(2,1)}, bf16[48,2048]{1,0:T(8,128)(2,1)}, u32[]{:S(2)}, u32[]{:S(2)}) collective-permute-start(bf16[48,2048]{1,0:T(8,128)(2,1)} %get-tuple-element.45), channel_id=1, source_target_pairs={{0,6},{1,7},{2,4},{3,5},{4,2},{5,3},{6,0},{7,1},{8,14},{9,15},{10,... | collective-permute-start | bytes 589832 | tf_op jit(solution)/shard_map/ppermute | solution.py:259
  69.1 11.7 %copy-start.9 = (bf16[48,2048]{1,0:T(8,128)(2,1)S(1)}, bf16[48,2048]{1,0:T(8,128)(2,1)}, u32[]{:S(2)}) copy-start(bf16[48,2048]{1,0:T(8,128)(2,1)} %get-tuple-element.46.refs_7_) | copy-start | bytes 589828
  88.8 16.1 %collective-permute-start.17 = (bf16[384,3584]{1,0:T(8,128)(2,1)}, bf16[384,3584]{1,0:T(8,128)(2,1)S(1)}, u32[]{:S(2)}, u32[]{:S(2)}) collective-permute-start(bf16[384,3584]{1,0:T(8,128)(2,1)} %get-tuple-element.64.refs_6_), channel_id=1, source_target_pairs={{0,1},{1,0},{2,3},{3,2},{4,5},{5,4},{6,7},{7,6},{8,9},{9,8},{10,11... | collective-permute-start | bytes 8257544 | tf_op jit(solution)/shard_map/ppermute | solution.py:255
  88.9 13.6 %collective-permute-start.16 = (bf16[384,2048]{1,0:T(8,128)(2,1)S(1)}, bf16[384,2048]{1,0:T(8,128)(2,1)S(1)}, u32[]{:S(2)}, u32[]{:S(2)}) collective-permute-start(bf16[384,2048]{1,0:T(8,128)(2,1)S(1)} %copy-done.6), channel_id=1, source_target_pairs={{0,1},{1,0},{2,3},{3,2},{4,5},{5,4},{6,7},{7,6},{8,9},{9,8},{10,11... | collective-permute-start | bytes 4718600 | tf_op jit(solution)/shard_map/ppermute | solution.py:255
  89.4 9.9 %collective-permute-start.9 = (bf16[48,2176]{1,0:T(8,128)(2,1)}, bf16[48,2176]{1,0:T(8,128)(2,1)S(1)}, u32[]{:S(2)}, u32[]{:S(2)}) collective-permute-start(bf16[48,2176]{1,0:T(8,128)(2,1)} %get-tuple-element.54), channel_id=1, source_target_pairs={{0,4},{1,5},{2,6},{3,7},{4,0},{5,1},{6,2},{7,3},{8,12},{9,13},{10,... | collective-permute-start | bytes 626696 | tf_op jit(solution)/shard_map/ppermute | solution.py:259
  93.4 8.3 %collective-permute-start.10 = (bf16[48,2176]{1,0:T(8,128)(2,1)}, bf16[48,2176]{1,0:T(8,128)(2,1)S(1)}, u32[]{:S(2)}, u32[]{:S(2)}) collective-permute-start(bf16[48,2176]{1,0:T(8,128)(2,1)} %get-tuple-element.55), channel_id=1, source_target_pairs={{0,2},{1,3},{2,0},{3,1},{4,6},{5,7},{6,4},{7,5},{8,10},{9,11},{10,... | collective-permute-start | bytes 626696 | tf_op jit(solution)/shard_map/ppermute | solution.py:259
  94.0 22.0 %collective-permute-start.11 = (bf16[48,2176]{1,0:T(8,128)(2,1)}, bf16[48,2176]{1,0:T(8,128)(2,1)S(1)}, u32[]{:S(2)}, u32[]{:S(2)}) collective-permute-start(bf16[48,2176]{1,0:T(8,128)(2,1)} %get-tuple-element.56), channel_id=1, source_target_pairs={{0,12},{1,13},{2,14},{3,15},{4,8},{5,9},{6,10},{7,11},{8,4},{9,5},... | collective-permute-start | bytes 626696 | tf_op jit(solution)/shard_map/ppermute | solution.py:259
  99.3 23.7 %collective-permute-start.12 = (bf16[48,2176]{1,0:T(8,128)(2,1)}, bf16[48,2176]{1,0:T(8,128)(2,1)S(1)}, u32[]{:S(2)}, u32[]{:S(2)}) collective-permute-start(bf16[48,2176]{1,0:T(8,128)(2,1)} %get-tuple-element.57), channel_id=1, source_target_pairs={{0,8},{1,9},{2,10},{3,11},{4,12},{5,13},{6,14},{7,15},{8,0},{9,1},... | collective-permute-start | bytes 626696 | tf_op jit(solution)/shard_map/ppermute | solution.py:259
  101.7 26.8 %collective-permute-start.13 = (bf16[48,2176]{1,0:T(8,128)(2,1)}, bf16[48,2176]{1,0:T(8,128)(2,1)S(1)}, u32[]{:S(2)}, u32[]{:S(2)}) collective-permute-start(bf16[48,2176]{1,0:T(8,128)(2,1)} %get-tuple-element.58), channel_id=1, source_target_pairs={{0,10},{1,11},{2,8},{3,9},{4,14},{5,15},{6,12},{7,13},{8,2},{9,3},... | collective-permute-start | bytes 626696 | tf_op jit(solution)/shard_map/ppermute | solution.py:259
  102.5 26.0 %collective-permute-start.14 = (bf16[48,2176]{1,0:T(8,128)(2,1)}, bf16[48,2176]{1,0:T(8,128)(2,1)S(1)}, u32[]{:S(2)}, u32[]{:S(2)}) collective-permute-start(bf16[48,2176]{1,0:T(8,128)(2,1)} %get-tuple-element.59), channel_id=1, source_target_pairs={{0,14},{1,15},{2,12},{3,13},{4,10},{5,11},{6,8},{7,9},{8,6},{9,7},... | collective-permute-start | bytes 626696 | tf_op jit(solution)/shard_map/ppermute | solution.py:259
  104.9 23.5 %collective-permute-start.15 = (bf16[48,2176]{1,0:T(8,128)(2,1)}, bf16[48,2176]{1,0:T(8,128)(2,1)S(1)}, u32[]{:S(2)}, u32[]{:S(2)}) collective-permute-start(bf16[48,2176]{1,0:T(8,128)(2,1)} %get-tuple-element.60), channel_id=1, source_target_pairs={{0,6},{1,7},{2,4},{3,5},{4,2},{5,3},{6,0},{7,1},{8,14},{9,15},{10,... | collective-permute-start | bytes 626696 | tf_op jit(solution)/shard_map/ppermute | solution.py:259
  109.7 18.8 %copy-start.8 = (bf16[48,2176]{1,0:T(8,128)(2,1)S(1)}, bf16[48,2176]{1,0:T(8,128)(2,1)}, u32[]{:S(2)}) copy-start(bf16[48,2176]{1,0:T(8,128)(2,1)} %get-tuple-element.61.refs_7_) | copy-start | bytes 626692
  109.7 18.8 %copy-start.10 = (bf16[384,128]{1,0:T(8,128)(2,1)S(1)}, bf16[384,128]{1,0:T(8,128)(2,1)}, u32[]{:S(2)}) copy-start(bf16[384,128]{1,0:T(8,128)(2,1)} %get-tuple-element.37.one_ref) | copy-start | bytes 294916
  109.7 18.8 %copy-start.11 = (bf16[384,128]{1,0:T(8,128)(2,1)S(1)}, bf16[384,128]{1,0:T(8,128)(2,1)}, u32[]{:S(2)}) copy-start(bf16[384,128]{1,0:T(8,128)(2,1)} %get-tuple-element.38.two_ref) | copy-start | bytes 294916
  109.7 18.8 %copy-start.12 = (bf16[128,2]{0,1:T(2,128)(2,1)S(1)}, bf16[128,2]{0,1:T(2,128)(2,1)}, u32[]{:S(2)}) copy-start(bf16[128,2]{0,1:T(2,128)(2,1)} %param.9) | copy-start | bytes 1540
  (8 other events, 50.7 us)

commit v4 on v3

--- a/solution.py
+++ b/solution.py
@@ -12,8 +12,8 @@
 BF16 = jnp.bfloat16
 LANES = 128
 MIB = 1024 * 1024
-GROUPS = ((2, 1, 6, 4, 5, 7, 3, 0),)
-HELD = 0
+ORDER = (1, 2, 5, 7, 4, 6, 3)
+BACK = (1, 2, 6, 4, 5, 7, 3)
 SLAB = 512
 EARLY = 3
 
@@ -58,7 +58,7 @@
 
 def pack_kernel(experts, rows, steps, with_x, held, order, chip_ref, *refs):
     hbm, refs = refs[: 3 + with_x], refs[3 + with_x + held :]
-    sends, kept_ones = len(steps) + with_x, 2 * with_x
+    sends, kept_ones = len(steps) + with_x, 2 * (1 - with_x)
     ones_refs, refs = refs[sends : sends + kept_ones], refs[:sends] + refs[sends + kept_ones :]
     outs, local, sends_local, sems = refs[:sends], refs[sends : 2 * sends + 3 + with_x][: 3 + with_x], refs[-1 - sends : -1], refs[-1]
     copies = load(zip(hbm, local), sems)
@@ -73,11 +73,12 @@
         for step in steps
     ]
     kept = []
-    if with_x:
-        plain = [picks(ids, place, e, 0, rows) for e in range(experts)]
+    if not with_x:
         ones = [picks(ids, place, chip ^ step, 0, rows) for step in order]
         for k, one_ref in enumerate(ones_refs):
             one_ref[...] = jnp.concatenate([one[k] for one in ones], axis=0).astype(BF16)
+    else:
+        plain = [picks(ids, place, e, 0, rows) for e in range(experts)]
         copies[3].wait()
         x_rows = dot(jnp.concatenate([sum(one) for one in plain], axis=0).astype(BF16), local[3][...], (1, 0))
         sends_local[-1][...] = x_rows.astype(BF16)
@@ -113,9 +114,9 @@
     kept[0].wait()
 
 
-def backward_kernel(count, first, held, *refs):
+def backward_kernel(count, *refs):
     ins, terms, (w_down, other_down, w_in, other_in) = refs[:count], refs[count : count + 6], refs[count + 6 : count + 10]
-    outs, (grad_ref, share_ref, back_ref, sems) = refs[count + 10 + held : -4], refs[-4:]
+    outs, (grad_ref, share_ref, back_ref, sems) = refs[count + 10 : -4], refs[-4:]
     back_outs, (share_out, grad_out) = outs[:count], outs[count:]
     total = grad_ref.shape[0]
     rows = total // count
@@ -126,36 +127,38 @@
     share_ref[:, 3 * half : at] = jnp.zeros((total, half), BF16)
     gate_parts = []
     for h, (weight, grad) in enumerate(((w_down, grad_ref), (other_down, share_ref))):
-        slope, active, hidden = [ref[first * rows : first * rows + total, :] for ref in terms[3 * h : 3 * h + 3]]
+        slope, active, hidden = [ref[...] for ref in terms[3 * h : 3 * h + 3]]
         pulled = dot(share_ref[:, at:], weight[...], (1, 1))
         gate_parts.append(jnp.sum(hidden * pulled, axis=1, keepdims=True))
         grad[:, :half] = (pulled * slope).astype(BF16)
         grad[:, half : 2 * half] = (pulled * active).astype(BF16)
     share_ref[:, 2 * half : 3 * half] = hidden.astype(BF16)
     kept = load([(share_ref, share_out), (grad_ref, grad_out)], sems)
-    back = dot(grad_ref[...], w_in[...], (1, 1)) + dot(share_ref[:, : 2 * half], other_in[...], (1, 1))
-    back_ref[:, :width] = back.astype(BF16)
     lane = lax.broadcasted_iota(jnp.int32, (total, LANES), 1)
     back_ref[:, width:] = jnp.where(
         lane == 0, gate_parts[0], jnp.where(lane == 1, gate_parts[1], 0.0)
     ).astype(BF16)
-    kept += load(
-        [(back_ref.at[b * rows : (b + 1) * rows, :], out) for b, out in enumerate(back_outs)], sems.at[2:]
-    )
+    for n, at in enumerate(range(0, width, SLAB)):
+        cut = slice(at, at + SLAB)
+        back = dot(grad_ref[...], w_in[cut, :], (1, 1)) + dot(share_ref[:, : 2 * half], other_in[cut, :], (1, 1))
+        back_ref[:, cut] = back.astype(BF16)
+        if at + SLAB == width:
+            cut = slice(at, width + LANES)
+        kept += load(
+            [(back_ref.at[b * rows : (b + 1) * rows, cut], out.at[:, cut]) for b, out in enumerate(back_outs)],
+            sems.at[2 + n * count :],
+        )
     for copy in kept:
         copy.wait()
 
 
-def weight_kernel(parts, scale, *refs):
-    (x_own, x_other, hidden_own), refs = refs[:3], refs[3:]
-    in_out, down_out = refs[-2:]
-    hidden_other, grad_own, grad_other, up_own, up_other = [refs[n * parts : (n + 1) * parts] for n in range(5)]
-    for lefts, rights, out in (
-        ((x_own, x_other), (*grad_own, *grad_other), in_out),
-        ((hidden_own, *hidden_other), (*up_own, *up_other), down_out),
+def weight_kernel(scale, x_own, x_other, hidden_own, hidden_other, grad_own, grad_other, up_own, up_other, in_out, down_out):
+    for own_left, other_left, own_right, other_right, out in (
+        (x_own, x_other, grad_own, grad_other, in_out),
+        (hidden_own, hidden_other, up_own, up_other, down_out),
     ):
-        left = jnp.concatenate([ref[...] for ref in lefts], axis=0)
-        right = jnp.concatenate([ref[...] for ref in rights], axis=0)
+        left = jnp.concatenate([own_left[...], other_left[...]], axis=0)
+        right = jnp.concatenate([own_right[...], other_right[...]], axis=0)
         out[...] = (dot(left, right, (0, 0)) * scale).astype(BF16)
 
 
@@ -200,27 +203,23 @@
     )(*chip, *args)
 
 
-def weight_grads(x_own, x_other, hidden, grads, own_shares, other_shares, scale):
+def weight_grads(x_own, x_other, hidden, grad, own_share, other_share, scale):
     rows, features = x_own.shape
     half = hidden.shape[1]
     tile = 512
-    sizes = [grad.shape[0] for grad in grads]
-
-    def cut(at, sizes):
-        return [pl.BlockSpec((n, tile), lambda i: (0, at // tile + i)) for n in sizes]
-
-    def full(width, at, sizes):
-        return [pl.BlockSpec((n, width), lambda i: (0, at // width)) for n in sizes]
+
+    def cut(at):
+        return pl.BlockSpec((rows, tile), lambda i: (0, at // tile + i))
+
+    def full(width, at):
+        return pl.BlockSpec((rows, width), lambda i: (0, at // width))
 
     return pl.pallas_call(
-        functools.partial(weight_kernel, len(sizes), scale),
+        functools.partial(weight_kernel, scale),
         grid=(features // tile,),
         out_shape=(pltpu.HBM((features, 2 * half), BF16), pltpu.HBM((half, features), BF16)),
-        in_specs=cut(0, [rows, rows])
-        + full(half, 0, [rows])
-        + full(half, 2 * half, sizes)
-        + full(2 * half, 0, sizes + sizes)
-        + cut(4 * half, sizes + sizes),
+        in_specs=[cut(0), cut(0), full(half, 0), full(half, 2 * half), full(2 * half, 0), full(2 * half, 0)]
+        + [cut(4 * half), cut(4 * half)],
         out_specs=(
             pl.BlockSpec((tile, 2 * half), lambda i: (i, 0)),
             pl.BlockSpec((half, tile), lambda i: (0, i)),
@@ -231,7 +230,7 @@
             bytes_accessed=4 * rows * (2 * features + 3 * half) + 6 * features * half,
             transcendentals=0,
         ),
-    )(x_own, x_other, hidden, *other_shares, *grads, *other_shares, *own_shares, *other_shares)
+    )(x_own, x_other, hidden, other_share, grad, other_share, own_share, other_share)
 
 
 def per_device(upstream, inputs, expert_ids, gate_weights, w_in, w_down):
@@ -247,8 +246,8 @@
     chip = [(lax.axis_index("ep") // 2).astype(jnp.int32).reshape(1)]
     ids, gates = expert_ids.T, gate_weights.T
     factor = 1.0 / math.sqrt(2 * routed)
-    parts = GROUPS if experts == 8 else ((*range(1, experts - 1), 0), (experts - 1,))
-    steps = sum(parts, ())
+    order, order_back = (ORDER, BACK) if experts == 8 else (tuple(range(1, experts)),) * 2
+    steps, steps_back = (*order, 0), (*order_back, 0)
     groups = [[2 * e + c for e in range(experts)] for c in range(2)]
 
     def swap(value):
@@ -282,8 +281,8 @@
         tokens_in = [ids, gates, upstream, inputs][: 3 + with_x]
         sends = [(rows, features)] * len(these) + [(total, features)] * with_x
         return call(
-            functools.partial(pack_kernel, experts, rows, these, with_x, len(held), steps),
-            [far(*size) for size in sends] + [pltpu.HBM((total, tokens), BF16)] * (choose * with_x),
+            functools.partial(pack_kernel, experts, rows, these, with_x, len(held), steps_back),
+            [far(*size) for size in sends] + [far(total, tokens)] * (choose * (1 - with_x)),
             chip,
             [*tokens_in, *held],
             like(*tokens_in) + [near(*size) for size in sends] + [dma(5 + len(these))],
@@ -295,8 +294,9 @@
         )
 
     early = EARLY if experts == 8 else experts // 2
-    *up_sent, x_sent, one, two = pack(steps[:early], 1)
-    up_sent += pack(steps[early:], 0, [other_in, other_down])
+    *up_sent, x_sent = pack(steps[:early], 1)
+    *rest, one, two = pack(steps[early:], 0, [other_in, other_down])
+    up_sent += rest
     x_rows = send_all(x_sent)
     up_blocks = send(dict(zip(steps, up_sent)))
 
@@ -314,35 +314,28 @@
     )
     operands = [*terms[:3], *terms[4:7], w_down, other_down, w_in, other_in]
     width, share_width = features + LANES, features + 4 * half
-    returned, shares, grads, first, held = {}, [], [], 0, []
-    for part in parts:
-        count, size = len(part), len(part) * rows
-        *back, share, grad = call(
-            functools.partial(backward_kernel, count, first, len(held)),
-            [far(rows, width)] * count + [far(size, share_width), far(size, 2 * half)],
-            [],
-            [*[up_blocks[step] for step in part], *operands, *held],
-            [near(size, 2 * half), near(size, share_width), near(size, width), dma(2 + count)],
-            12 * size * half * features,
-            16,
-            tuple(range(count + len(operands))),
-            tuple(range(count + len(operands), count + len(operands) + len(held))),
-            tuple(range(count + 2)),
-        )
-        returned.update(send(dict(zip(part, back))))
-        shares.append(share)
-        grads.append(grad)
-        first += count
-        held = [returned[step] for step in part[:HELD]]
-
-    other_shares = [swap(share) for share in shares]
-    grad_in, grad_down = weight_grads(x_rows, swap(x_rows), terms[3], grads, shares, other_shares, factor)
+    *back, share, grad = call(
+        functools.partial(backward_kernel, experts),
+        [far(rows, width)] * experts + [far(total, share_width), far(total, 2 * half)],
+        [],
+        [*[up_blocks[step] for step in steps], *operands],
+        [near(total, 2 * half), near(total, share_width), near(total, width), dma(2 + experts * features // SLAB)],
+        12 * total * half * features,
+        16,
+        tuple(range(experts + len(operands))),
+        (),
+        tuple(range(experts + 2)),
+    )
+    back = dict(zip(steps, back))
+    returned = send({step: back[step] for step in steps_back})
+
+    grad_in, grad_down = weight_grads(x_rows, swap(x_rows), terms[3], grad, share, swap(share), factor)
 
     grad_inputs, grad_gates = call(
         functools.partial(combine_kernel, experts),
         [jax.ShapeDtypeStruct((tokens, features), BF16), jax.ShapeDtypeStruct((choose, tokens), F32)],
         [],
-        [gates, one, two, *[returned[step] for step in steps], grad_in, grad_down],
+        [gates, one, two, *[returned[step] for step in steps_back], grad_in, grad_down],
         [near(total, width)],
         2 * total * tokens * features,
         12,

time: 132 us -> 129 us (0.977)
  waiting for transfers between devices: 60.6 us -> 54.7 us
  starting transfers between devices: 36.3 us -> 41.5 us
    ppermute x14, waiting for transfers between devices: 42.5 us -> 34.8 us  [send(): lax.ppermute(blocks[step], 'ep', [(d, d ^ 2 * step) for d in range(device...]
    ppermute x14, starting transfers between devices: 28.2 us -> 33.3 us  [send(): lax.ppermute(blocks[step], 'ep', [(d, d ^ 2 * step) for d in range(device...]
    all_to_all x1, waiting for transfers between devices: 18.1 us -> 19.9 us  [send_all(): lax.all_to_all(block, 'ep', 0, 0, axis_index_groups=groups, tiled=True)]
where the time goes in v4:
time: 129 us; the launch traced here: 128 us
  waiting for transfers between devices  54.7 us (42%)
  starting transfers between devices  41.5 us (32%)
  Pallas kernels  26.1 us (20%)
  local copies, waits for them, and re-layouts  4.77 us (4%)
    ppermute x14, waiting for transfers between devices, send(): lax.ppermute(blocks[step], 'ep', [(d, d ^ 2 * step) for d in range(device...  34.8 us
    ppermute x14, starting transfers between devices, send(): lax.ppermute(blocks[step], 'ep', [(d, d ^ 2 * step) for d in range(device...  33.3 us
    pallas_call x5, Pallas kernels, call(): pl.pallas_call(kernel, out_shape=tuple(out_shape), in_specs=[pl.BlockSpec...  19.9 us
    all_to_all x1, waiting for transfers between devices, send_all(): lax.all_to_all(block, 'ep', 0, 0, axis_index_groups=groups, tiled=True)  19.9 us
    all_to_all x1, starting transfers between devices, send_all(): lax.all_to_all(block, 'ep', 0, 0, axis_index_groups=groups, tiled=True)  6.88 us
    pallas_call x1, Pallas kernels, weight_grads(): pl.pallas_call(functools.partial(weight_kernel, scale), grid=(features //...  6.23 us
    unnamed x26, local copies, waits for them, and re-layouts  4.77 us
  transfers between devices with their start and end apart: 19, of which 7 were waited for; matrix products, arithmetic and copies ran while one was open for 0% of the time, Pallas kernels for 14%

profile of v4, /device:TPU:0, one launch (start us, length us, event | category | flops | bytes accessed | tf_op | source)
XLA Modules:
  0.0 127.8 jit_solution(9921154444818243721)
XLA Ops:
  1.1 3.2 %shard_map.94 = (bf16[48,2048]{1,0:T(8,128)(2,1)}, bf16[48,2048]{1,0:T(8,128)(2,1)}, bf16[48,2048]{1,0:T(8,128)(2,1)}, bf16[384,2048]{1,0:T(8,128)(2,1)}) custom-call(s32[1]{0:T(128)} %bitcast.1.chip_ref, s32[2,128]{1,0:T(2,128)} %bitcast.21, bf16[2,128]{1,0:T(2,128)(2,1)} %bitcast.15, bf16[128,2048]{1,0:T(8,128)(2,1)} %refs_2_.3, bf16[128,2048]{1,0:T(8,128)(2,1)} %refs_3_.1), custom_call_target="tpu_custom_call" | custom-call | flops 402653184 | bytes 3212800 | tf_op jit(solution)/shard_map/pallas_call | solution.py:194
  4.3 6.9 %all-to-all-start = ((bf16[8,48,2048]{2,1,0:T(8,128)(2,1)}), bf16[8,48,2048]{2,1,0:T(8,128)(2,1)}, u32[]{:S(2)}, u32[]{:S(2)}) async-start(bf16[8,48,2048]{2,1,0:T(8,128)(2,1)} %bitcast.19), calls=%async_computation | async-start | bytes 3145728 | tf_op jit(solution)/shard_map/all_to_all | solution.py:263
  11.4 1.8 %collective-permute-start.2 = (bf16[48,2048]{1,0:T(8,128)(2,1)}, bf16[48,2048]{1,0:T(8,128)(2,1)S(1)}, u32[]{:S(2)}, u32[]{:S(2)}) collective-permute-start(bf16[48,2048]{1,0:T(8,128)(2,1)} %get-tuple-element.39), channel_id=1, source_target_pairs={{0,2},{1,3},{2,0},{3,1},{4,6},{5,7},{6,4},{7,5},{8,10},{9,11},{10,... | collective-permute-start | bytes 589832 | tf_op jit(solution)/shard_map/ppermute | solution.py:258
  14.7 2.4 %collective-permute-start.4 = (bf16[48,2048]{1,0:T(8,128)(2,1)}, bf16[48,2048]{1,0:T(8,128)(2,1)}, u32[]{:S(2)}, u32[]{:S(2)}) collective-permute-start(bf16[48,2048]{1,0:T(8,128)(2,1)} %get-tuple-element.41), channel_id=1, source_target_pairs={{0,10},{1,11},{2,8},{3,9},{4,14},{5,15},{6,12},{7,13},{8,2},{9,3},... | collective-permute-start | bytes 589832 | tf_op jit(solution)/shard_map/ppermute | solution.py:258
  17.1 3.6 %shard_map.93 = (bf16[48,2048]{1,0:T(8,128)(2,1)}, bf16[48,2048]{1,0:T(8,128)(2,1)}, bf16[48,2048]{1,0:T(8,128)(2,1)}, bf16[48,2048]{1,0:T(8,128)(2,1)}, bf16[48...) custom-call(s32[1]{0:T(128)} %bitcast.1.chip_ref, s32[2,128]{1,0:T(2,128)} %bitcast.22, ...), custom_call_target="tpu_custom_call" | custom-call | flops 402653184 | bytes 6424064 | tf_op jit(solution)/shard_map/pallas_call | solution.py:194
  20.7 2.5 %collective-permute-start.5 = (bf16[48,2048]{1,0:T(8,128)(2,1)}, bf16[48,2048]{1,0:T(8,128)(2,1)}, u32[]{:S(2)}, u32[]{:S(2)}) collective-permute-start(bf16[48,2048]{1,0:T(8,128)(2,1)} %get-tuple-element.42), channel_id=1, source_target_pairs={{0,14},{1,15},{2,12},{3,13},{4,10},{5,11},{6,8},{7,9},{8,6},{9,7},... | collective-permute-start | bytes 589832 | tf_op jit(solution)/shard_map/ppermute | solution.py:258
  23.7 6.3 %collective-permute-done.2.refs_0_ = bf16[48,2048]{1,0:T(8,128)(2,1)S(1)} collective-permute-done((bf16[48,2048]{1,0:T(8,128)(2,1)}, bf16[48,2048]{1,0:T(8,128)(2,1)S(1)}, u32[]{:S(2)}, u32[]{:S(2)}) %collective-permute-start.2) | collective-permute-done | bytes 196640 | tf_op jit(solution)/shard_map/ppermute | solution.py:258
  30.0 4.7 %collective-permute-start.7 = (bf16[48,2048]{1,0:T(8,128)(2,1)}, bf16[48,2048]{1,0:T(8,128)(2,1)}, u32[]{:S(2)}, u32[]{:S(2)}) collective-permute-start(bf16[48,2048]{1,0:T(8,128)(2,1)} %get-tuple-element.44), channel_id=1, source_target_pairs={{0,12},{1,13},{2,14},{3,15},{4,8},{5,9},{6,10},{7,11},{8,4},{9,5},... | collective-permute-start | bytes 589832 | tf_op jit(solution)/shard_map/ppermute | solution.py:258
  34.7 8.7 %collective-permute-done.3.refs_1_ = bf16[48,2048]{1,0:T(8,128)(2,1)S(1)} collective-permute-done((bf16[48,2048]{1,0:T(8,128)(2,1)}, bf16[48,2048]{1,0:T(8,128)(2,1)S(1)}, u32[]{:S(2)}, u32[]{:S(2)}) %collective-permute-start.3) | collective-permute-done | bytes 196640 | tf_op jit(solution)/shard_map/ppermute | solution.py:258
  43.3 3.4 %collective-permute-start.8 = (bf16[48,2048]{1,0:T(8,128)(2,1)}, bf16[48,2048]{1,0:T(8,128)(2,1)}, u32[]{:S(2)}, u32[]{:S(2)}) collective-permute-start(bf16[48,2048]{1,0:T(8,128)(2,1)} %get-tuple-element.45), channel_id=1, source_target_pairs={{0,6},{1,7},{2,4},{3,5},{4,2},{5,3},{6,0},{7,1},{8,14},{9,15},{10,... | collective-permute-start | bytes 589832 | tf_op jit(solution)/shard_map/ppermute | solution.py:258
  46.7 19.9 %all-to-all-done = bf16[8,48,2048]{2,1,0:T(8,128)(2,1)} async-done(((bf16[8,48,2048]{2,1,0:T(8,128)(2,1)}), bf16[8,48,2048]{2,1,0:T(8,128)(2,1)}, u32[]{:S(2)}, u32[]{:S(2)}) %all-to-all-start) | async-done | bytes 1572896 | tf_op jit(solution)/shard_map/all_to_all | solution.py:263
  66.6 1.9 %copy-done.2 = bf16[1,2048,768]{2,1,0:T(8,128)(2,1)S(1)} copy-done((bf16[1,2048,768]{2,1,0:T(8,128)(2,1)S(1)}, bf16[1,2048,768]{2,1,0:T(8,128)(2,1)}, u32[]{:S(2)}) %copy-start.2) | copy-done | bytes 3145752
  68.5 5.0 %shard_map.95 = (bf16[384,2048]{1,0:T(8,128)(2,1)}, f32[384,384]{1,0:T(8,128)S(1)}, f32[384,384]{1,0:T(8,128)S(1)}, f32[384,384]{1,0:T(8,128)S(1)}, bf16[384,384...) custom-call(s32[1]{0:T(128)} %bitcast.1.chip_ref, ...), custom_call_target="tpu_custom_call" | custom-call | flops 2415919104 | bytes 13565952 | tf_op jit(solution)/shard_map/pallas_call | solution.py:194
  73.5 5.7 %collective-permute-done.6.refs_4_ = bf16[48,2048]{1,0:T(8,128)(2,1)} collective-permute-done((bf16[48,2048]{1,0:T(8,128)(2,1)}, bf16[48,2048]{1,0:T(8,128)(2,1)}, u32[]{:S(2)}, u32[]{:S(2)}) %collective-permute-start.6) | collective-permute-done | bytes 196640 | tf_op jit(solution)/shard_map/ppermute | solution.py:258
  79.3 6.8 %shard_map.96 = (bf16[48,2176]{1,0:T(8,128)(2,1)}, bf16[48,2176]{1,0:T(8,128)(2,1)}, bf16[48,2176]{1,0:T(8,128)(2,1)}, bf16[48,2176]{1,0:T(8,128)(2,1)}, bf16[48...) custom-call(bf16[48,2048]{1,0:T(8,128)(2,1)S(1)} %collective-permute, ...), custom_call_target="tpu_custom_call" | custom-call | flops 3623878656 | bytes 19562496 | tf_op jit(solution)/shard_map/pallas_call | solution.py:194
  88.1 4.0 %collective-permute-start.10 = (bf16[48,2176]{1,0:T(8,128)(2,1)}, bf16[48,2176]{1,0:T(8,128)(2,1)S(1)}, u32[]{:S(2)}, u32[]{:S(2)}) collective-permute-start(bf16[48,2176]{1,0:T(8,128)(2,1)} %get-tuple-element.55), channel_id=1, source_target_pairs={{0,4},{1,5},{2,6},{3,7},{4,0},{5,1},{6,2},{7,3},{8,12},{9,13},{10,... | collective-permute-start | bytes 626696 | tf_op jit(solution)/shard_map/ppermute | solution.py:258
  92.2 1.5 %collective-permute-start.11 = (bf16[48,2176]{1,0:T(8,128)(2,1)}, bf16[48,2176]{1,0:T(8,128)(2,1)S(1)}, u32[]{:S(2)}, u32[]{:S(2)}) collective-permute-start(bf16[48,2176]{1,0:T(8,128)(2,1)} %get-tuple-element.56), channel_id=1, source_target_pairs={{0,12},{1,13},{2,14},{3,15},{4,8},{5,9},{6,10},{7,11},{8,4},{9,5},... | collective-permute-start | bytes 626696 | tf_op jit(solution)/shard_map/ppermute | solution.py:258
  94.1 4.8 %collective-permute-start.12 = (bf16[48,2176]{1,0:T(8,128)(2,1)}, bf16[48,2176]{1,0:T(8,128)(2,1)S(1)}, u32[]{:S(2)}, u32[]{:S(2)}) collective-permute-start(bf16[48,2176]{1,0:T(8,128)(2,1)} %get-tuple-element.57), channel_id=1, source_target_pairs={{0,8},{1,9},{2,10},{3,11},{4,12},{5,13},{6,14},{7,15},{8,0},{9,1},... | collective-permute-start | bytes 626696 | tf_op jit(solution)/shard_map/ppermute | solution.py:258
  98.9 2.4 %collective-permute-start.13 = (bf16[48,2176]{1,0:T(8,128)(2,1)}, bf16[48,2176]{1,0:T(8,128)(2,1)S(1)}, u32[]{:S(2)}, u32[]{:S(2)}) collective-permute-start(bf16[48,2176]{1,0:T(8,128)(2,1)} %get-tuple-element.58), channel_id=1, source_target_pairs={{0,10},{1,11},{2,8},{3,9},{4,14},{5,15},{6,12},{7,13},{8,2},{9,3},... | collective-permute-start | bytes 626696 | tf_op jit(solution)/shard_map/ppermute | solution.py:258
  101.3 2.4 %collective-permute-start.14 = (bf16[48,2176]{1,0:T(8,128)(2,1)}, bf16[48,2176]{1,0:T(8,128)(2,1)S(1)}, u32[]{:S(2)}, u32[]{:S(2)}) collective-permute-start(bf16[48,2176]{1,0:T(8,128)(2,1)} %get-tuple-element.59), channel_id=1, source_target_pairs={{0,14},{1,15},{2,12},{3,13},{4,10},{5,11},{6,8},{7,9},{8,6},{9,7},... | collective-permute-start | bytes 626696 | tf_op jit(solution)/shard_map/ppermute | solution.py:258
  103.7 1.8 %copy-done.4 = bf16[384,3584]{1,0:T(8,128)(2,1)S(1)} copy-done((bf16[384,3584]{1,0:T(8,128)(2,1)S(1)}, bf16[384,3584]{1,0:T(8,128)(2,1)}, u32[]{:S(2)}) %copy-start.4) | copy-done | bytes 2752536
  106.6 6.2 %shard_map.97 = (bf16[2048,768]{1,0:T(8,128)(2,1)}, bf16[384,2048]{1,0:T(8,128)(2,1)}) custom-call(bf16[384,2048]{1,0:T(8,128)(2,1)S(1)} %copy-done.6, bf16[384,2048]{1,0:T(8,128)(2,1)S(1)} %collective-permute-done.16.x_other, bf16[384,384]{1,0:T(8,128)(2,1)S(1)} %get-tuple-element.63.hidden_own, ...), custom_call_target="tpu_custom_call" | custom-call | flops 3623878656 | bytes 12779520 | tf_op jit(solution)/shard_map/pallas_call | solution.py:217
  112.8 8.5 %collective-permute-done.12.refs_3_ = bf16[48,2176]{1,0:T(8,128)(2,1)S(1)} collective-permute-done((bf16[48,2176]{1,0:T(8,128)(2,1)}, bf16[48,2176]{1,0:T(8,128)(2,1)S(1)}, u32[]{:S(2)}, u32[]{:S(2)}) %collective-permute-start.12) | collective-permute-done | bytes 208928 | tf_op jit(solution)/shard_map/ppermute | solution.py:258
  121.3 5.2 %collective-permute-done.13.refs_4_ = bf16[48,2176]{1,0:T(8,128)(2,1)S(1)} collective-permute-done((bf16[48,2176]{1,0:T(8,128)(2,1)}, bf16[48,2176]{1,0:T(8,128)(2,1)S(1)}, u32[]{:S(2)}, u32[]{:S(2)}) %collective-permute-start.13) | collective-permute-done | bytes 208928 | tf_op jit(solution)/shard_map/ppermute | solution.py:258
  (46 shorter events, 7.5 us)
Async XLA Ops:
  0.6 16.4 %collective-permute-start = (bf16[2048,768]{1,0:T(8,128)(2,1)}, bf16[2048,768]{1,0:T(8,128)(2,1)S(1)}, u32[]{:S(2)}, u32[]{:S(2)}) collective-permute-start(bf16[2048,768]{1,0:T(8,128)(2,1)} %bitcast.10), channel_id=1, source_target_pairs={{0,1},{1,0},{2,3},{3,2},{4,5},{5,4},{6,7},{7,6},{8,9},{9,8},{10,11... | collective-permute-start | bytes 9437192 | tf_op jit(solution)/shard_map/ppermute | solution.py:254
  4.3 62.3 %all-to-all-start = ((bf16[8,48,2048]{2,1,0:T(8,128)(2,1)}), bf16[8,48,2048]{2,1,0:T(8,128)(2,1)}, u32[]{:S(2)}, u32[]{:S(2)}) async-start(bf16[8,48,2048]{2,1,0:T(8,128)(2,1)} %bitcast.19), calls=%async_computation | async-start | bytes 3145728 | tf_op jit(solution)/shard_map/all_to_all | solution.py:263
  11.2 5.9 %collective-permute-start.1 = (bf16[384,2048]{1,0:T(8,128)(2,1)}, bf16[384,2048]{1,0:T(8,128)(2,1)S(1)}, u32[]{:S(2)}, u32[]{:S(2)}) collective-permute-start(bf16[384,2048]{1,0:T(8,128)(2,1)} %bitcast.13), channel_id=1, source_target_pairs={{0,1},{1,0},{2,3},{3,2},{4,5},{5,4},{6,7},{7,6},{8,9},{9,8},{10,11... | collective-permute-start | bytes 4718600 | tf_op jit(solution)/shard_map/ppermute | solution.py:254
  11.4 18.6 %collective-permute-start.2 = (bf16[48,2048]{1,0:T(8,128)(2,1)}, bf16[48,2048]{1,0:T(8,128)(2,1)S(1)}, u32[]{:S(2)}, u32[]{:S(2)}) collective-permute-start(bf16[48,2048]{1,0:T(8,128)(2,1)} %get-tuple-element.39), channel_id=1, source_target_pairs={{0,2},{1,3},{2,0},{3,1},{4,6},{5,7},{6,4},{7,5},{8,10},{9,11},{10,... | collective-permute-start | bytes 589832 | tf_op jit(solution)/shard_map/ppermute | solution.py:258
  13.2 30.1 %collective-permute-start.3 = (bf16[48,2048]{1,0:T(8,128)(2,1)}, bf16[48,2048]{1,0:T(8,128)(2,1)S(1)}, u32[]{:S(2)}, u32[]{:S(2)}) collective-permute-start(bf16[48,2048]{1,0:T(8,128)(2,1)} %get-tuple-element.40), channel_id=1, source_target_pairs={{0,4},{1,5},{2,6},{3,7},{4,0},{5,1},{6,2},{7,3},{8,12},{9,13},{10,... | collective-permute-start | bytes 589832 | tf_op jit(solution)/shard_map/ppermute | solution.py:258
  14.7 58.8 %collective-permute-start.4 = (bf16[48,2048]{1,0:T(8,128)(2,1)}, bf16[48,2048]{1,0:T(8,128)(2,1)}, u32[]{:S(2)}, u32[]{:S(2)}) collective-permute-start(bf16[48,2048]{1,0:T(8,128)(2,1)} %get-tuple-element.41), channel_id=1, source_target_pairs={{0,10},{1,11},{2,8},{3,9},{4,14},{5,15},{6,12},{7,13},{8,2},{9,3},... | collective-permute-start | bytes 589832 | tf_op jit(solution)/shard_map/ppermute | solution.py:258
  20.7 52.8 %collective-permute-start.5 = (bf16[48,2048]{1,0:T(8,128)(2,1)}, bf16[48,2048]{1,0:T(8,128)(2,1)}, u32[]{:S(2)}, u32[]{:S(2)}) collective-permute-start(bf16[48,2048]{1,0:T(8,128)(2,1)} %get-tuple-element.42), channel_id=1, source_target_pairs={{0,14},{1,15},{2,12},{3,13},{4,10},{5,11},{6,8},{7,9},{8,6},{9,7},... | collective-permute-start | bytes 589832 | tf_op jit(solution)/shard_map/ppermute | solution.py:258
  23.2 56.0 %collective-permute-start.6 = (bf16[48,2048]{1,0:T(8,128)(2,1)}, bf16[48,2048]{1,0:T(8,128)(2,1)}, u32[]{:S(2)}, u32[]{:S(2)}) collective-permute-start(bf16[48,2048]{1,0:T(8,128)(2,1)} %get-tuple-element.43), channel_id=1, source_target_pairs={{0,8},{1,9},{2,10},{3,11},{4,12},{5,13},{6,14},{7,15},{8,0},{9,1},... | collective-permute-start | bytes 589832 | tf_op jit(solution)/shard_map/ppermute | solution.py:258
  30.0 49.2 %collective-permute-start.7 = (bf16[48,2048]{1,0:T(8,128)(2,1)}, bf16[48,2048]{1,0:T(8,128)(2,1)}, u32[]{:S(2)}, u32[]{:S(2)}) collective-permute-start(bf16[48,2048]{1,0:T(8,128)(2,1)} %get-tuple-element.44), channel_id=1, source_target_pairs={{0,12},{1,13},{2,14},{3,15},{4,8},{5,9},{6,10},{7,11},{8,4},{9,5},... | collective-permute-start | bytes 589832 | tf_op jit(solution)/shard_map/ppermute | solution.py:258
  43.3 35.9 %collective-permute-start.8 = (bf16[48,2048]{1,0:T(8,128)(2,1)}, bf16[48,2048]{1,0:T(8,128)(2,1)}, u32[]{:S(2)}, u32[]{:S(2)}) collective-permute-start(bf16[48,2048]{1,0:T(8,128)(2,1)} %get-tuple-element.45), channel_id=1, source_target_pairs={{0,6},{1,7},{2,4},{3,5},{4,2},{5,3},{6,0},{7,1},{8,14},{9,15},{10,... | collective-permute-start | bytes 589832 | tf_op jit(solution)/shard_map/ppermute | solution.py:258
  68.5 10.8 %copy-start.9 = (bf16[48,2048]{1,0:T(8,128)(2,1)S(1)}, bf16[48,2048]{1,0:T(8,128)(2,1)}, u32[]{:S(2)}) copy-start(bf16[48,2048]{1,0:T(8,128)(2,1)} %get-tuple-element.46.refs_7_) | copy-start | bytes 589828
  86.1 17.6 %collective-permute-start.17 = (bf16[384,3584]{1,0:T(8,128)(2,1)}, bf16[384,3584]{1,0:T(8,128)(2,1)S(1)}, u32[]{:S(2)}, u32[]{:S(2)}) collective-permute-start(bf16[384,3584]{1,0:T(8,128)(2,1)} %get-tuple-element.64.up_own), channel_id=1, source_target_pairs={{0,1},{1,0},{2,3},{3,2},{4,5},{5,4},{6,7},{7,6},{8,9},{9,8},{10,11... | collective-permute-start | bytes 8257544 | tf_op jit(solution)/shard_map/ppermute | solution.py:254
  86.2 15.1 %collective-permute-start.16 = (bf16[384,2048]{1,0:T(8,128)(2,1)S(1)}, bf16[384,2048]{1,0:T(8,128)(2,1)S(1)}, u32[]{:S(2)}, u32[]{:S(2)}) collective-permute-start(bf16[384,2048]{1,0:T(8,128)(2,1)S(1)} %copy-done.6), channel_id=1, source_target_pairs={{0,1},{1,0},{2,3},{3,2},{4,5},{5,4},{6,7},{7,6},{8,9},{9,8},{10,11... | collective-permute-start | bytes 4718600 | tf_op jit(solution)/shard_map/ppermute | solution.py:254
  86.7 7.4 %collective-permute-start.9 = (bf16[48,2176]{1,0:T(8,128)(2,1)}, bf16[48,2176]{1,0:T(8,128)(2,1)S(1)}, u32[]{:S(2)}, u32[]{:S(2)}) collective-permute-start(bf16[48,2176]{1,0:T(8,128)(2,1)} %get-tuple-element.54), channel_id=1, source_target_pairs={{0,2},{1,3},{2,0},{3,1},{4,6},{5,7},{6,4},{7,5},{8,10},{9,11},{10,... | collective-permute-start | bytes 626696 | tf_op jit(solution)/shard_map/ppermute | solution.py:258
  88.1 10.7 %collective-permute-start.10 = (bf16[48,2176]{1,0:T(8,128)(2,1)}, bf16[48,2176]{1,0:T(8,128)(2,1)S(1)}, u32[]{:S(2)}, u32[]{:S(2)}) collective-permute-start(bf16[48,2176]{1,0:T(8,128)(2,1)} %get-tuple-element.55), channel_id=1, source_target_pairs={{0,4},{1,5},{2,6},{3,7},{4,0},{5,1},{6,2},{7,3},{8,12},{9,13},{10,... | collective-permute-start | bytes 626696 | tf_op jit(solution)/shard_map/ppermute | solution.py:258
  92.2 20.6 %collective-permute-start.11 = (bf16[48,2176]{1,0:T(8,128)(2,1)}, bf16[48,2176]{1,0:T(8,128)(2,1)S(1)}, u32[]{:S(2)}, u32[]{:S(2)}) collective-permute-start(bf16[48,2176]{1,0:T(8,128)(2,1)} %get-tuple-element.56), channel_id=1, source_target_pairs={{0,12},{1,13},{2,14},{3,15},{4,8},{5,9},{6,10},{7,11},{8,4},{9,5},... | collective-permute-start | bytes 626696 | tf_op jit(solution)/shard_map/ppermute | solution.py:258
  94.1 27.3 %collective-permute-start.12 = (bf16[48,2176]{1,0:T(8,128)(2,1)}, bf16[48,2176]{1,0:T(8,128)(2,1)S(1)}, u32[]{:S(2)}, u32[]{:S(2)}) collective-permute-start(bf16[48,2176]{1,0:T(8,128)(2,1)} %get-tuple-element.57), channel_id=1, source_target_pairs={{0,8},{1,9},{2,10},{3,11},{4,12},{5,13},{6,14},{7,15},{8,0},{9,1},... | collective-permute-start | bytes 626696 | tf_op jit(solution)/shard_map/ppermute | solution.py:258
  98.9 27.6 %collective-permute-start.13 = (bf16[48,2176]{1,0:T(8,128)(2,1)}, bf16[48,2176]{1,0:T(8,128)(2,1)S(1)}, u32[]{:S(2)}, u32[]{:S(2)}) collective-permute-start(bf16[48,2176]{1,0:T(8,128)(2,1)} %get-tuple-element.58), channel_id=1, source_target_pairs={{0,10},{1,11},{2,8},{3,9},{4,14},{5,15},{6,12},{7,13},{8,2},{9,3},... | collective-permute-start | bytes 626696 | tf_op jit(solution)/shard_map/ppermute | solution.py:258
  101.3 25.2 %collective-permute-start.14 = (bf16[48,2176]{1,0:T(8,128)(2,1)}, bf16[48,2176]{1,0:T(8,128)(2,1)S(1)}, u32[]{:S(2)}, u32[]{:S(2)}) collective-permute-start(bf16[48,2176]{1,0:T(8,128)(2,1)} %get-tuple-element.59), channel_id=1, source_target_pairs={{0,14},{1,15},{2,12},{3,13},{4,10},{5,11},{6,8},{7,9},{8,6},{9,7},... | collective-permute-start | bytes 626696 | tf_op jit(solution)/shard_map/ppermute | solution.py:258
  103.7 22.8 %collective-permute-start.15 = (bf16[48,2176]{1,0:T(8,128)(2,1)}, bf16[48,2176]{1,0:T(8,128)(2,1)S(1)}, u32[]{:S(2)}, u32[]{:S(2)}) collective-permute-start(bf16[48,2176]{1,0:T(8,128)(2,1)} %get-tuple-element.60), channel_id=1, source_target_pairs={{0,6},{1,7},{2,4},{3,5},{4,2},{5,3},{6,0},{7,1},{8,14},{9,15},{10,... | collective-permute-start | bytes 626696 | tf_op jit(solution)/shard_map/ppermute | solution.py:258
  106.6 19.9 %copy-start.8 = (bf16[48,2176]{1,0:T(8,128)(2,1)S(1)}, bf16[48,2176]{1,0:T(8,128)(2,1)}, u32[]{:S(2)}) copy-start(bf16[48,2176]{1,0:T(8,128)(2,1)} %get-tuple-element.61.refs_7_) | copy-start | bytes 626692
  106.6 19.9 %copy-start.10 = (bf16[384,128]{1,0:T(8,128)(2,1)S(1)}, bf16[384,128]{1,0:T(8,128)(2,1)}, u32[]{:S(2)}) copy-start(bf16[384,128]{1,0:T(8,128)(2,1)} %get-tuple-element.37.one_ref) | copy-start | bytes 294916
  106.6 20.0 %copy-start.11 = (bf16[384,128]{1,0:T(8,128)(2,1)S(1)}, bf16[384,128]{1,0:T(8,128)(2,1)}, u32[]{:S(2)}) copy-start(bf16[384,128]{1,0:T(8,128)(2,1)} %get-tuple-element.38.two_ref) | copy-start | bytes 294916
  106.6 20.0 %copy-start.12 = (bf16[128,2]{0,1:T(2,128)(2,1)S(1)}, bf16[128,2]{0,1:T(2,128)(2,1)}, u32[]{:S(2)}) copy-start(bf16[128,2]{0,1:T(2,128)(2,1)} %param.9) | copy-start | bytes 1540
  (8 other events, 47.6 us)

commit v5 on v4

--- a/solution.py
+++ b/solution.py
@@ -13,7 +13,7 @@
 LANES = 128
 MIB = 1024 * 1024
 ORDER = (1, 2, 5, 7, 4, 6, 3)
-BACK = (1, 2, 6, 4, 5, 7, 3)
+BACK = (1, 6, 2, 4, 5, 7, 3)
 SLAB = 512
 EARLY = 3
 

time: 129 us -> 128 us (level)
  waiting for transfers between devices: 54.7 us -> 52.5 us
  starting transfers between devices: 41.5 us -> 43.3 us
    ppermute x14, waiting for transfers between devices: 34.8 us -> 32.6 us  [send(): lax.ppermute(blocks[step], 'ep', [(d, d ^ 2 * step) for d in range(device...]
    ppermute x14, starting transfers between devices: 33.3 us -> 35.2 us  [send(): lax.ppermute(blocks[step], 'ep', [(d, d ^ 2 * step) for d in range(device...]
  transfers between devices with their start and end apart: 19 -> 19, of which waited for: 7 -> 8; matrix products, arithmetic and copies ran while one was open for 0% -> 0% of each run, Pallas kernels for 14% -> 14%
where the time goes in v5:
time: 128 us; the launch traced here: 127 us
  waiting for transfers between devices  52.5 us (41%)
  starting transfers between devices  43.3 us (34%)
  Pallas kernels  26.1 us (20%)
  local copies, waits for them, and re-layouts  4.77 us (4%)
    ppermute x14, starting transfers between devices, send(): lax.ppermute(blocks[step], 'ep', [(d, d ^ 2 * step) for d in range(device...  35.2 us
    ppermute x14, waiting for transfers between devices, send(): lax.ppermute(blocks[step], 'ep', [(d, d ^ 2 * step) for d in range(device...  32.6 us
    pallas_call x5, Pallas kernels, call(): pl.pallas_call(kernel, out_shape=tuple(out_shape), in_specs=[pl.BlockSpec...  19.9 us
    all_to_all x1, waiting for transfers between devices, send_all(): lax.all_to_all(block, 'ep', 0, 0, axis_index_groups=groups, tiled=True)  19.9 us
    all_to_all x1, starting transfers between devices, send_all(): lax.all_to_all(block, 'ep', 0, 0, axis_index_groups=groups, tiled=True)  6.88 us
    pallas_call x1, Pallas kernels, weight_grads(): pl.pallas_call(functools.partial(weight_kernel, scale), grid=(features //...  6.23 us
    unnamed x26, local copies, waits for them, and re-layouts  4.77 us
  transfers between devices with their start and end apart: 19, of which 8 were waited for; matrix products, arithmetic and copies ran while one was open for 0% of the time, Pallas kernels for 14%

profile of v5, /device:TPU:0, one launch (start us, length us, event | category | flops | bytes accessed | tf_op | source)
XLA Modules:
  0.0 127.5 jit_solution(8183550468169675778)
XLA Ops:
  1.1 3.2 %shard_map.94 = (bf16[48,2048]{1,0:T(8,128)(2,1)}, bf16[48,2048]{1,0:T(8,128)(2,1)}, bf16[48,2048]{1,0:T(8,128)(2,1)}, bf16[384,2048]{1,0:T(8,128)(2,1)}) custom-call(s32[1]{0:T(128)} %bitcast.1.chip_ref, s32[2,128]{1,0:T(2,128)} %bitcast.21, bf16[2,128]{1,0:T(2,128)(2,1)} %bitcast.15, bf16[128,2048]{1,0:T(8,128)(2,1)} %refs_2_.3, bf16[128,2048]{1,0:T(8,128)(2,1)} %refs_3_.1), custom_call_target="tpu_custom_call" | custom-call | flops 402653184 | bytes 3212800 | tf_op jit(solution)/shard_map/pallas_call | solution.py:194
  4.3 6.9 %all-to-all-start = ((bf16[8,48,2048]{2,1,0:T(8,128)(2,1)}), bf16[8,48,2048]{2,1,0:T(8,128)(2,1)}, u32[]{:S(2)}, u32[]{:S(2)}) async-start(bf16[8,48,2048]{2,1,0:T(8,128)(2,1)} %bitcast.19), calls=%async_computation | async-start | bytes 3145728 | tf_op jit(solution)/shard_map/all_to_all | solution.py:263
  11.4 1.8 %collective-permute-start.2 = (bf16[48,2048]{1,0:T(8,128)(2,1)}, bf16[48,2048]{1,0:T(8,128)(2,1)S(1)}, u32[]{:S(2)}, u32[]{:S(2)}) collective-permute-start(bf16[48,2048]{1,0:T(8,128)(2,1)} %get-tuple-element.39), channel_id=1, source_target_pairs={{0,2},{1,3},{2,0},{3,1},{4,6},{5,7},{6,4},{7,5},{8,10},{9,11},{10,... | collective-permute-start | bytes 589832 | tf_op jit(solution)/shard_map/ppermute | solution.py:258
  14.7 2.4 %collective-permute-start.4 = (bf16[48,2048]{1,0:T(8,128)(2,1)}, bf16[48,2048]{1,0:T(8,128)(2,1)}, u32[]{:S(2)}, u32[]{:S(2)}) collective-permute-start(bf16[48,2048]{1,0:T(8,128)(2,1)} %get-tuple-element.41), channel_id=1, source_target_pairs={{0,10},{1,11},{2,8},{3,9},{4,14},{5,15},{6,12},{7,13},{8,2},{9,3},... | collective-permute-start | bytes 589832 | tf_op jit(solution)/shard_map/ppermute | solution.py:258
  17.1 3.6 %shard_map.93 = (bf16[48,2048]{1,0:T(8,128)(2,1)}, bf16[48,2048]{1,0:T(8,128)(2,1)}, bf16[48,2048]{1,0:T(8,128)(2,1)}, bf16[48,2048]{1,0:T(8,128)(2,1)}, bf16[48...) custom-call(s32[1]{0:T(128)} %bitcast.1.chip_ref, s32[2,128]{1,0:T(2,128)} %bitcast.22, ...), custom_call_target="tpu_custom_call" | custom-call | flops 402653184 | bytes 6424064 | tf_op jit(solution)/shard_map/pallas_call | solution.py:194
  20.7 2.5 %collective-permute-start.5 = (bf16[48,2048]{1,0:T(8,128)(2,1)}, bf16[48,2048]{1,0:T(8,128)(2,1)}, u32[]{:S(2)}, u32[]{:S(2)}) collective-permute-start(bf16[48,2048]{1,0:T(8,128)(2,1)} %get-tuple-element.42), channel_id=1, source_target_pairs={{0,14},{1,15},{2,12},{3,13},{4,10},{5,11},{6,8},{7,9},{8,6},{9,7},... | collective-permute-start | bytes 589832 | tf_op jit(solution)/shard_map/ppermute | solution.py:258
  23.7 6.3 %collective-permute-done.2.refs_0_ = bf16[48,2048]{1,0:T(8,128)(2,1)S(1)} collective-permute-done((bf16[48,2048]{1,0:T(8,128)(2,1)}, bf16[48,2048]{1,0:T(8,128)(2,1)S(1)}, u32[]{:S(2)}, u32[]{:S(2)}) %collective-permute-start.2) | collective-permute-done | bytes 196640 | tf_op jit(solution)/shard_map/ppermute | solution.py:258
  30.0 4.7 %collective-permute-start.7 = (bf16[48,2048]{1,0:T(8,128)(2,1)}, bf16[48,2048]{1,0:T(8,128)(2,1)}, u32[]{:S(2)}, u32[]{:S(2)}) collective-permute-start(bf16[48,2048]{1,0:T(8,128)(2,1)} %get-tuple-element.44), channel_id=1, source_target_pairs={{0,12},{1,13},{2,14},{3,15},{4,8},{5,9},{6,10},{7,11},{8,4},{9,5},... | collective-permute-start | bytes 589832 | tf_op jit(solution)/shard_map/ppermute | solution.py:258
  34.7 8.7 %collective-permute-done.3.refs_1_ = bf16[48,2048]{1,0:T(8,128)(2,1)S(1)} collective-permute-done((bf16[48,2048]{1,0:T(8,128)(2,1)}, bf16[48,2048]{1,0:T(8,128)(2,1)S(1)}, u32[]{:S(2)}, u32[]{:S(2)}) %collective-permute-start.3) | collective-permute-done | bytes 196640 | tf_op jit(solution)/shard_map/ppermute | solution.py:258
  43.3 3.4 %collective-permute-start.8 = (bf16[48,2048]{1,0:T(8,128)(2,1)}, bf16[48,2048]{1,0:T(8,128)(2,1)}, u32[]{:S(2)}, u32[]{:S(2)}) collective-permute-start(bf16[48,2048]{1,0:T(8,128)(2,1)} %get-tuple-element.45), channel_id=1, source_target_pairs={{0,6},{1,7},{2,4},{3,5},{4,2},{5,3},{6,0},{7,1},{8,14},{9,15},{10,... | collective-permute-start | bytes 589832 | tf_op jit(solution)/shard_map/ppermute | solution.py:258
  46.7 19.9 %all-to-all-done = bf16[8,48,2048]{2,1,0:T(8,128)(2,1)} async-done(((bf16[8,48,2048]{2,1,0:T(8,128)(2,1)}), bf16[8,48,2048]{2,1,0:T(8,128)(2,1)}, u32[]{:S(2)}, u32[]{:S(2)}) %all-to-all-start) | async-done | bytes 1572896 | tf_op jit(solution)/shard_map/all_to_all | solution.py:263
  66.6 1.9 %copy-done.2 = bf16[1,2048,768]{2,1,0:T(8,128)(2,1)S(1)} copy-done((bf16[1,2048,768]{2,1,0:T(8,128)(2,1)S(1)}, bf16[1,2048,768]{2,1,0:T(8,128)(2,1)}, u32[]{:S(2)}) %copy-start.2) | copy-done | bytes 3145752
  68.5 5.0 %shard_map.95 = (bf16[384,2048]{1,0:T(8,128)(2,1)}, f32[384,384]{1,0:T(8,128)S(1)}, f32[384,384]{1,0:T(8,128)S(1)}, f32[384,384]{1,0:T(8,128)S(1)}, bf16[384,384...) custom-call(s32[1]{0:T(128)} %bitcast.1.chip_ref, ...), custom_call_target="tpu_custom_call" | custom-call | flops 2415919104 | bytes 13565952 | tf_op jit(solution)/shard_map/pallas_call | solution.py:194
  73.5 5.7 %collective-permute-done.6.refs_4_ = bf16[48,2048]{1,0:T(8,128)(2,1)} collective-permute-done((bf16[48,2048]{1,0:T(8,128)(2,1)}, bf16[48,2048]{1,0:T(8,128)(2,1)}, u32[]{:S(2)}, u32[]{:S(2)}) %collective-permute-start.6) | collective-permute-done | bytes 196640 | tf_op jit(solution)/shard_map/ppermute | solution.py:258
  79.3 6.8 %shard_map.96 = (bf16[48,2176]{1,0:T(8,128)(2,1)}, bf16[48,2176]{1,0:T(8,128)(2,1)}, bf16[48,2176]{1,0:T(8,128)(2,1)}, bf16[48,2176]{1,0:T(8,128)(2,1)}, bf16[48...) custom-call(bf16[48,2048]{1,0:T(8,128)(2,1)S(1)} %collective-permute, ...), custom_call_target="tpu_custom_call" | custom-call | flops 3623878656 | bytes 19562496 | tf_op jit(solution)/shard_map/pallas_call | solution.py:194
  89.0 3.8 %collective-permute-start.11 = (bf16[48,2176]{1,0:T(8,128)(2,1)}, bf16[48,2176]{1,0:T(8,128)(2,1)S(1)}, u32[]{:S(2)}, u32[]{:S(2)}) collective-permute-start(bf16[48,2176]{1,0:T(8,128)(2,1)} %get-tuple-element.56), channel_id=1, source_target_pairs={{0,4},{1,5},{2,6},{3,7},{4,0},{5,1},{6,2},{7,3},{8,12},{9,13},{10,... | collective-permute-start | bytes 626696 | tf_op jit(solution)/shard_map/ppermute | solution.py:258
  94.1 4.8 %collective-permute-start.12 = (bf16[48,2176]{1,0:T(8,128)(2,1)}, bf16[48,2176]{1,0:T(8,128)(2,1)S(1)}, u32[]{:S(2)}, u32[]{:S(2)}) collective-permute-start(bf16[48,2176]{1,0:T(8,128)(2,1)} %get-tuple-element.57), channel_id=1, source_target_pairs={{0,8},{1,9},{2,10},{3,11},{4,12},{5,13},{6,14},{7,15},{8,0},{9,1},... | collective-permute-start | bytes 626696 | tf_op jit(solution)/shard_map/ppermute | solution.py:258
  98.9 3.6 %collective-permute-start.13 = (bf16[48,2176]{1,0:T(8,128)(2,1)}, bf16[48,2176]{1,0:T(8,128)(2,1)S(1)}, u32[]{:S(2)}, u32[]{:S(2)}) collective-permute-start(bf16[48,2176]{1,0:T(8,128)(2,1)} %get-tuple-element.58), channel_id=1, source_target_pairs={{0,10},{1,11},{2,8},{3,9},{4,14},{5,15},{6,12},{7,13},{8,2},{9,3},... | collective-permute-start | bytes 626696 | tf_op jit(solution)/shard_map/ppermute | solution.py:258
  102.5 3.9 %collective-permute-start.14 = (bf16[48,2176]{1,0:T(8,128)(2,1)}, bf16[48,2176]{1,0:T(8,128)(2,1)S(1)}, u32[]{:S(2)}, u32[]{:S(2)}) collective-permute-start(bf16[48,2176]{1,0:T(8,128)(2,1)} %get-tuple-element.59), channel_id=1, source_target_pairs={{0,14},{1,15},{2,12},{3,13},{4,10},{5,11},{6,8},{7,9},{8,6},{9,7},... | collective-permute-start | bytes 626696 | tf_op jit(solution)/shard_map/ppermute | solution.py:258
  106.4 1.8 %copy-done.4 = bf16[384,3584]{1,0:T(8,128)(2,1)S(1)} copy-done((bf16[384,3584]{1,0:T(8,128)(2,1)S(1)}, bf16[384,3584]{1,0:T(8,128)(2,1)}, u32[]{:S(2)}) %copy-start.4) | copy-done | bytes 2752536
  109.3 6.2 %shard_map.97 = (bf16[2048,768]{1,0:T(8,128)(2,1)}, bf16[384,2048]{1,0:T(8,128)(2,1)}) custom-call(bf16[384,2048]{1,0:T(8,128)(2,1)S(1)} %copy-done.6, bf16[384,2048]{1,0:T(8,128)(2,1)S(1)} %collective-permute-done.16.x_other, bf16[384,384]{1,0:T(8,128)(2,1)S(1)} %get-tuple-element.63.hidden_own, ...), custom_call_target="tpu_custom_call" | custom-call | flops 3623878656 | bytes 12779520 | tf_op jit(solution)/shard_map/pallas_call | solution.py:217
  115.5 4.1 %collective-permute-done.12.refs_3_ = bf16[48,2176]{1,0:T(8,128)(2,1)S(1)} collective-permute-done((bf16[48,2176]{1,0:T(8,128)(2,1)}, bf16[48,2176]{1,0:T(8,128)(2,1)S(1)}, u32[]{:S(2)}, u32[]{:S(2)}) %collective-permute-start.12) | collective-permute-done | bytes 208928 | tf_op jit(solution)/shard_map/ppermute | solution.py:258
  119.6 4.4 %collective-permute-done.13.refs_4_ = bf16[48,2176]{1,0:T(8,128)(2,1)S(1)} collective-permute-done((bf16[48,2176]{1,0:T(8,128)(2,1)}, bf16[48,2176]{1,0:T(8,128)(2,1)S(1)}, u32[]{:S(2)}, u32[]{:S(2)}) %collective-permute-start.13) | collective-permute-done | bytes 208928 | tf_op jit(solution)/shard_map/ppermute | solution.py:258
  124.0 2.1 %collective-permute-done.15.refs_6_ = bf16[48,2176]{1,0:T(8,128)(2,1)S(1)} collective-permute-done((bf16[48,2176]{1,0:T(8,128)(2,1)}, bf16[48,2176]{1,0:T(8,128)(2,1)S(1)}, u32[]{:S(2)}, u32[]{:S(2)}) %collective-permute-start.15) | collective-permute-done | bytes 208928 | tf_op jit(solution)/shard_map/ppermute | solution.py:258
  (46 shorter events, 9.2 us)
Async XLA Ops:
  0.6 16.4 %collective-permute-start = (bf16[2048,768]{1,0:T(8,128)(2,1)}, bf16[2048,768]{1,0:T(8,128)(2,1)S(1)}, u32[]{:S(2)}, u32[]{:S(2)}) collective-permute-start(bf16[2048,768]{1,0:T(8,128)(2,1)} %bitcast.10), channel_id=1, source_target_pairs={{0,1},{1,0},{2,3},{3,2},{4,5},{5,4},{6,7},{7,6},{8,9},{9,8},{10,11... | collective-permute-start | bytes 9437192 | tf_op jit(solution)/shard_map/ppermute | solution.py:254
  4.3 62.3 %all-to-all-start = ((bf16[8,48,2048]{2,1,0:T(8,128)(2,1)}), bf16[8,48,2048]{2,1,0:T(8,128)(2,1)}, u32[]{:S(2)}, u32[]{:S(2)}) async-start(bf16[8,48,2048]{2,1,0:T(8,128)(2,1)} %bitcast.19), calls=%async_computation | async-start | bytes 3145728 | tf_op jit(solution)/shard_map/all_to_all | solution.py:263
  11.2 5.9 %collective-permute-start.1 = (bf16[384,2048]{1,0:T(8,128)(2,1)}, bf16[384,2048]{1,0:T(8,128)(2,1)S(1)}, u32[]{:S(2)}, u32[]{:S(2)}) collective-permute-start(bf16[384,2048]{1,0:T(8,128)(2,1)} %bitcast.13), channel_id=1, source_target_pairs={{0,1},{1,0},{2,3},{3,2},{4,5},{5,4},{6,7},{7,6},{8,9},{9,8},{10,11... | collective-permute-start | bytes 4718600 | tf_op jit(solution)/shard_map/ppermute | solution.py:254
  11.4 18.6 %collective-permute-start.2 = (bf16[48,2048]{1,0:T(8,128)(2,1)}, bf16[48,2048]{1,0:T(8,128)(2,1)S(1)}, u32[]{:S(2)}, u32[]{:S(2)}) collective-permute-start(bf16[48,2048]{1,0:T(8,128)(2,1)} %get-tuple-element.39), channel_id=1, source_target_pairs={{0,2},{1,3},{2,0},{3,1},{4,6},{5,7},{6,4},{7,5},{8,10},{9,11},{10,... | collective-permute-start | bytes 589832 | tf_op jit(solution)/shard_map/ppermute | solution.py:258
  13.2 30.1 %collective-permute-start.3 = (bf16[48,2048]{1,0:T(8,128)(2,1)}, bf16[48,2048]{1,0:T(8,128)(2,1)S(1)}, u32[]{:S(2)}, u32[]{:S(2)}) collective-permute-start(bf16[48,2048]{1,0:T(8,128)(2,1)} %get-tuple-element.40), channel_id=1, source_target_pairs={{0,4},{1,5},{2,6},{3,7},{4,0},{5,1},{6,2},{7,3},{8,12},{9,13},{10,... | collective-permute-start | bytes 589832 | tf_op jit(solution)/shard_map/ppermute | solution.py:258
  14.7 58.8 %collective-permute-start.4 = (bf16[48,2048]{1,0:T(8,128)(2,1)}, bf16[48,2048]{1,0:T(8,128)(2,1)}, u32[]{:S(2)}, u32[]{:S(2)}) collective-permute-start(bf16[48,2048]{1,0:T(8,128)(2,1)} %get-tuple-element.41), channel_id=1, source_target_pairs={{0,10},{1,11},{2,8},{3,9},{4,14},{5,15},{6,12},{7,13},{8,2},{9,3},... | collective-permute-start | bytes 589832 | tf_op jit(solution)/shard_map/ppermute | solution.py:258
  20.7 52.8 %collective-permute-start.5 = (bf16[48,2048]{1,0:T(8,128)(2,1)}, bf16[48,2048]{1,0:T(8,128)(2,1)}, u32[]{:S(2)}, u32[]{:S(2)}) collective-permute-start(bf16[48,2048]{1,0:T(8,128)(2,1)} %get-tuple-element.42), channel_id=1, source_target_pairs={{0,14},{1,15},{2,12},{3,13},{4,10},{5,11},{6,8},{7,9},{8,6},{9,7},... | collective-permute-start | bytes 589832 | tf_op jit(solution)/shard_map/ppermute | solution.py:258
  23.2 56.0 %collective-permute-start.6 = (bf16[48,2048]{1,0:T(8,128)(2,1)}, bf16[48,2048]{1,0:T(8,128)(2,1)}, u32[]{:S(2)}, u32[]{:S(2)}) collective-permute-start(bf16[48,2048]{1,0:T(8,128)(2,1)} %get-tuple-element.43), channel_id=1, source_target_pairs={{0,8},{1,9},{2,10},{3,11},{4,12},{5,13},{6,14},{7,15},{8,0},{9,1},... | collective-permute-start | bytes 589832 | tf_op jit(solution)/shard_map/ppermute | solution.py:258
  30.0 49.2 %collective-permute-start.7 = (bf16[48,2048]{1,0:T(8,128)(2,1)}, bf16[48,2048]{1,0:T(8,128)(2,1)}, u32[]{:S(2)}, u32[]{:S(2)}) collective-permute-start(bf16[48,2048]{1,0:T(8,128)(2,1)} %get-tuple-element.44), channel_id=1, source_target_pairs={{0,12},{1,13},{2,14},{3,15},{4,8},{5,9},{6,10},{7,11},{8,4},{9,5},... | collective-permute-start | bytes 589832 | tf_op jit(solution)/shard_map/ppermute | solution.py:258
  43.3 35.9 %collective-permute-start.8 = (bf16[48,2048]{1,0:T(8,128)(2,1)}, bf16[48,2048]{1,0:T(8,128)(2,1)}, u32[]{:S(2)}, u32[]{:S(2)}) collective-permute-start(bf16[48,2048]{1,0:T(8,128)(2,1)} %get-tuple-element.45), channel_id=1, source_target_pairs={{0,6},{1,7},{2,4},{3,5},{4,2},{5,3},{6,0},{7,1},{8,14},{9,15},{10,... | collective-permute-start | bytes 589832 | tf_op jit(solution)/shard_map/ppermute | solution.py:258
  68.5 10.8 %copy-start.9 = (bf16[48,2048]{1,0:T(8,128)(2,1)S(1)}, bf16[48,2048]{1,0:T(8,128)(2,1)}, u32[]{:S(2)}) copy-start(bf16[48,2048]{1,0:T(8,128)(2,1)} %get-tuple-element.46.refs_7_) | copy-start | bytes 589828
  86.1 20.3 %collective-permute-start.17 = (bf16[384,3584]{1,0:T(8,128)(2,1)}, bf16[384,3584]{1,0:T(8,128)(2,1)S(1)}, u32[]{:S(2)}, u32[]{:S(2)}) collective-permute-start(bf16[384,3584]{1,0:T(8,128)(2,1)} %get-tuple-element.64.up_own), channel_id=1, source_target_pairs={{0,1},{1,0},{2,3},{3,2},{4,5},{5,4},{6,7},{7,6},{8,9},{9,8},{10,11... | collective-permute-start | bytes 8257544 | tf_op jit(solution)/shard_map/ppermute | solution.py:254
  86.2 16.3 %collective-permute-start.16 = (bf16[384,2048]{1,0:T(8,128)(2,1)S(1)}, bf16[384,2048]{1,0:T(8,128)(2,1)S(1)}, u32[]{:S(2)}, u32[]{:S(2)}) collective-permute-start(bf16[384,2048]{1,0:T(8,128)(2,1)S(1)} %copy-done.6), channel_id=1, source_target_pairs={{0,1},{1,0},{2,3},{3,2},{4,5},{5,4},{6,7},{7,6},{8,9},{9,8},{10,11... | collective-permute-start | bytes 4718600 | tf_op jit(solution)/shard_map/ppermute | solution.py:254
  86.7 7.4 %collective-permute-start.9 = (bf16[48,2176]{1,0:T(8,128)(2,1)}, bf16[48,2176]{1,0:T(8,128)(2,1)S(1)}, u32[]{:S(2)}, u32[]{:S(2)}) collective-permute-start(bf16[48,2176]{1,0:T(8,128)(2,1)} %get-tuple-element.54), channel_id=1, source_target_pairs={{0,2},{1,3},{2,0},{3,1},{4,6},{5,7},{6,4},{7,5},{8,10},{9,11},{10,... | collective-permute-start | bytes 626696 | tf_op jit(solution)/shard_map/ppermute | solution.py:258
  88.1 10.7 %collective-permute-start.10 = (bf16[48,2176]{1,0:T(8,128)(2,1)}, bf16[48,2176]{1,0:T(8,128)(2,1)S(1)}, u32[]{:S(2)}, u32[]{:S(2)}) collective-permute-start(bf16[48,2176]{1,0:T(8,128)(2,1)} %get-tuple-element.55), channel_id=1, source_target_pairs={{0,12},{1,13},{2,14},{3,15},{4,8},{5,9},{6,10},{7,11},{8,4},{9,5},... | collective-permute-start | bytes 626696 | tf_op jit(solution)/shard_map/ppermute | solution.py:258
  89.0 26.5 %collective-permute-start.11 = (bf16[48,2176]{1,0:T(8,128)(2,1)}, bf16[48,2176]{1,0:T(8,128)(2,1)S(1)}, u32[]{:S(2)}, u32[]{:S(2)}) collective-permute-start(bf16[48,2176]{1,0:T(8,128)(2,1)} %get-tuple-element.56), channel_id=1, source_target_pairs={{0,4},{1,5},{2,6},{3,7},{4,0},{5,1},{6,2},{7,3},{8,12},{9,13},{10,... | collective-permute-start | bytes 626696 | tf_op jit(solution)/shard_map/ppermute | solution.py:258
  94.1 25.6 %collective-permute-start.12 = (bf16[48,2176]{1,0:T(8,128)(2,1)}, bf16[48,2176]{1,0:T(8,128)(2,1)S(1)}, u32[]{:S(2)}, u32[]{:S(2)}) collective-permute-start(bf16[48,2176]{1,0:T(8,128)(2,1)} %get-tuple-element.57), channel_id=1, source_target_pairs={{0,8},{1,9},{2,10},{3,11},{4,12},{5,13},{6,14},{7,15},{8,0},{9,1},... | collective-permute-start | bytes 626696 | tf_op jit(solution)/shard_map/ppermute | solution.py:258
  98.9 25.1 %collective-permute-start.13 = (bf16[48,2176]{1,0:T(8,128)(2,1)}, bf16[48,2176]{1,0:T(8,128)(2,1)S(1)}, u32[]{:S(2)}, u32[]{:S(2)}) collective-permute-start(bf16[48,2176]{1,0:T(8,128)(2,1)} %get-tuple-element.58), channel_id=1, source_target_pairs={{0,10},{1,11},{2,8},{3,9},{4,14},{5,15},{6,12},{7,13},{8,2},{9,3},... | collective-permute-start | bytes 626696 | tf_op jit(solution)/shard_map/ppermute | solution.py:258
  102.5 21.5 %collective-permute-start.14 = (bf16[48,2176]{1,0:T(8,128)(2,1)}, bf16[48,2176]{1,0:T(8,128)(2,1)S(1)}, u32[]{:S(2)}, u32[]{:S(2)}) collective-permute-start(bf16[48,2176]{1,0:T(8,128)(2,1)} %get-tuple-element.59), channel_id=1, source_target_pairs={{0,14},{1,15},{2,12},{3,13},{4,10},{5,11},{6,8},{7,9},{8,6},{9,7},... | collective-permute-start | bytes 626696 | tf_op jit(solution)/shard_map/ppermute | solution.py:258
  106.4 19.7 %collective-permute-start.15 = (bf16[48,2176]{1,0:T(8,128)(2,1)}, bf16[48,2176]{1,0:T(8,128)(2,1)S(1)}, u32[]{:S(2)}, u32[]{:S(2)}) collective-permute-start(bf16[48,2176]{1,0:T(8,128)(2,1)} %get-tuple-element.60), channel_id=1, source_target_pairs={{0,6},{1,7},{2,4},{3,5},{4,2},{5,3},{6,0},{7,1},{8,14},{9,15},{10,... | collective-permute-start | bytes 626696 | tf_op jit(solution)/shard_map/ppermute | solution.py:258
  109.3 16.9 %copy-start.8 = (bf16[48,2176]{1,0:T(8,128)(2,1)S(1)}, bf16[48,2176]{1,0:T(8,128)(2,1)}, u32[]{:S(2)}) copy-start(bf16[48,2176]{1,0:T(8,128)(2,1)} %get-tuple-element.61.refs_7_) | copy-start | bytes 626692
  109.3 16.9 %copy-start.10 = (bf16[384,128]{1,0:T(8,128)(2,1)S(1)}, bf16[384,128]{1,0:T(8,128)(2,1)}, u32[]{:S(2)}) copy-start(bf16[384,128]{1,0:T(8,128)(2,1)} %get-tuple-element.37.one_ref) | copy-start | bytes 294916
  109.3 16.9 %copy-start.11 = (bf16[384,128]{1,0:T(8,128)(2,1)S(1)}, bf16[384,128]{1,0:T(8,128)(2,1)}, u32[]{:S(2)}) copy-start(bf16[384,128]{1,0:T(8,128)(2,1)} %get-tuple-element.38.two_ref) | copy-start | bytes 294916
  109.3 16.9 %copy-start.12 = (bf16[128,2]{0,1:T(2,128)(2,1)S(1)}, bf16[128,2]{0,1:T(2,128)(2,1)}, u32[]{:S(2)}) copy-start(bf16[128,2]{0,1:T(2,128)(2,1)} %param.9) | copy-start | bytes 1540
  (8 other events, 47.6 us)
